TPU v7x, 32 devices: a whole 2x2x4 slice. The times are simulated.
32 devices in a mesh: view: 16 (over z, x, core), dp: 2 (over y).
Axes of the slice: x: 2, y: 2, z: 4, core: 2. Of those that a mesh axis runs over, the one named last changes fastest.
Arguments:
- tokens: bfloat16 [2, 16, 1, 512, 512], P('dp', 'view'), may hold values from -6 to 6
- counts: int32 [2, 16], P('dp', 'view'), may hold values from 1 to 1, as said below
- slot_item: int32 [2, 16, 1], P('dp', 'view'), may hold values from -1 to 2, as said below
- slot_view: int32 [2, 16, 1], P('dp', 'view'), may hold values from 0 to 4, as said below
- keyframe: int32 [2, 16, 1], P('dp', 'view'), may hold values 0 or 1
- w_query: bfloat16 [512, 512], replicated, may hold values from -0.25 to 0.25
- w_keyval: bfloat16 [512, 1024], replicated, may hold values from -0.25 to 0.25
- w_output: bfloat16 [512, 512], replicated, may hold values from -2 to 2
- w_up: bfloat16 [512, 2048], replicated, may hold values from -0.25 to 0.25
- bias_up: bfloat16 [2048], replicated, may hold values from -1.5 to 1.5
- w_down: bfloat16 [2048, 512], replicated, may hold values from -0.125 to 0.125
- bias_down: bfloat16 [512], replicated, may hold values from -1.5 to 1.5
- gain_attn: bfloat16 [512], replicated, may hold values from 0.5 to 1.5
- shift_attn: bfloat16 [512], replicated, may hold values from -1.5 to 1.5
- gain_mlp: bfloat16 [512], replicated, may hold values from 0.5 to 1.5
- shift_mlp: bfloat16 [512], replicated, may hold values from -1.5 to 1.5
- cotangent: bfloat16 [2, 16, 1, 512, 512], P('dp', 'view'), may hold values from -6 to 6
Outputs:
- block_output: bfloat16 [2, 16, 1, 512, 512], P('dp', 'view')
- grad_tokens: float32 [2, 16, 1, 512, 512], P('dp', 'view')
- grad_query: float32 [512, 512], replicated
- grad_keyval: float32 [512, 1024], replicated
- grad_output: float32 [512, 512], replicated
- grad_up: float32 [512, 2048], replicated
- grad_bias_up: float32 [2048], replicated
- grad_down: float32 [2048, 512], replicated
- grad_bias_down: float32 [512], replicated
- grad_gain_attn: float32 [512], replicated
- grad_shift_attn: float32 [512], replicated
- grad_gain_mlp: float32 [512], replicated
- grad_shift_mlp: float32 [512], replicated
Inputs may be any that keep to these rules, and one draw needn't show every extreme that they name: `counts`: A device's filled slots are its first ones; in every group some device of the cycle has all 1 filled. `slot_item`: for each group and slot index, items hold that slot on runs of 5 neighbouring devices of the cycle, wrapping past its last device; one such run crosses from the last device to the first; -1 marks a slot without an item. `slot_view`: along an item's run of devices its view numbers rise from 0 to 4.
All inputs are finite; a program needn't handle non-finite values. No bound on the sum of `keyframe` on one device may be relied on, other than what follows from the above.
Results may differ from a plain program's by a relative error of at most 0.01.
Values may be sent and summed in bfloat16 or wider, within the bound.
A program may use at most 256 MiB of HBM per device.

v0:
```python
from functools import partial

import jax
import jax.numpy as jnp
from jax import lax
from jax.sharding import PartitionSpec as P

D = 512
HEADS = 8
HEAD_DIM = 64
VIEWS = 5
PATCHES = 400
LANG = 77
ROWS = 512


NEGATIVE = -1e30
EPSILON = 1e-05


def passed_along(value, axis, steps):
    count = lax.axis_size(axis)
    pairs = [(source, (source + steps) % count) for source in range(count)]
    return lax.ppermute(value, axis, pairs)


def label_rows(counts, slot_item, slot_view, keyframe):
    slot_index = jnp.arange(slot_item.shape[-1], dtype=jnp.int32)
    slot_filled = (slot_index < counts[..., None]) & (keyframe == 1) & (slot_item >= 0)
    row_index = jnp.arange(ROWS, dtype=jnp.int32)
    language = row_index - PATCHES
    row_live = (row_index < PATCHES) | (slot_view[..., None] == 0) & (language < LANG)
    return jnp.where(slot_filled[..., None] & row_live, slot_item[..., None], -1)


def layer_norm(values, gain, shift):
    average = jnp.mean(values, -1, keepdims=True)
    centered = values - average
    variance = jnp.mean(centered * centered, -1, keepdims=True)
    return centered * lax.rsqrt(variance + EPSILON) * gain + shift


def fetch_window(key_values, label_values):
    blocks = []
    label_blocks = []
    for offset in range(1 - VIEWS, VIEWS):
        if offset == 0:
            blocks.append(key_values)
            label_blocks.append(label_values)
        else:
            arrived, arrived_labels = passed_along((key_values, label_values), "view", offset)
            blocks.append(arrived)
            label_blocks.append(arrived_labels)
    slot_count = key_values.shape[0]
    window = jnp.stack(blocks, 1).reshape(slot_count, -1, key_values.shape[2])
    window_labels = jnp.stack(label_blocks, 1).reshape(slot_count, -1).astype(jnp.int32)
    return (window, window_labels)


def to_pairs(array):
    slot_count = array.shape[0]
    length = array.shape[1]
    divided = array.reshape(slot_count, length, HEADS // 2, 2 * HEAD_DIM)
    return jnp.moveaxis(divided, 2, 1).reshape(-1, length, 2 * HEAD_DIM)


def from_pairs(array):
    length = array.shape[1]
    divided = array.reshape(-1, HEADS // 2, length, 2 * HEAD_DIM)
    return jnp.moveaxis(divided, 1, 2).reshape(-1, length, D)


def pair_labels(labels):
    return jnp.repeat(labels, HEADS // 2, 0)


def pair_scores(query_pair, key_pair, query_labels, key_labels):
    query_heads = query_pair.reshape(query_pair.shape[0], 2, HEAD_DIM)
    key_heads = key_pair.reshape(key_pair.shape[0], 2, HEAD_DIM)
    scores = jnp.einsum(
        "rhe,khe->hrk", query_heads, key_heads, preferred_element_type=jnp.float32
    ) * HEAD_DIM ** (-0.5)
    matching = (query_labels[None, :, None] == key_labels[None, None, :]) & (
        key_labels[None, None, :] >= 0
    )
    return jnp.where(matching, scores, NEGATIVE)


def forward_pair(blocks):
    query_pair, key_pair, value_pair, query_labels, key_labels = blocks
    masked = pair_scores(query_pair, key_pair, query_labels, key_labels)
    top_score = jnp.max(masked, -1, keepdims=True)
    log_total = top_score + jnp.log(jnp.sum(jnp.exp(masked - top_score), -1, keepdims=True))
    attention = jnp.exp(masked - log_total).astype(jnp.bfloat16)
    value_heads = value_pair.reshape(value_pair.shape[0], 2, HEAD_DIM)
    mixed = jnp.einsum("hrk,khe->rhe", attention, value_heads, preferred_element_type=jnp.float32)
    return (mixed.reshape(-1, 2 * HEAD_DIM).astype(jnp.bfloat16), log_total[..., 0])


def backward_pair(blocks, with_keys):
    query_pair, key_pair, value_pair, query_labels, key_labels, grad_pair, log_total = blocks
    masked = pair_scores(query_pair, key_pair, query_labels, key_labels)
    attention_full = jnp.exp(masked - log_total[..., None])
    query_heads = query_pair.reshape(query_pair.shape[0], 2, HEAD_DIM)
    key_heads = key_pair.reshape(key_pair.shape[0], 2, HEAD_DIM)
    value_heads = value_pair.reshape(value_pair.shape[0], 2, HEAD_DIM)
    grad_heads = grad_pair.reshape(grad_pair.shape[0], 2, HEAD_DIM)
    score_dot = jnp.einsum(
        "rhe,khe->hrk", grad_heads, value_heads, preferred_element_type=jnp.float32
    )
    row_dots = jnp.sum(attention_full * score_dot, -1, keepdims=True)
    score_grad = (attention_full * (score_dot - row_dots)).astype(jnp.bfloat16)
    query_grad = jnp.einsum(
        "hrk,khe->rhe", score_grad, key_heads, preferred_element_type=jnp.float32
    ) * HEAD_DIM ** (-0.5)
    query_grad = query_grad.reshape(-1, 2 * HEAD_DIM)
    key_part = jnp.einsum(
        "hrk,rhe->khe", score_grad, query_heads, preferred_element_type=jnp.float32
    ) * HEAD_DIM ** (-0.5)
    value_part = jnp.einsum(
        "hrk,rhe->khe",
        attention_full.astype(jnp.bfloat16),
        grad_heads,
        preferred_element_type=jnp.float32,
    )
    return (query_grad, key_part.reshape(-1, 2 * HEAD_DIM), value_part.reshape(-1, 2 * HEAD_DIM))


def on_device(
    tokens,
    counts,
    slot_item,
    slot_view,
    keyframe,
    w_query,
    w_keyval,
    w_output,
    w_up,
    bias_up,
    w_down,
    bias_down,
    gain_attn,
    shift_attn,
    gain_mlp,
    shift_mlp,
    cotangent,
):
    slot_count = tokens.shape[2]
    labels = label_rows(counts, slot_item, slot_view, keyframe).reshape(slot_count, ROWS)
    live = (labels >= 0).astype(jnp.float32).reshape(-1, 1)
    inputs = tokens.reshape(-1, D).astype(jnp.float32)
    norm_params = tuple(
        (param.astype(jnp.float32) for param in (gain_attn, shift_attn, gain_mlp, shift_mlp))
    )
    normed = layer_norm(inputs, norm_params[0], norm_params[1]).astype(jnp.bfloat16)
    queries = jnp.dot(normed, w_query, preferred_element_type=jnp.float32).astype(jnp.bfloat16)
    key_values = jnp.dot(normed, w_keyval, preferred_element_type=jnp.float32).astype(jnp.bfloat16)
    own_keyval = key_values.reshape(slot_count, ROWS, 2 * D)
    label_values = labels.astype(jnp.bfloat16)
    query_pairs = to_pairs(queries.reshape(slot_count, ROWS, D))
    query_label_pairs = pair_labels(labels)
    window, window_labels = fetch_window(own_keyval, label_values)
    mixed_pairs, log_total = lax.map(
        forward_pair,
        (
            query_pairs,
            to_pairs(window[..., :D]),
            to_pairs(window[..., D:]),
            query_label_pairs,
            pair_labels(window_labels),
        ),
    )
    mixed = from_pairs(mixed_pairs).reshape(-1, D)
    attended = jnp.dot(mixed, w_output, preferred_element_type=jnp.float32)
    residual = inputs + live * attended
    normed_mlp = layer_norm(residual, norm_params[2], norm_params[3]).astype(jnp.bfloat16)
    before = jnp.dot(normed_mlp, w_up, preferred_element_type=jnp.float32) + bias_up.astype(
        jnp.float32
    )
    activated = jax.nn.gelu(before, approximate=False).astype(jnp.bfloat16)
    branch = jnp.dot(activated, w_down, preferred_element_type=jnp.float32) + bias_down.astype(
        jnp.float32
    )
    block_output = (residual + live * branch).astype(jnp.bfloat16)
    upstream = cotangent.reshape(-1, D).astype(jnp.float32)
    branch_grad = (live * upstream).astype(jnp.bfloat16)
    grad_down = jnp.einsum("rf,rd->fd", activated, branch_grad, preferred_element_type=jnp.float32)
    grad_bias_down = jnp.sum(branch_grad.astype(jnp.float32), 0)
    activated_grad = jnp.einsum(
        "rd,fd->rf", branch_grad, w_down, preferred_element_type=jnp.float32
    )
    unused, gelu_back = jax.vjp(partial(jax.nn.gelu, approximate=False), before)
    before_grad = gelu_back(activated_grad)[0].astype(jnp.bfloat16)
    grad_up = jnp.einsum("rd,rf->df", normed_mlp, before_grad, preferred_element_type=jnp.float32)
    grad_bias_up = jnp.sum(before_grad.astype(jnp.float32), 0)
    normed_mlp_grad = jnp.einsum("rf,df->rd", before_grad, w_up, preferred_element_type=jnp.float32)
    unused, norm_back = jax.vjp(layer_norm, residual, norm_params[2], norm_params[3])
    residual_part, grad_gain_mlp, grad_shift_mlp = norm_back(normed_mlp_grad)
    residual_grad = upstream + residual_part
    attended_grad = (live * residual_grad).astype(jnp.bfloat16)
    grad_output = jnp.einsum("rd,re->de", mixed, attended_grad, preferred_element_type=jnp.float32)
    mixed_grad = jnp.einsum(
        "re,de->rd", attended_grad, w_output, preferred_element_type=jnp.float32
    ).astype(jnp.bfloat16)
    grad_pairs = to_pairs(mixed_grad.reshape(slot_count, ROWS, D))
    window_back, window_labels_back = fetch_window(own_keyval, label_values)
    backward_inputs = (
        query_pairs,
        to_pairs(window_back[..., :D]),
        to_pairs(window_back[..., D:]),
        query_label_pairs,
        pair_labels(window_labels_back),
        grad_pairs,
        log_total,
    )
    query_grad_pairs, key_parts, value_parts = lax.map(
        partial(backward_pair, with_keys=True), backward_inputs
    )
    window_grad = jnp.concatenate([from_pairs(key_parts), from_pairs(value_parts)], -1)
    window_grad = window_grad.reshape(slot_count, 2 * VIEWS - 1, ROWS, 2 * D)
    keyval_grad = window_grad[:, VIEWS - 1]
    for offset in range(1 - VIEWS, VIEWS):
        if offset != 0:
            keyval_grad = keyval_grad + passed_along(
                window_grad[:, offset + VIEWS - 1], "view", -offset
            )
    query_grad = from_pairs(query_grad_pairs).reshape(-1, D).astype(jnp.bfloat16)
    keyval_grad = keyval_grad.reshape(-1, 2 * D).astype(jnp.bfloat16)
    grad_query = jnp.einsum("rd,re->de", normed, query_grad, preferred_element_type=jnp.float32)
    grad_keyval = jnp.einsum("rd,re->de", normed, keyval_grad, preferred_element_type=jnp.float32)
    normed_grad = jnp.einsum("re,de->rd", query_grad, w_query, preferred_element_type=jnp.float32)
    normed_grad = normed_grad + jnp.einsum(
        "re,de->rd", keyval_grad, w_keyval, preferred_element_type=jnp.float32
    )
    unused, first_back = jax.vjp(layer_norm, inputs, norm_params[0], norm_params[1])
    input_part, grad_gain_attn, grad_shift_attn = first_back(normed_grad)
    grad_tokens = residual_grad + input_part
    summed = lax.psum(
        (
            grad_query,
            grad_keyval,
            grad_output,
            grad_up,
            grad_bias_up,
            grad_down,
            grad_bias_down,
            grad_gain_attn,
            grad_shift_attn,
            grad_gain_mlp,
            grad_shift_mlp,
        ),
        ("view", "dp"),
    )
    return (block_output.reshape(tokens.shape), grad_tokens.reshape(tokens.shape)) + tuple(summed)


def solution(mesh):
    in_specs = (
        P("dp", "view", None, None, None),
        P("dp", "view"),
        P("dp", "view", None),
        P("dp", "view", None),
        P("dp", "view", None),
        P(),
        P(),
        P(),
        P(),
        P(),
        P(),
        P(),
        P(),
        P(),
        P(),
        P(),
        P("dp", "view", None, None, None),
    )
    out_specs = (
        P("dp", "view", None, None, None),
        P("dp", "view", None, None, None),
        P(),
        P(),
        P(),
        P(),
        P(),
        P(),
        P(),
        P(),
        P(),
        P(),
        P(),
    )
    return jax.shard_map(
        on_device, mesh=mesh, in_specs=in_specs, out_specs=out_specs, check_vma=False
    )
```

profile of v0, /device:TPU:0, one launch (start us, length us, event | category | flops | bytes accessed | tf_op | source)
XLA Modules:
  0.0 1201.4 jit_solution(12074821936171666258)
XLA Ops:
  23.9 41.5 %collective-permute-done.8 = bf16[1,512]{1,0:T(2,128)(2,1)S(1)} collective-permute-done((bf16[1,512]{1,0:T(2,128)(2,1)S(1)}, bf16[1,512]{1,0:T(2,128)(2,1)S(1)}, u32[]{:S(2)}, u32[]{:S(2)}) %collective-permute-start.8) | collective-permute-done | bytes 1056 | tf_op jit(solution)/shard_map/ppermute | solution.py:24
  68.6 18.3 %collective-permute-done.10 = bf16[1,512]{1,0:T(2,128)(2,1)S(1)} collective-permute-done((bf16[1,512]{1,0:T(2,128)(2,1)S(1)}, bf16[1,512]{1,0:T(2,128)(2,1)S(1)}, u32[]{:S(2)}, u32[]{:S(2)}) %collective-permute-start.10) | collective-permute-done | bytes 1056 | tf_op jit(solution)/shard_map/ppermute | solution.py:24
  87.1 5.6 collective-permute-done.12
  100.8 7.3 collective-permute-done.15
  115.9 20.1 %collective-permute-done.4 = bf16[1,512,1024]{2,1,0:T(8,128)(2,1)} collective-permute-done((bf16[1,512,1024]{2,1,0:T(8,128)(2,1)}, bf16[1,512,1024]{2,1,0:T(8,128)(2,1)}, u32[]{:S(2)}, u32[]{:S(2)}) %collective-permute-start.4) | collective-permute-done | bytes 1048608 | tf_op jit(solution)/shard_map/ppermute | solution.py:24
  137.3 11.6 collective-permute-done.6
  151.6 35.1 %pad_maximum_fusion = (bf16[1,18432,128]{2,1,0:T(8,128)(2,1)}, bf16[1,18432,128]{2,1,0:T(8,128)(2,1)}) fusion(bf16[1,4608,128]{2,1,0:T(8,128)(2,1)S(1)} %get-tuple-element.245, bf16[1,4608,128]{2,1,0:T(8,128)(2,1)S(1)} %get-tuple-element.246, bf16[1,4608,128]{2,1,0:T(8,128)(2,1)S(1)} %get-tuple-element.247, bf16[1,4608,128]{2,1,0:T(8,128)(2,1)S(1)} %get-tuple-element.248, ...), kind=kLoop, calls=%fused_computation.39 | loop fusion | flops 37748736 | bytes 18874368 | tf_op jit(solution)/shard_map/concatenate.2
  186.8 6.7 copy.48
  193.4 7.2 copy.49
  200.7 109.5 %while.26 = (s32[]{:T(128)}, bf16[4,512,128]{1,2,0:T(8,128)(2,1)}, f32[4,2,512]{2,1,0:T(2,128)}, bf16[4,4608,128]{1,2,0:T(8,128)(2,1)}, s32[4,512]{1,0:T(4,128)S...) while((s32[]{:T(128)}, bf16[4,512,128]{1,2,0:T(8,128)(2,1)}, ...), condition=%wide.region_5.6_spmd, body=%wide.region_2.5_spmd.sunk | while | flops 1264651776 | bytes 149545104 | solution.py:163
  205.7 5.6 fusion.129
  218.3 9.0 fusion.130
  233.0 5.6 fusion.129
  245.7 9.0 fusion.130
  260.4 5.6 fusion.129
  273.0 9.0 fusion.130
  287.7 5.6 fusion.129
  300.4 9.0 fusion.130
  313.2 11.5 multiply_convert_fusion.1
  336.8 253.1 %while.27 = (s32[]{:T(128)}, bf16[4,512,128]{1,2,0:T(8,128)(2,1)}, f32[4,4608,128]{1,2,0:T(8,128)}, f32[4,4608,128]{1,2,0:T(8,128)}, bf16[4,4608,128]{1,2,0:T(8,...) while((s32[]{:T(128)}, bf16[4,512,128]{1,2,0:T(8,128)(2,1)}, ...), condition=%wide.region_12.13_spmd, body=%wide.region_10.12_spmd.sunk | while | flops 3067809280 | bytes 268808576 | solution.py:216
  340.2 7.9 fusion.141
  351.0 14.3 %multiply_reduce_fusion.5 = (f32[2,512]{1,0:T(2,128)S(1)}, f32[2,512,4608]{2,1,0:T(8,128)}) fusion(f32[2,512,4608]{2,1,0:T(8,128)} %fusion.141, f32[2,512]{1,0:T(2,128)S(1)} %dynamic-slice_bitcast_fusion.2, bf16[512,2,64]{0,2,1:T(8,128)(2,1)S(1)} %bitcast.284, bf16[4608,2,64]{0,2,1:T(8,128)(2,1)S(1)} %bitcast.270, ...), kind=kOutput, calls=%fused_computation.20.clone.1 | convolution fusion | flops 627571712 | bytes 41426944 | tf_op jit(solution)/shard_map/while/body/eval_jaxpr/rhe,khe->hrk/dot_general | solution.py:80
  365.4 17.7 %multiply_convert_fusion.4 = bf16[2,512,4608]{2,1,0:T(8,128)(2,1)} fusion(f32[2,512,4608]{2,1,0:T(8,128)} %get-tuple-element.393, f32[2,512,4608]{2,1,0:T(8,128)} %fusion.141, f32[2,512]{1,0:T(2,128)S(1)} %get-tuple-element.394), kind=kLoop, calls=%fused_computation.19.clone.1 | loop fusion | flops 14155776 | bytes 47190016 | tf_op jit(solution)/shard_map/while/body/eval_jaxpr/convert_element_type | solution.py:112
  383.1 6.4 convolution_multiply_fusion.6
  403.4 7.9 fusion.141
  414.3 14.3 %multiply_reduce_fusion.5 = (f32[2,512]{1,0:T(2,128)S(1)}, f32[2,512,4608]{2,1,0:T(8,128)}) fusion(f32[2,512,4608]{2,1,0:T(8,128)} %fusion.141, f32[2,512]{1,0:T(2,128)S(1)} %dynamic-slice_bitcast_fusion.2, bf16[512,2,64]{0,2,1:T(8,128)(2,1)S(1)} %bitcast.284, bf16[4608,2,64]{0,2,1:T(8,128)(2,1)S(1)} %bitcast.270, ...), kind=kOutput, calls=%fused_computation.20.clone.1 | convolution fusion | flops 627571712 | bytes 41426944 | tf_op jit(solution)/shard_map/while/body/eval_jaxpr/rhe,khe->hrk/dot_general | solution.py:80
  428.6 17.7 %multiply_convert_fusion.4 = bf16[2,512,4608]{2,1,0:T(8,128)(2,1)} fusion(f32[2,512,4608]{2,1,0:T(8,128)} %get-tuple-element.393, f32[2,512,4608]{2,1,0:T(8,128)} %fusion.141, f32[2,512]{1,0:T(2,128)S(1)} %get-tuple-element.394), kind=kLoop, calls=%fused_computation.19.clone.1 | loop fusion | flops 14155776 | bytes 47190016 | tf_op jit(solution)/shard_map/while/body/eval_jaxpr/convert_element_type | solution.py:112
  446.3 6.4 convolution_multiply_fusion.6
  466.7 7.9 fusion.141
  477.5 14.3 %multiply_reduce_fusion.5 = (f32[2,512]{1,0:T(2,128)S(1)}, f32[2,512,4608]{2,1,0:T(8,128)}) fusion(f32[2,512,4608]{2,1,0:T(8,128)} %fusion.141, f32[2,512]{1,0:T(2,128)S(1)} %dynamic-slice_bitcast_fusion.2, bf16[512,2,64]{0,2,1:T(8,128)(2,1)S(1)} %bitcast.284, bf16[4608,2,64]{0,2,1:T(8,128)(2,1)S(1)} %bitcast.270, ...), kind=kOutput, calls=%fused_computation.20.clone.1 | convolution fusion | flops 627571712 | bytes 41426944 | tf_op jit(solution)/shard_map/while/body/eval_jaxpr/rhe,khe->hrk/dot_general | solution.py:80
  491.8 17.7 %multiply_convert_fusion.4 = bf16[2,512,4608]{2,1,0:T(8,128)(2,1)} fusion(f32[2,512,4608]{2,1,0:T(8,128)} %get-tuple-element.393, f32[2,512,4608]{2,1,0:T(8,128)} %fusion.141, f32[2,512]{1,0:T(2,128)S(1)} %get-tuple-element.394), kind=kLoop, calls=%fused_computation.19.clone.1 | loop fusion | flops 14155776 | bytes 47190016 | tf_op jit(solution)/shard_map/while/body/eval_jaxpr/convert_element_type | solution.py:112
  509.5 6.4 convolution_multiply_fusion.6
  529.9 7.9 fusion.141
  540.7 14.3 %multiply_reduce_fusion.5 = (f32[2,512]{1,0:T(2,128)S(1)}, f32[2,512,4608]{2,1,0:T(8,128)}) fusion(f32[2,512,4608]{2,1,0:T(8,128)} %fusion.141, f32[2,512]{1,0:T(2,128)S(1)} %dynamic-slice_bitcast_fusion.2, bf16[512,2,64]{0,2,1:T(8,128)(2,1)S(1)} %bitcast.284, bf16[4608,2,64]{0,2,1:T(8,128)(2,1)S(1)} %bitcast.270, ...), kind=kOutput, calls=%fused_computation.20.clone.1 | convolution fusion | flops 627571712 | bytes 41426944 | tf_op jit(solution)/shard_map/while/body/eval_jaxpr/rhe,khe->hrk/dot_general | solution.py:80
  555.0 17.7 %multiply_convert_fusion.4 = bf16[2,512,4608]{2,1,0:T(8,128)(2,1)} fusion(f32[2,512,4608]{2,1,0:T(8,128)} %get-tuple-element.393, f32[2,512,4608]{2,1,0:T(8,128)} %fusion.141, f32[2,512]{1,0:T(2,128)S(1)} %get-tuple-element.394), kind=kLoop, calls=%fused_computation.19.clone.1 | loop fusion | flops 14155776 | bytes 47190016 | tf_op jit(solution)/shard_map/while/body/eval_jaxpr/convert_element_type | solution.py:112
  572.8 6.4 convolution_multiply_fusion.6
  590.0 11.8 copy.55
  601.8 11.9 copy.56
  613.7 19.8 %maximum_bitcast_fusion.6 = (f32[1,512,1024]{2,0,1:T(1,128)}, f32[1,512,1024]{2,0,1:T(1,128)}, f32[1,512,1024]{2,0,1:T(1,128)}, f32[1,512,1024]{2,0,1:T(1,128)},...) fusion(f32[1,9,512,512]{3,0,2,1:T(1,128)} %bitcast.278, f32[1,9,512,512]{3,0,2,1:T(1,128)} %bitcast.273), kind=kLoop, calls=%fused_computation.66 | loop fusion | flops 3670016 | bytes 33554432 | tf_op jit(solution)/shard_map/squeeze | solution.py:225
  634.3 42.8 %collective-permute-start.17 = (f32[1,512,1024]{2,0,1:T(1,128)}, f32[1,512,1024]{2,0,1:T(1,128)S(1)}, u32[]{:S(2)}, u32[]{:S(2)}) collective-permute-start(f32[1,512,1024]{2,0,1:T(1,128)} %get-tuple-element.239), channel_id=1, source_target_pairs={{0,6},{2,8},{4,10},{6,12},{8,14},{10,16},{12,18},{14,20},{16,22},{... | collective-permute-start | bytes 6291464 | tf_op jit(solution)/shard_map/ppermute | solution.py:24
  684.9 22.3 %collective-permute-start.21 = (f32[1,512,1024]{2,0,1:T(1,128)}, f32[1,512,1024]{2,0,1:T(1,128)S(1)}, u32[]{:S(2)}, u32[]{:S(2)}) collective-permute-start(f32[1,512,1024]{2,0,1:T(1,128)} %get-tuple-element.235), channel_id=1, source_target_pairs={{0,28},{2,30},{4,0},{6,2},{8,4},{10,6},{12,8},{14,10},{16,12},{18,... | collective-permute-start | bytes 6291464 | tf_op jit(solution)/shard_map/ppermute | solution.py:24
  707.2 83.6 %collective-permute-done.17 = f32[1,512,1024]{2,0,1:T(1,128)S(1)} collective-permute-done((f32[1,512,1024]{2,0,1:T(1,128)}, f32[1,512,1024]{2,0,1:T(1,128)S(1)}, u32[]{:S(2)}, u32[]{:S(2)}) %collective-permute-start.17) | collective-permute-done | bytes 2097184 | tf_op jit(solution)/shard_map/ppermute | solution.py:24
  790.8 44.5 %collective-permute-done.18 = f32[1,512,1024]{2,0,1:T(1,128)S(1)} collective-permute-done((f32[1,512,1024]{2,0,1:T(1,128)}, f32[1,512,1024]{2,0,1:T(1,128)S(1)}, u32[]{:S(2)}, u32[]{:S(2)}) %collective-permute-start.18) | collective-permute-done | bytes 2097184 | tf_op jit(solution)/shard_map/ppermute | solution.py:24
  835.3 25.9 %collective-permute-start.23 = (f32[1,512,1024]{2,0,1:T(1,128)}, f32[1,512,1024]{2,0,1:T(1,128)S(1)}, u32[]{:S(2)}, u32[]{:S(2)}) collective-permute-start(f32[1,512,1024]{2,0,1:T(1,128)} %fusion.14), channel_id=1, source_target_pairs={{0,24},{2,26},{4,28},{6,30},{8,0},{10,2},{12,4},{14,6},{16,8},{18,... | collective-permute-start | bytes 6291464 | tf_op jit(solution)/shard_map/ppermute | solution.py:24
  871.1 14.1 %collective-permute-done.23 = f32[1,512,1024]{2,0,1:T(1,128)S(1)} collective-permute-done((f32[1,512,1024]{2,0,1:T(1,128)}, f32[1,512,1024]{2,0,1:T(1,128)S(1)}, u32[]{:S(2)}, u32[]{:S(2)}) %collective-permute-start.23) | collective-permute-done | bytes 2097184 | tf_op jit(solution)/shard_map/ppermute | solution.py:24
  885.1 12.2 %add_convert_fusion.1 = bf16[1,512,1024]{2,0,1:T(2,128)(2,1)S(1)} fusion(f32[1,512,1024]{2,0,1:T(1,128)S(1)} %collective-permute-done.23, f32[1,512,1024]{2,0,1:T(1,128)S(1)} %collective-permute-done.22, f32[1,512,1024]{2,0,1:T(1,128)S(1)} %collective-permute-done.21, f32[1,512,1024]{2,0,1:T(1,128)} %collective-permute-done.20, ...), kind=kLoop, calls=%fused_computation.71 | loop fusion | flops 5242880 | bytes 36700160 | tf_op jit(solution)/shard_map/convert_element_type | solution.py:228
  913.0 88.1 %all-reduce = (f32[2048]{0:T(1024)}, f32[512]{0:T(512)}, f32[512]{0:T(512)}, f32[512]{0:T(512)}, f32[512]{0:T(512)}, /*index=5*/f32[512]{0:T(512)}) all-reduce(f32[2048]{0:T(1024)S(1)} %copy-done.51, f32[512]{0:T(512)S(1)} %copy-done.50, f32[512]{0:T(512)S(1)} %get-tuple-element.167, ...), channel_id=1, replica_groups=mesh['view'=16,'dp'=2] {'view','dp'}, use_global_device_ids=true, to_apply=%region_20.21 | all-reduce | flops 4608 | bytes 36864 | tf_op jit(solution)/shard_map/psum | solution.py:238
  1001.1 181.0 %all-reduce.4.cloned.1.call-done = (f32[512,512]{1,0:T(8,128)}, f32[512,1024]{1,0:T(8,128)}, f32[512,512]{1,0:T(8,128)}, f32[512,2048]{1,0:T(8,128)}, f32[2048,512]{1,0:T(8,128)}) async-done(((f32[512,512]{1,0:T(8,128)}, f32[512,1024]{1,0:T(8,128)}, f32[512,512]{1,0:T(8,128)}, f32[512,2048]{1,0:T(8,128)}, f32[2048,512]{1,0:T(8,128)}), (f32[512,512]{1,0:T(8,128)}, f32[512,1024]{1,0:T(8,128)}, ...) | async-done | bytes 12582928 | tf_op jit(solution)/shard_map/psum | solution.py:238
  (399 shorter events, 216.0 us)
Async XLA Ops:
  7.2 305.9 %copy-start = (bf16[512,2048]{1,0:T(8,128)(2,1)S(1)}, bf16[512,2048]{1,0:T(8,128)(2,1)}, u32[]{:S(2)}) copy-start(bf16[512,2048]{1,0:T(8,128)(2,1)} %param.29) | copy-start | bytes 6291460
  7.2 91.5 %copy-start.56 = (bf16[512]{0:T(512)(128)(2,1)S(1)}, bf16[512]{0:T(512)(128)(2,1)}, u32[]{:S(2)}) copy-start(bf16[512]{0:T(512)(128)(2,1)} %param.35) | copy-start | bytes 3076
  7.2 91.5 %copy-start.52 = (bf16[2048]{0:T(1024)(128)(2,1)S(1)}, bf16[2048]{0:T(1024)(128)(2,1)}, u32[]{:S(2)}) copy-start(bf16[2048]{0:T(1024)(128)(2,1)} %param.30) | copy-start | bytes 12292
  7.2 91.5 %copy-start.57 = (bf16[512]{0:T(512)(128)(2,1)S(1)}, bf16[512]{0:T(512)(128)(2,1)}, u32[]{:S(2)}) copy-start(bf16[512]{0:T(512)(128)(2,1)} %param.36) | copy-start | bytes 3076
  7.2 1174.9 %all-reduce.4.cloned.1.call-start = ((), (), s32[]{:S(2)}) async-start(), calls=%async_computation | async-start | bytes 25165824 | tf_op jit(solution)/shard_map/psum | solution.py:238
  8.7 92.2 %copy-start.6 = (bf16[1,1,1,512,512]{3,4,2,1,0:T(8,128)(2,1)}, bf16[1,1,1,512,512]{3,4,2,1,0:T(8,128)(2,1)S(1)}, u32[]{:S(2)}) copy-start(bf16[1,1,1,512,512]{3,4,2,1,0:T(8,128)(2,1)S(1)} %copy.47) | copy-start | bytes 1572868
  8.8 100.8 %copy-start.37 = (f32[512]{0:T(512)}, f32[512]{0:T(512)S(1)}, u32[]{:S(2)}) copy-start(f32[512]{0:T(512)S(1)} %broadcast_multiply_fusion.1) | copy-start | bytes 6148
  9.6 100.0 %copy-start.41 = (f32[512]{0:T(512)}, f32[512]{0:T(512)S(1)}, u32[]{:S(2)}) copy-start(f32[512]{0:T(512)S(1)} %fusion.59) | copy-start | bytes 6148
  10.3 99.3 %copy-start.43 = (f32[512]{0:T(512)}, f32[512]{0:T(512)S(1)}, u32[]{:S(2)}) copy-start(f32[512]{0:T(512)S(1)} %convert_element_type.163) | copy-start | bytes 6148
  11.0 82.8 %copy-start.54 = (f32[512]{0:T(512)}, f32[512]{0:T(512)S(1)}, u32[]{:S(2)}) copy-start(f32[512]{0:T(512)S(1)} %convert_element_type.164) | copy-start | bytes 6148
  14.0 94.2 %collective-permute-start = (bf16[1,512,1024]{2,1,0:T(8,128)(2,1)}, bf16[1,512,1024]{2,1,0:T(8,128)(2,1)}, u32[]{:S(2)}, u32[]{:S(2)}) collective-permute-start(bf16[1,512,1024]{2,1,0:T(8,128)(2,1)} %bitcast.24), channel_id=1, source_target_pairs={{0,24},{2,26},{4,28},{6,30},{8,0},{10,2},{12,4},{14,6},{16,8},{18,... | collective-permute-start | bytes 3145736 | tf_op jit(solution)/shard_map/ppermute | solution.py:24
  19.1 90.5 %collective-permute-start.1 = (bf16[1,512,1024]{2,1,0:T(8,128)(2,1)}, bf16[1,512,1024]{2,1,0:T(8,128)(2,1)}, u32[]{:S(2)}, u32[]{:S(2)}) collective-permute-start(bf16[1,512,1024]{2,1,0:T(8,128)(2,1)} %bitcast.24), channel_id=1, source_target_pairs={{0,26},{2,28},{4,30},{6,0},{8,2},{10,4},{12,6},{14,8},{16,10},{18,... | collective-permute-start | bytes 3145736 | tf_op jit(solution)/shard_map/ppermute | solution.py:24
  21.7 43.7 %collective-permute-start.8 = (bf16[1,512]{1,0:T(2,128)(2,1)S(1)}, bf16[1,512]{1,0:T(2,128)(2,1)S(1)}, u32[]{:S(2)}, u32[]{:S(2)}) collective-permute-start(bf16[1,512]{1,0:T(2,128)(2,1)S(1)} %fusion.54), channel_id=1, source_target_pairs={{0,24},{2,26},{4,28},{6,30},{8,0},{10,2},{12,4},{14,6},{16,8},{18,... | collective-permute-start | bytes 3080 | tf_op jit(solution)/shard_map/ppermute | solution.py:24
  22.2 43.2 %collective-permute-start.9 = (bf16[1,512]{1,0:T(2,128)(2,1)S(1)}, bf16[1,512]{1,0:T(2,128)(2,1)S(1)}, u32[]{:S(2)}, u32[]{:S(2)}) collective-permute-start(bf16[1,512]{1,0:T(2,128)(2,1)S(1)} %fusion.54), channel_id=1, source_target_pairs={{0,26},{2,28},{4,30},{6,0},{8,2},{10,4},{12,6},{14,8},{16,10},{18,... | collective-permute-start | bytes 3080 | tf_op jit(solution)/shard_map/ppermute | solution.py:24
  23.5 88.4 %collective-permute-start.2 = (bf16[1,512,1024]{2,1,0:T(8,128)(2,1)}, bf16[1,512,1024]{2,1,0:T(8,128)(2,1)}, u32[]{:S(2)}, u32[]{:S(2)}) collective-permute-start(bf16[1,512,1024]{2,1,0:T(8,128)(2,1)} %bitcast.24), channel_id=1, source_target_pairs={{0,28},{2,30},{4,0},{6,2},{8,4},{10,6},{12,8},{14,10},{16,12},{18,... | collective-permute-start | bytes 3145736 | tf_op jit(solution)/shard_map/ppermute | solution.py:24
  65.4 21.4 %collective-permute-start.10 = (bf16[1,512]{1,0:T(2,128)(2,1)S(1)}, bf16[1,512]{1,0:T(2,128)(2,1)S(1)}, u32[]{:S(2)}, u32[]{:S(2)}) collective-permute-start(bf16[1,512]{1,0:T(2,128)(2,1)S(1)} %fusion.54), channel_id=1, source_target_pairs={{0,28},{2,30},{4,0},{6,2},{8,4},{10,6},{12,8},{14,10},{16,12},{18,... | collective-permute-start | bytes 3080 | tf_op jit(solution)/shard_map/ppermute | solution.py:24
  65.4 21.4 %collective-permute-start.11 = (bf16[1,512]{1,0:T(2,128)(2,1)S(1)}, bf16[1,512]{1,0:T(2,128)(2,1)S(1)}, u32[]{:S(2)}, u32[]{:S(2)}) collective-permute-start(bf16[1,512]{1,0:T(2,128)(2,1)S(1)} %fusion.54), channel_id=1, source_target_pairs={{0,30},{2,0},{4,2},{6,4},{8,6},{10,8},{12,10},{14,12},{16,14},{18,... | collective-permute-start | bytes 3080 | tf_op jit(solution)/shard_map/ppermute | solution.py:24
  86.9 5.8 collective-permute-start.12
  86.9 6.8 collective-permute-start.13
  92.7 20.6 %collective-permute-start.3 = (bf16[1,512,1024]{2,1,0:T(8,128)(2,1)}, bf16[1,512,1024]{2,1,0:T(8,128)(2,1)}, u32[]{:S(2)}, u32[]{:S(2)}) collective-permute-start(bf16[1,512,1024]{2,1,0:T(8,128)(2,1)} %bitcast.24), channel_id=1, source_target_pairs={{0,30},{2,0},{4,2},{6,4},{8,6},{10,8},{12,10},{14,12},{16,14},{18,... | collective-permute-start | bytes 3145736 | tf_op jit(solution)/shard_map/ppermute | solution.py:24
  93.7 4.9 collective-permute-start.14
  98.6 9.5 collective-permute-start.15
  98.6 235.1 %copy-start.39 = (f32[512]{0:T(512)}, f32[512]{0:T(512)S(1)}, u32[]{:S(2)}) copy-start(f32[512]{0:T(512)S(1)} %compare_convert_fusion) | copy-start | bytes 6148
  98.7 234.7 %copy-start.29 = (f32[512]{0:T(512)}, f32[512]{0:T(512)S(1)}, u32[]{:S(2)}) copy-start(f32[512]{0:T(512)S(1)} %convert_element_type.172) | copy-start | bytes 6148
  98.8 214.3 %copy-start.35 = (f32[512]{0:T(512)}, f32[512]{0:T(512)S(1)}, u32[]{:S(2)}) copy-start(f32[512]{0:T(512)S(1)} %convert_element_type.173) | copy-start | bytes 6148
  108.2 27.8 %collective-permute-start.4 = (bf16[1,512,1024]{2,1,0:T(8,128)(2,1)}, bf16[1,512,1024]{2,1,0:T(8,128)(2,1)}, u32[]{:S(2)}, u32[]{:S(2)}) collective-permute-start(bf16[1,512,1024]{2,1,0:T(8,128)(2,1)} %bitcast.24), channel_id=1, source_target_pairs={{0,2},{2,4},{4,6},{6,8},{8,10},{10,12},{12,14},{14,16},{16,18},{18... | collective-permute-start | bytes 3145736 | tf_op jit(solution)/shard_map/ppermute | solution.py:24
  108.2 29.0 %collective-permute-start.5 = (bf16[1,512,1024]{2,1,0:T(8,128)(2,1)}, bf16[1,512,1024]{2,1,0:T(8,128)(2,1)S(1)}, u32[]{:S(2)}, u32[]{:S(2)}) collective-permute-start(bf16[1,512,1024]{2,1,0:T(8,128)(2,1)} %bitcast.24), channel_id=1, source_target_pairs={{0,4},{2,6},{4,8},{6,10},{8,12},{10,14},{12,16},{14,18},{16,20},{1... | collective-permute-start | bytes 3145736 | tf_op jit(solution)/shard_map/ppermute | solution.py:24
  109.6 39.3 %collective-permute-start.6 = (bf16[1,512,1024]{2,1,0:T(8,128)(2,1)}, bf16[1,512,1024]{2,1,0:T(8,128)(2,1)S(1)}, u32[]{:S(2)}, u32[]{:S(2)}) collective-permute-start(bf16[1,512,1024]{2,1,0:T(8,128)(2,1)} %bitcast.24), channel_id=1, source_target_pairs={{0,6},{2,8},{4,10},{6,12},{8,14},{10,16},{12,18},{14,20},{16,22},{... | collective-permute-start | bytes 3145736 | tf_op jit(solution)/shard_map/ppermute | solution.py:24
  111.9 37.1 %collective-permute-start.7 = (bf16[1,512,1024]{2,1,0:T(8,128)(2,1)}, bf16[1,512,1024]{2,1,0:T(8,128)(2,1)S(1)}, u32[]{:S(2)}, u32[]{:S(2)}) collective-permute-start(bf16[1,512,1024]{2,1,0:T(8,128)(2,1)} %bitcast.24), channel_id=1, source_target_pairs={{0,8},{2,10},{4,12},{6,14},{8,16},{10,18},{12,20},{14,22},{16,24},... | collective-permute-start | bytes 3145736 | tf_op jit(solution)/shard_map/ppermute | solution.py:24
  633.4 51.5 %collective-permute-start.16 = (f32[1,512,1024]{2,0,1:T(1,128)}, f32[1,512,1024]{2,0,1:T(1,128)S(1)}, u32[]{:S(2)}, u32[]{:S(2)}) collective-permute-start(f32[1,512,1024]{2,0,1:T(1,128)} %get-tuple-element.234), channel_id=1, source_target_pairs={{0,8},{2,10},{4,12},{6,14},{8,16},{10,18},{12,20},{14,22},{16,24},... | collective-permute-start | bytes 6291464 | tf_op jit(solution)/shard_map/ppermute | solution.py:24
  634.3 156.5 %collective-permute-start.17 = (f32[1,512,1024]{2,0,1:T(1,128)}, f32[1,512,1024]{2,0,1:T(1,128)S(1)}, u32[]{:S(2)}, u32[]{:S(2)}) collective-permute-start(f32[1,512,1024]{2,0,1:T(1,128)} %get-tuple-element.239), channel_id=1, source_target_pairs={{0,6},{2,8},{4,10},{6,12},{8,14},{10,16},{12,18},{14,20},{16,22},{... | collective-permute-start | bytes 6291464 | tf_op jit(solution)/shard_map/ppermute | solution.py:24
  677.2 158.2 %collective-permute-start.18 = (f32[1,512,1024]{2,0,1:T(1,128)}, f32[1,512,1024]{2,0,1:T(1,128)S(1)}, u32[]{:S(2)}, u32[]{:S(2)}) collective-permute-start(f32[1,512,1024]{2,0,1:T(1,128)} %get-tuple-element.238), channel_id=1, source_target_pairs={{0,4},{2,6},{4,8},{6,10},{8,12},{10,14},{12,16},{14,18},{16,20},{1... | collective-permute-start | bytes 6291464 | tf_op jit(solution)/shard_map/ppermute | solution.py:24
  677.2 193.9 %collective-permute-start.19 = (f32[1,512,1024]{2,0,1:T(1,128)}, f32[1,512,1024]{2,0,1:T(1,128)}, u32[]{:S(2)}, u32[]{:S(2)}) collective-permute-start(f32[1,512,1024]{2,0,1:T(1,128)} %get-tuple-element.237), channel_id=1, source_target_pairs={{0,2},{2,4},{4,6},{6,8},{8,10},{10,12},{12,14},{14,16},{16,18},{18... | collective-permute-start | bytes 6291464 | tf_op jit(solution)/shard_map/ppermute | solution.py:24
  677.3 183.9 %copy-start.13 = (bf16[512,512]{0,1:T(8,128)(2,1)S(1)}, bf16[512,512]{0,1:T(8,128)(2,1)}, u32[]{:S(2)}) copy-start(bf16[512,512]{0,1:T(8,128)(2,1)} %copy-done.12) | copy-start | bytes 1572868
  677.3 183.9 %copy-start.22 = (bf16[4,512,128]{1,2,0:T(8,128)(2,1)S(1)}, bf16[4,512,128]{1,2,0:T(8,128)(2,1)}, u32[]{:S(2)}) copy-start(bf16[4,512,128]{1,2,0:T(8,128)(2,1)} %get-tuple-element.115) | copy-start | bytes 1572868
  677.3 185.4 %copy-start.7 = (bf16[1,1,1,512,512]{3,4,2,1,0:T(8,128)(2,1)S(1)}, bf16[1,1,1,512,512]{3,4,2,1,0:T(8,128)(2,1)}, u32[]{:S(2)}) copy-start(bf16[1,1,1,512,512]{3,4,2,1,0:T(8,128)(2,1)} %copy-done.6) | copy-start | bytes 1572868
  677.3 185.4 %copy-start.28 = (bf16[4,512,128]{1,2,0:T(8,128)(2,1)S(1)}, bf16[4,512,128]{1,2,0:T(8,128)(2,1)}, u32[]{:S(2)}) copy-start(bf16[4,512,128]{1,2,0:T(8,128)(2,1)} %get-tuple-element.117) | copy-start | bytes 1572868
  677.4 185.4 %copy-start.38 = (f32[512]{0:T(512)S(1)}, f32[512]{0:T(512)}, u32[]{:S(2)}) copy-start(f32[512]{0:T(512)} %copy-done.37) | copy-start | bytes 6148
  677.4 185.4 %copy-start.42 = (f32[512]{0:T(512)S(1)}, f32[512]{0:T(512)}, u32[]{:S(2)}) copy-start(f32[512]{0:T(512)} %copy-done.41) | copy-start | bytes 6148
  677.4 185.4 %copy-start.44 = (f32[512]{0:T(512)S(1)}, f32[512]{0:T(512)}, u32[]{:S(2)}) copy-start(f32[512]{0:T(512)} %copy-done.43) | copy-start | bytes 6148
  677.4 185.4 %copy-start.55 = (f32[512]{0:T(512)S(1)}, f32[512]{0:T(512)}, u32[]{:S(2)}) copy-start(f32[512]{0:T(512)} %copy-done.54) | copy-start | bytes 6148
  677.4 193.6 %collective-permute-start.20 = (f32[1,512,1024]{2,0,1:T(1,128)}, f32[1,512,1024]{2,0,1:T(1,128)}, u32[]{:S(2)}, u32[]{:S(2)}) collective-permute-start(f32[1,512,1024]{2,0,1:T(1,128)} %get-tuple-element.236), channel_id=1, source_target_pairs={{0,30},{2,0},{4,2},{6,4},{8,6},{10,8},{12,10},{14,12},{16,14},{18,... | collective-permute-start | bytes 6291464 | tf_op jit(solution)/shard_map/ppermute | solution.py:24
  684.9 179.3 %copy-start.11 = (bf16[1,1,1,512,512]{3,4,2,1,0:T(8,128)(2,1)S(1)}, bf16[1,1,1,512,512]{3,4,2,1,0:T(8,128)(2,1)}, u32[]{:S(2)}) copy-start(bf16[1,1,1,512,512]{3,4,2,1,0:T(8,128)(2,1)} %copy.51) | copy-start | bytes 1572868
  684.9 179.3 %copy-start.16 = (bf16[512,2048]{1,0:T(8,128)(2,1)S(1)}, bf16[512,2048]{1,0:T(8,128)(2,1)}, u32[]{:S(2)}) copy-start(bf16[512,2048]{1,0:T(8,128)(2,1)} %get-tuple-element.224) | copy-start | bytes 6291460
  684.9 179.3 %copy-start.40 = (f32[512]{0:T(512)S(1)}, f32[512]{0:T(512)}, u32[]{:S(2)}) copy-start(f32[512]{0:T(512)} %copy-done.39) | copy-start | bytes 6148
  684.9 186.1 %collective-permute-start.21 = (f32[1,512,1024]{2,0,1:T(1,128)}, f32[1,512,1024]{2,0,1:T(1,128)S(1)}, u32[]{:S(2)}, u32[]{:S(2)}) collective-permute-start(f32[1,512,1024]{2,0,1:T(1,128)} %get-tuple-element.235), channel_id=1, source_target_pairs={{0,28},{2,30},{4,0},{6,2},{8,4},{10,6},{12,8},{14,10},{16,12},{18,... | collective-permute-start | bytes 6291464 | tf_op jit(solution)/shard_map/ppermute | solution.py:24
  790.8 80.2 %collective-permute-start.22 = (f32[1,512,1024]{2,0,1:T(1,128)}, f32[1,512,1024]{2,0,1:T(1,128)S(1)}, u32[]{:S(2)}, u32[]{:S(2)}) collective-permute-start(f32[1,512,1024]{2,0,1:T(1,128)} %get-tuple-element.240), channel_id=1, source_target_pairs={{0,26},{2,28},{4,30},{6,0},{8,2},{10,4},{12,6},{14,8},{16,10},{18,... | collective-permute-start | bytes 6291464 | tf_op jit(solution)/shard_map/ppermute | solution.py:24
  835.3 49.8 %collective-permute-start.23 = (f32[1,512,1024]{2,0,1:T(1,128)}, f32[1,512,1024]{2,0,1:T(1,128)S(1)}, u32[]{:S(2)}, u32[]{:S(2)}) collective-permute-start(f32[1,512,1024]{2,0,1:T(1,128)} %fusion.14), channel_id=1, source_target_pairs={{0,24},{2,26},{4,28},{6,30},{8,0},{10,2},{12,4},{14,6},{16,8},{18,... | collective-permute-start | bytes 6291464 | tf_op jit(solution)/shard_map/ppermute | solution.py:24
  (75 other events, 1157.4 us)
Sparse Core Ops, SparseCore 0:
  901.1 280.9 all-reduce.3
where the time goes:
time: 1210 us; the launch traced here: 1200 us
  waiting for transfers between devices  433 us (36%)
  matrix products  235 us (19%)
  other arithmetic  184 us (15%)
  local copies, waits for them, and re-layouts  134 us (11%)
  starting transfers between devices  108 us (9%)
  blocking collectives  88.1 us (7%)
  between operations  17.7 us (1%)
    ppermute x24, waiting for transfers between devices, passed_along(): return lax.ppermute(value, axis, pairs)  252 us
    psum x1, waiting for transfers between devices, on_device(): lax.psum((grad_query, grad_keyval, grad_output, grad_up, grad_bias_up, gr...  181 us
    ppermute x24, starting transfers between devices, passed_along(): return lax.ppermute(value, axis, pairs)  108 us
    psum x1, blocking collectives, on_device(): lax.psum((grad_query, grad_keyval, grad_output, grad_up, grad_bias_up, gr...  88.1 us
    dot_general x8, matrix products, pair_scores(): jnp.einsum('rhe,khe->hrk', query_heads, key_heads, preferred_element_type...  79.8 us
    convert_element_type x4, other arithmetic, backward_pair(): score_grad = (attention_full * (score_dot - row_dots)).astype(jnp.bfloat16)  70.9 us
    dot_general x4, matrix products, forward_pair(): jnp.einsum('hrk,khe->rhe', attention, value_heads, preferred_element_type...  36.1 us
    another operation x3, other arithmetic  35.1 us
  transfers between devices with their start and end apart: 25, of which 12 were waited for; matrix products, arithmetic and copies ran while one was open for 3% of the time, Pallas kernels for 0%

commit v1 on v0

v1 whole, which is shorter than its diff:
```python
import functools

import jax
import jax.numpy as jnp
from jax import lax
from jax.experimental import pallas as pl
from jax.experimental.pallas import tpu as pltpu
from jax.sharding import PartitionSpec as P

D = 512
HEADS = 8
HEAD_DIM = 64
PAIRS = HEADS // 2
PAIR = 2 * HEAD_DIM
VIEWS = 5
PATCHES = 400
LANG = 77
ROWS = 512
USED = 480
TAIL = USED - PATCHES
SENT = 496
KEYS = VIEWS * PATCHES + TAIL
KEYS_PADDED = 2176
FF = 2048
FF_BLOCK = 512
NEGATIVE = -1e30
EPSILON = 1e-5
CHUNKS = 6
CHUNK_ROWS = 1024

BF16 = jnp.bfloat16
F32 = jnp.float32
MESH = pl.DeviceIdType.MESH
NN = (((1,), (0,)), ((), ()))
NT = (((1,), (1,)), ((), ()))
TN = (((0,), (0,)), ((), ()))
TT = (((0,), (1,)), ((), ()))
MIB = 2**20

VMEM = pltpu.VMEM
IN_VMEM = pl.BlockSpec(memory_space=pltpu.VMEM)
IN_SMEM = pl.BlockSpec(memory_space=pltpu.SMEM)
ANYWHERE = pl.BlockSpec(memory_space=pl.ANY)


def dot(left, right, dims):
    return lax.dot_general(left, right, dims, preferred_element_type=F32)


def normalise(values):
    average = jnp.mean(values, -1, keepdims=True)
    centered = values - average
    variance = jnp.mean(centered * centered, -1, keepdims=True)
    scale = lax.rsqrt(variance + EPSILON)
    return centered * scale, scale


def norm_backward(grad, unit, scale, gain):
    grad = grad * gain
    first = jnp.mean(grad, -1, keepdims=True)
    second = jnp.mean(grad * unit, -1, keepdims=True)
    return scale * (grad - first - unit * second)


def greet(others):
    barrier = pltpu.get_barrier_semaphore()
    for other in others:
        pl.semaphore_signal(barrier, inc=1, device_id=other, device_id_type=MESH)
    pl.semaphore_wait(barrier, len(others))


def gather_kernel(count, block, window, own_sem, send_sem, recv_sem, pass_sem, given_sem):
    me = lax.axis_index("view")
    step = 1 - 2 * lax.rem(me, 2)

    def at(offset):
        return {"view": lax.rem(me + offset + count, count)}

    far = (4, -4, 2, -2)
    greet([at(offset) for offset in far] + [at(step)])
    own = pltpu.make_async_copy(block, window.at[4], own_sem)
    own.start()

    def to(k, offset):
        return pltpu.make_async_remote_copy(
            block, window.at[4 - offset], send_sem.at[k], recv_sem.at[k], at(offset), MESH
        )

    def across(k, offset, source):
        return pltpu.make_async_remote_copy(
            source,
            window.at[4 + offset - step],
            pass_sem.at[k],
            given_sem.at[k],
            at(step),
            MESH,
        )

    sends = [to(k, offset) for k, offset in enumerate(far)]
    for copy in sends:
        copy.start()
    passes = [across(0, 0, block)]
    passes[0].start()
    for k, offset in ((2, -2), (3, 2)):
        sends[k].wait_recv()
        copy = across(k - 1, offset, window.at[4 + offset])
        copy.start()
        passes.append(copy)
    even = lax.rem(me, 2) == 0
    for k in (0, 1):
        sends[k].wait_recv()
    copy = across(3, 4 * step, window.at[4 + 4 * step])
    copy.start()
    passes.append(copy)
    for copy in passes:
        copy.wait()
    for copy in sends:
        copy.wait_send()
    own.wait()


def gather_window(block, count):
    return pl.pallas_call(
        functools.partial(gather_kernel, count),
        out_shape=jax.ShapeDtypeStruct((2 * VIEWS - 1, SENT, D), BF16),
        in_specs=[ANYWHERE],
        out_specs=ANYWHERE,
        scratch_shapes=[pltpu.SemaphoreType.DMA] + [pltpu.SemaphoreType.DMA((4,))] * 4,
        compiler_params=pltpu.CompilerParams(collective_id=0, has_side_effects=True),
        name="gather_window",
    )(block)


def compute_kernel(
    view,
    filled,
    window,
    cotangent,
    w_query,
    w_keyval,
    w_output,
    w_up,
    bias_up,
    w_down,
    bias_down,
    gain_attn,
    shift_attn,
    gain_mlp,
    shift_mlp,
    block_output,
    residual_grad,
    grads,
    sums_up,
    sums,
    parts,
    own_part,
    normed_all,
    query_norm,
    key_bias,
    keyval,
    query,
    weights,
    mixed,
    inverse,
    keyval_grad,
    query_grad,
    mixed_grad,
    normed_mlp,
    branch_grad,
    branch,
    mlp_back,
    blocks,
    block_sem,
):
    my_view = view[0]
    my_filled = filled[0]
    gain_a = gain_attn[...].astype(F32)
    shift_a = shift_attn[...].astype(F32)
    gain_m = gain_mlp[...].astype(F32)
    shift_m = shift_mlp[...].astype(F32)

    copies = []
    for j in range(VIEWS):
        slot = jnp.where(my_view + j < VIEWS, 4 + j, j - 1)
        copies.append(pltpu.make_async_copy(window.at[slot], blocks.at[j], block_sem.at[j]))
        copies[-1].start()
    copies[0].wait()
    own_rows = blocks[0, :USED, :]
    own_unit, _ = normalise(own_rows.astype(F32))
    own_normed = (own_unit * gain_a + shift_a).astype(BF16)
    query_norm[...] = own_normed
    normed_all[:PATCHES, :] = own_normed[:PATCHES, :]
    my_label = blocks[0, USED:SENT, :PAIR].astype(F32)

    def bias_of(label):
        match = jnp.logical_and(label == my_label, label >= 0)
        return jnp.where(match, 0.0, NEGATIVE)[:1, :]

    key_bias[:PATCHES, :] = jnp.broadcast_to(bias_of(my_label), (PATCHES, PAIR)).astype(BF16)
    language = own_rows[PATCHES:, :]
    language_bias = bias_of(my_label)
    for j in range(1, VIEWS):
        copies[j].wait()
        block = blocks[j, :USED, :]
        label = blocks[j, USED:SENT, :PAIR].astype(F32)
        unit, _ = normalise(block[:PATCHES, :].astype(F32))
        rows = slice(j * PATCHES, (j + 1) * PATCHES)
        normed_all[rows, :] = (unit * gain_a + shift_a).astype(BF16)
        bias = bias_of(label)
        key_bias[rows, :] = jnp.broadcast_to(bias, (PATCHES, PAIR)).astype(BF16)
        holds = lax.rem(my_view + j, VIEWS) == 0
        language = jnp.where(holds, block[PATCHES:, :], language)
        language_bias = jnp.where(holds, bias, language_bias)
    unit, _ = normalise(language.astype(F32))
    normed_all[VIEWS * PATCHES : KEYS, :] = (unit * gain_a + shift_a).astype(BF16)
    index = lax.broadcasted_iota(jnp.int32, (TAIL, PAIR), 0)
    key_bias[VIEWS * PATCHES : KEYS, :] = jnp.where(
        index < LANG, jnp.broadcast_to(language_bias, (TAIL, PAIR)), NEGATIVE
    ).astype(BF16)
    normed_all[KEYS:, :] = jnp.zeros((KEYS_PADDED - KEYS, D), BF16)
    key_bias[KEYS:, :] = jnp.full((KEYS_PADDED - KEYS, PAIR), NEGATIVE, BF16)

    query[...] = (dot(own_normed, w_query[...], NN).astype(BF16) * HEAD_DIM**-0.5).astype(BF16)
    for c in range(2):
        columns = slice(c * D, (c + 1) * D)
        keyval[:, columns] = dot(normed_all[...], w_keyval[:, columns], NN).astype(BF16)

    lane = lax.broadcasted_iota(jnp.int32, (1, PAIR), 1)
    low_half = lane < HEAD_DIM

    def half_of(half, first, second):
        return jnp.where(low_half, first, second) if half == 0 else jnp.where(low_half, second, first)

    def head_keys(p, half):
        pair = keyval[:, pl.ds(pl.multiple_of(p * PAIR, PAIR), PAIR)]
        return half_of(half, pair, key_bias[...])

    def head_values(p, half):
        pair = keyval[:, pl.ds(pl.multiple_of(D + p * PAIR, PAIR), PAIR)]
        return half_of(half, pair, jnp.ones((), BF16))

    def forward_pair(p, _):
        columns = pl.ds(pl.multiple_of(p * PAIR, PAIR), PAIR)
        pair = query[:, columns]
        outs = []
        totals = []
        for half in range(2):
            one = (lane == HEAD_DIM * (1 - half)).astype(BF16)
            scores = dot(half_of(half, pair, one), head_keys(p, half), NT)
            top = jnp.max(scores, -1, keepdims=True)
            weight = jnp.exp(scores - top).astype(BF16)
            weights[2 * p + half] = weight
            out = dot(weight, head_values(p, half), NN)
            outs.append(out)
            totals.append(pltpu.roll(out, HEAD_DIM, 1))
        inv = 1.0 / jnp.where(low_half, totals[0], totals[1])
        full = jnp.where(low_half, outs[0], outs[1]) * inv
        inverse[:, columns] = inv
        own_part[:, columns] = full
        mixed[:, columns] = full.astype(BF16)
        return 0

    lax.fori_loop(0, PAIRS, forward_pair, 0)

    row = lax.broadcasted_iota(jnp.int32, (USED, PAIR), 0)
    has_language = (my_view == 0).astype(jnp.int32)
    live_rows = my_filled * (PATCHES + LANG * has_language)
    live = (row < live_rows).astype(F32)[:, :1]
    own = own_rows.astype(F32)
    res = own + live * dot(mixed[...], w_output[...], NN)
    residual_grad[...] = res
    unit_m, scale_m = normalise(res)
    normed_mlp[...] = (unit_m * gain_m + shift_m).astype(BF16)
    upstream = cotangent[:USED, :].astype(F32)
    branch_grad[...] = (live * upstream).astype(BF16)
    branch[...] = jnp.zeros((USED, D), F32)
    mlp_back[...] = jnp.zeros((USED, D), F32)

    def feed_forward(c, _):
        columns = pl.ds(pl.multiple_of(c * FF_BLOCK, FF_BLOCK), FF_BLOCK)
        before = dot(normed_mlp[...], w_up[:, columns], NN) + bias_up[:, columns].astype(F32)
        chance = 0.5 + 0.5 * lax.erf(before * 0.5**0.5)
        density = jnp.exp(-0.5 * before * before) * 0.3989422804014327
        activated = (before * chance).astype(BF16)
        slope = chance + before * density
        grads[pl.ds(pl.multiple_of(FF + c * FF_BLOCK, FF_BLOCK), FF_BLOCK), :] = dot(
            activated, branch_grad[...], TN
        ).astype(BF16)
        branch[...] += dot(activated, w_down[columns, :], NN)
        before_full = dot(branch_grad[...], w_down[columns, :], NT) * slope
        before_grad = before_full.astype(BF16)
        sums_up[:, columns] = jnp.sum(before_grad.astype(F32), 0, keepdims=True)
        grads[columns, :] = dot(normed_mlp[...], before_grad, TN).astype(BF16)
        mlp_back[...] += dot(before_grad, w_up[:, columns], NT)
        return 0

    lax.fori_loop(0, FF // FF_BLOCK, feed_forward, 0)
    block_output[:USED, :] = (
        residual_grad[...] + live * (branch[...] + bias_down[...].astype(F32))
    ).astype(BF16)
    block_output[USED:, :] = jnp.zeros((ROWS - USED, D), BF16)
    unit_m, scale_m = normalise(residual_grad[...])
    back = mlp_back[...]
    sums[0:1, :] = jnp.sum(branch_grad[...].astype(F32), 0, keepdims=True)
    sums[1:2, :] = jnp.sum(back * unit_m, 0, keepdims=True)
    sums[2:3, :] = jnp.sum(back, 0, keepdims=True)
    res_grad = upstream + norm_backward(back, unit_m, scale_m, gain_m)
    residual_grad[...] = res_grad
    attended_grad = (live * res_grad).astype(BF16)
    grads[2 * FF : 2 * FF + D, :] = dot(mixed[...], attended_grad, TN).astype(BF16)
    mixed_grad[...] = dot(attended_grad, w_output[...], NT).astype(BF16)

    def backward_pair(p, _):
        columns = pl.ds(pl.multiple_of(p * PAIR, PAIR), PAIR)
        grad = mixed_grad[:, columns].astype(F32)
        inv = inverse[:, columns]
        scaled = grad * inv
        product = scaled * own_part[:, columns]
        scaled_low = scaled.astype(BF16)
        scaled_t = scaled.T.astype(BF16)
        query_t = query[:, columns].astype(F32).T.astype(BF16)
        query_parts = []
        for half in range(2):
            here = low_half if half == 0 else jnp.logical_not(low_half)
            dots = -jnp.sum(jnp.where(here, product, 0.0), -1, keepdims=True)
            dots_high = dots.astype(BF16)
            dots_low = (dots - dots_high.astype(F32)).astype(BF16)
            other = HEAD_DIM * (1 - half)
            rest = jnp.where(
                lane == other, dots_high, jnp.where(lane == other + 1, dots_low, jnp.zeros((), BF16))
            )
            weight = weights[2 * p + half]
            slope = dot(half_of(half, scaled_low, rest), head_values(p, half), NT)
            score_grad = weight * slope.astype(BF16)
            query_parts.append(dot(score_grad, head_keys(p, half), NN))
            rows = slice(half * HEAD_DIM, (half + 1) * HEAD_DIM)
            start = pl.multiple_of(p * PAIR, PAIR) + half * HEAD_DIM
            keyval_grad[pl.ds(start, HEAD_DIM), :] = dot(query_t[rows, :], score_grad, NN).astype(
                BF16
            )
            keyval_grad[pl.ds(D + start, HEAD_DIM), :] = dot(
                scaled_t[rows, :], weight, NN
            ).astype(BF16)
        part = jnp.where(low_half, query_parts[0], query_parts[1]) * HEAD_DIM**-0.5
        query_grad[:, columns] = part.astype(BF16)
        return 0

    lax.fori_loop(0, PAIRS, backward_pair, 0)

    base = 2 * FF + D
    grads[base : base + D, :] = dot(query_norm[...], query_grad[...], TN).astype(BF16)
    for c in range(2):
        rows = slice(c * D, (c + 1) * D)
        grads[base + D + c * D : base + 2 * D + c * D, :] = dot(
            keyval_grad[rows, :], normed_all[...], NN
        ).astype(BF16)
    from_query = dot(query_grad[...], w_query[...], NT)
    normed = query_norm[...].astype(F32)
    shift_sum = jnp.sum(from_query, 0, keepdims=True)
    gain_sum = jnp.sum(from_query * normed, 0, keepdims=True)
    parts_at = []
    for j in range(VIEWS + 1):
        rows = slice(j * PATCHES, min((j + 1) * PATCHES, KEYS))
        piece = dot(keyval_grad[:, rows], w_keyval[...], TT)
        normed = normed_all[rows, :].astype(F32)
        shift_sum += jnp.sum(piece, 0, keepdims=True)
        gain_sum += jnp.sum(piece * normed, 0, keepdims=True)
        if j == 0:
            own_part[:PATCHES, :] = from_query[:PATCHES, :] + piece
        elif j < VIEWS:
            parts[j - 1, :PATCHES, :] = piece.astype(BF16)
        else:
            own_part[PATCHES:, :] = from_query[PATCHES:, :] + jnp.where(my_view == 0, piece, 0.0)
            for i in range(1, VIEWS):
                holds = lax.rem(my_view + i, VIEWS) == 0
                parts[i - 1, PATCHES:, :] = jnp.where(holds, piece, 0.0).astype(BF16)
    sums[3:4, :] = (gain_sum - shift_a * shift_sum) / gain_a
    sums[4:5, :] = shift_sum
    sums[5:8, :] = jnp.zeros((3, D), F32)


def compute(*args):
    shape = jax.ShapeDtypeStruct
    outs = (
        shape((ROWS, D), BF16),
        shape((USED, D), F32),
        shape((CHUNKS * CHUNK_ROWS, D), BF16),
        shape((1, FF), F32),
        shape((8, D), F32),
        shape((VIEWS - 1, USED, D), BF16),
        shape((USED, D), F32),
    )
    scratch = [
        VMEM((KEYS_PADDED, D), BF16),
        VMEM((USED, D), BF16),
        VMEM((KEYS_PADDED, PAIR), BF16),
        VMEM((KEYS_PADDED, 2 * D), BF16),
        VMEM((USED, D), BF16),
        VMEM((HEADS, USED, KEYS_PADDED), BF16),
        VMEM((USED, D), BF16),
        VMEM((USED, D), F32),
        VMEM((2 * D, KEYS_PADDED), BF16),
        VMEM((USED, D), BF16),
        VMEM((USED, D), BF16),
        VMEM((USED, D), BF16),
        VMEM((USED, D), BF16),
        VMEM((USED, D), F32),
        VMEM((USED, D), F32),
        VMEM((VIEWS, SENT, D), BF16),
        pltpu.SemaphoreType.DMA((VIEWS,)),
    ]
    return pl.pallas_call(
        compute_kernel,
        out_shape=outs,
        in_specs=[IN_SMEM] * 2 + [ANYWHERE] + [IN_VMEM] * (len(args) - 3),
        out_specs=[IN_VMEM] * len(outs),
        scratch_shapes=scratch,
        compiler_params=pltpu.CompilerParams(vmem_limit_bytes=63 * MIB),
        name="compute",
    )(*args)


def on_device(count, tokens, counts, slot_item, slot_view, keyframe, *rest):
    weights, cotangent = rest[:-1], rest[-1]
    rows = tokens.reshape(ROWS, D)
    item = slot_item.reshape(())
    filled = (counts.reshape(()) > 0) & (keyframe.reshape(()) == 1) & (item >= 0)
    label = jnp.where(filled, item, -1).astype(BF16)
    block = jnp.concatenate([rows[:USED], jnp.broadcast_to(label, (SENT - USED, D))])
    window = gather_window(block, count)
    weights = tuple(w.reshape(1, -1) if w.ndim == 1 else w for w in weights)
    cot = cotangent.reshape(ROWS, D)
    block_output, residual_grad, grads, sums_up, sums, parts, own_part = compute(
        slot_view.reshape(1), filled.astype(jnp.int32).reshape(1), window, cot, *weights
    )
    block_output = jnp.concatenate([block_output[:USED], rows[USED:]])
    view = slot_view.reshape(())
    total = own_part
    for offset in range(1 - VIEWS, VIEWS):
        if offset != 0:
            valid = (view + offset >= 0) & (view + offset < VIEWS)
            sent = jnp.where(valid, parts[(offset + VIEWS) % VIEWS - 1], 0)
            pairs = [(source, (source + offset) % count) for source in range(count)]
            total = total + lax.ppermute(sent, "view", pairs).astype(F32)
    gain = rest[7].astype(F32)
    unit, scale = normalise(rows[:USED].astype(F32))
    used = residual_grad + norm_backward(total, unit, scale, gain)
    grad_tokens = jnp.concatenate([used, cot[USED:].astype(F32)])
    grads, sums_up, sums = lax.psum((grads.astype(F32), sums_up, sums), ("view", "dp"))
    return (
        block_output.reshape(tokens.shape),
        grad_tokens.reshape(tokens.shape),
        grads[2 * FF + D : 2 * FF + 2 * D],
        grads[2 * FF + 2 * D :].T,
        grads[2 * FF : 2 * FF + D],
        jnp.concatenate([grads[c * D : (c + 1) * D] for c in range(FF // D)], 1),
        sums_up.reshape(-1),
        grads[FF : 2 * FF],
        sums[0],
        sums[3],
        sums[4],
        sums[1],
        sums[2],
    )


def solution(mesh):
    count = mesh.shape["view"]
    slots = P("dp", "view", None)
    rows = P("dp", "view", None, None, None)
    in_specs = (rows, P("dp", "view"), slots, slots, slots) + (P(),) * 11 + (rows,)
    out_specs = (rows, rows) + (P(),) * 11
    return jax.shard_map(
        functools.partial(on_device, count),
        mesh=mesh,
        in_specs=in_specs,
        out_specs=out_specs,
        check_vma=False,
    )
```

time: 1210 us -> 409 us (0.34)
  waiting for transfers between devices: 433 us -> 13 us
  matrix products: 235 us -> 0 us
  other arithmetic: 184 us -> 14.5 us
  blocking collectives: 88.1 us -> 240 us
  local copies, waits for them, and re-layouts: 134 us -> 24 us
  Pallas kernels: 0 us -> 104 us
  starting transfers between devices: 108 us -> 9.18 us
  between operations: 17.7 us -> 3.51 us
    ppermute x24 -> x8, waiting for transfers between devices: 252 us -> 13 us  [on_device(): total = total + lax.ppermute(sent, 'view', pairs).astype(F32)]
    dot_general x43 -> x0, matrix products: 235 us -> none  [the longest x8 79.8 us: pair_scores(): jnp.einsum('rhe,khe->hrk', query_heads, key_heads, preferred_element_type...]
    psum x1 -> x0, waiting for transfers between devices: 181 us -> none  [on_device(): lax.psum((grad_query, grad_keyval, grad_output, grad_up, grad_bias_up, gr...]
    psum x1, blocking collectives: 88.1 us -> 240 us  [on_device(): lax.psum((grads.astype(F32), sums_up, sums), ('view', 'dp'))]
    pallas_call x0 -> x2, Pallas kernels: none -> 104 us  [the longest x1 59.9 us: compute(): pl.pallas_call(compute_kernel, out_shape=outs, in_specs=[IN_SMEM] * 2 + [...]
    ppermute x24 -> x8, starting transfers between devices: 108 us -> 9.18 us  [on_device(): total = total + lax.ppermute(sent, 'view', pairs).astype(F32)]
    convert_element_type x15 -> x2, other arithmetic: 84.5 us -> 0.77 us  [the longest x1 0.77 us: on_device(): grad_tokens = jnp.concatenate([used, cot[USED:].astype(F32)])]
    another operation x3 -> x0, other arithmetic: 35.1 us -> none
  transfers between devices with their start and end apart: 25 -> 8, of which waited for: 12 -> 2; matrix products, arithmetic and copies ran while one was open for 3% -> 5% of each run, Pallas kernels for 0% -> 0%
where the time goes in v1:
time: 409 us; the launch traced here: 408 us
  blocking collectives  240 us (59%)
  Pallas kernels  104 us (25%)
  local copies, waits for them, and re-layouts  24 us (6%)
  other arithmetic  14.5 us (4%)
  waiting for transfers between devices  13 us (3%)
  starting transfers between devices  9.18 us (2%)
    psum x1, blocking collectives, on_device(): lax.psum((grads.astype(F32), sums_up, sums), ('view', 'dp'))  240 us
    pallas_call x1, Pallas kernels, compute(): pl.pallas_call(compute_kernel, out_shape=outs, in_specs=[IN_SMEM] * 2 + [...  59.9 us
    pallas_call x1, Pallas kernels, gather_window(): pl.pallas_call(functools.partial(gather_kernel, count), out_shape=jax.Sha...  43.8 us
    ppermute x8, waiting for transfers between devices, on_device(): total = total + lax.ppermute(sent, 'view', pairs).astype(F32)  13 us
    ppermute x8, starting transfers between devices, on_device(): total = total + lax.ppermute(sent, 'view', pairs).astype(F32)  9.18 us
  transfers between devices with their start and end apart: 8, of which 2 were waited for; matrix products, arithmetic and copies ran while one was open for 5% of the time, Pallas kernels for 0%

profile of v1, /device:TPU:0, one launch (start us, length us, event | category | flops | bytes accessed | tf_op | source)
XLA Modules:
  0.0 407.9 jit_solution(15947464065957783897)
XLA Ops:
  3.3 1.3 reshape.187.bias_down
  4.5 1.3 reshape.189.shift_attn
  5.8 1.3 reshape.190.gain_mlp
  7.1 1.3 reshape.191.shift_mlp
  8.3 1.3 reshape.188.gain_attn
  9.6 1.3 reshape.186.bias_up
  10.9 1.1 slice_bitcast_fusion.1
  11.9 0.8 concatenate.12.block
  12.8 43.8 %gather_window.1.window = bf16[9,496,512]{2,1,0:T(8,128)(2,1)} custom-call(bf16[496,512]{1,0:T(8,128)(2,1)} %concatenate.12.block), custom_call_target="tpu_custom_call" | custom-call | tf_op jit(solution)/shard_map/gather_window/pallas_call | solution.py:123
  56.6 59.9 %compute.1 = (bf16[512,512]{1,0:T(8,128)(2,1)}, f32[480,512]{1,0:T(8,128)}, bf16[6144,512]{1,0:T(8,128)(2,1)}, f32[1,2048]{1,0:T(1,128)}, f32[8,512]{1,0:T(8,128...) custom-call(s32[1]{0:T(128)} %bitcast.59.view, s32[1]{0:T(128)} %bitcast.4.filled, ...), custom_call_target="tpu_custom_call" | custom-call | tf_op jit(solution)/shard_map/compute/pallas_call | solution.py:412
  116.6 0.0 copy-start
  116.6 0.0 copy-start.6
  116.6 0.0 copy-start.7
  116.6 3.5 select_bitcast_fusion.7
  120.1 1.0 collective-permute-start
  121.2 0.1 collective-permute-start.4
  121.2 2.5 collective-permute-start.5
  123.8 0.0 collective-permute-start.6
  123.8 0.7 collective-permute-start.7
  124.4 0.1 convert_reduce_fusion
  124.6 0.8 bitcast_convert_fusion
  125.4 0.0 copy-done.6
  125.4 240.0 %all-reduce.3 = (f32[6144,512]{1,0:T(8,128)}, f32[2048]{0:T(1024)}, f32[8,512]{1,0:T(8,128)S(1)}) all-reduce(bf16[6144,512]{1,0:T(8,128)(2,1)} %get-tuple-element.24, f32[2048]{0:T(1024)S(1)} %bitcast.61, f32[8,512]{1,0:T(8,128)S(1)} %copy-done.6), channel_id=1, replica_groups=mesh['view'=16,'dp'=2] {'view','dp'}, use_global_device_ids=true, to_apply=%region_4.5 | all-reduce | flops 3151872 | bytes 18923520 | tf_op jit(solution)/shard_map/psum | solution.py:449
  365.4 0.6 fusion.11
  366.0 1.8 slice_bitcast_fusion
  367.8 0.3 fusion.8
  368.1 5.5 %fusion.10 = (f32[512,512]{1,0:T(8,128)}, f32[512,512]{1,0:T(8,128)}, f32[512,512]{1,0:T(8,128)}, f32[512,512]{1,0:T(8,128)}, f32[512,512]{1,0:T(8,128)}, /*index=5*/f32[512,512]{1,0:T(8,128)}) fusion(f32[6144,512]{1,0:T(8,128)} %get-tuple-element.42), kind=kLoop, calls=%fused_computation.32 | loop fusion | bytes 12582912 | tf_op jit(solution)/shard_map/slice | solution.py:456
  373.7 0.0 collective-permute-done
  373.7 2.3 collective-permute-start.3
  376.0 0.0 collective-permute-done.4
  376.0 2.6 collective-permute-start.2
  378.5 0.0 collective-permute-done.5
  378.5 0.0 collective-permute-start.1
  378.6 0.0 copy-start.5
  378.6 4.7 %slice.105 = f32[2048,512]{1,0:T(8,128)} slice(f32[6144,512]{1,0:T(8,128)} %get-tuple-element.42), slice={[2048:4096], [0:512]} | slice | bytes 8388608 | tf_op jit(solution)/shard_map/slice | solution.py:458
  383.3 0.0 copy-done.5
  383.3 1.8 copy.30
  385.1 0.8 maximum_bitcast_fusion.1
  386.0 4.7 %pad_maximum_fusion = f32[512,2048]{1,0:T(8,128)} fusion(f32[512,512]{1,0:T(8,128)} %get-tuple-element.47, f32[512,512]{1,0:T(8,128)} %get-tuple-element.48, f32[512,512]{1,0:T(8,128)} %get-tuple-element.49, f32[512,512]{1,0:T(8,128)} %get-tuple-element.46), kind=kLoop, calls=%fused_computation | loop fusion | flops 3145728 | bytes 8388608 | tf_op jit(solution)/shard_map/concatenate | solution.py:456
  390.7 0.0 collective-permute-done.6
  390.7 0.0 collective-permute-done.7
  390.7 0.0 collective-permute-done.3
  390.7 7.5 %collective-permute-done.2 = bf16[480,512]{1,0:T(8,128)(2,1)} collective-permute-done((bf16[480,512]{1,0:T(8,128)(2,1)}, bf16[480,512]{1,0:T(8,128)(2,1)}, u32[]{:S(2)}, u32[]{:S(2)}) %collective-permute-start.2) | collective-permute-done | bytes 491552 | tf_op jit(solution)/shard_map/ppermute | solution.py:444
  398.2 5.5 %collective-permute-done.1 = bf16[480,512]{1,0:T(8,128)(2,1)} collective-permute-done((bf16[480,512]{1,0:T(8,128)(2,1)}, bf16[480,512]{1,0:T(8,128)(2,1)}, u32[]{:S(2)}, u32[]{:S(2)}) %collective-permute-start.1) | collective-permute-done | bytes 491552 | tf_op jit(solution)/shard_map/ppermute | solution.py:444
  403.7 0.0 copy-done.1
  403.7 2.8 fusion.9
  406.5 0.4 fusion.7
  406.9 1.0 maximum_bitcast_fusion
  (17 shorter events, 0.1 us)
Async XLA Ops:
  116.6 7.9 %copy-start = (bf16[1,1,1,512,512]{4,3,2,1,0:T(8,128)(2,1)S(1)}, bf16[1,1,1,512,512]{4,3,2,1,0:T(8,128)(2,1)}, u32[]{:S(2)}) copy-start(bf16[1,1,1,512,512]{4,3,2,1,0:T(8,128)(2,1)} %param.17) | copy-start | bytes 1572868
  116.6 8.8 %copy-start.6 = (f32[8,512]{1,0:T(8,128)S(1)}, f32[8,512]{1,0:T(8,128)}, u32[]{:S(2)}) copy-start(f32[8,512]{1,0:T(8,128)} %get-tuple-element.26) | copy-start | bytes 49156
  116.6 8.8 %copy-start.7 = (f32[1,2048]{1,0:T(1,128)S(1)}, f32[1,2048]{1,0:T(1,128)}, u32[]{:S(2)}) copy-start(f32[1,2048]{1,0:T(1,128)} %get-tuple-element.25) | copy-start | bytes 24580
  120.1 253.5 %collective-permute-start = (bf16[480,512]{1,0:T(8,128)(2,1)}, bf16[480,512]{1,0:T(8,128)(2,1)S(1)}, u32[]{:S(2)}, u32[]{:S(2)}) collective-permute-start(bf16[480,512]{1,0:T(8,128)(2,1)} %get-tuple-element.52), channel_id=1, source_target_pairs={{0,24},{2,26},{4,28},{6,30},{8,0},{10,2},{12,4},{14,6},{16,8},{18,... | collective-permute-start | bytes 1474568 | tf_op jit(solution)/shard_map/ppermute | solution.py:444
  121.2 254.8 %collective-permute-start.4 = (bf16[480,512]{1,0:T(8,128)(2,1)}, bf16[480,512]{1,0:T(8,128)(2,1)}, u32[]{:S(2)}, u32[]{:S(2)}) collective-permute-start(bf16[480,512]{1,0:T(8,128)(2,1)} %get-tuple-element.53), channel_id=1, source_target_pairs={{0,2},{2,4},{4,6},{6,8},{8,10},{10,12},{12,14},{14,16},{16,18},{18... | collective-permute-start | bytes 1474568 | tf_op jit(solution)/shard_map/ppermute | solution.py:444
  121.2 257.3 %collective-permute-start.5 = (bf16[480,512]{1,0:T(8,128)(2,1)}, bf16[480,512]{1,0:T(8,128)(2,1)}, u32[]{:S(2)}, u32[]{:S(2)}) collective-permute-start(bf16[480,512]{1,0:T(8,128)(2,1)} %get-tuple-element.54), channel_id=1, source_target_pairs={{0,4},{2,6},{4,8},{6,10},{8,12},{10,14},{12,16},{14,18},{16,20},{1... | collective-permute-start | bytes 1474568 | tf_op jit(solution)/shard_map/ppermute | solution.py:444
  123.8 266.9 %collective-permute-start.6 = (bf16[480,512]{1,0:T(8,128)(2,1)}, bf16[480,512]{1,0:T(8,128)(2,1)}, u32[]{:S(2)}, u32[]{:S(2)}) collective-permute-start(bf16[480,512]{1,0:T(8,128)(2,1)} %get-tuple-element.55), channel_id=1, source_target_pairs={{0,6},{2,8},{4,10},{6,12},{8,14},{10,16},{12,18},{14,20},{16,22},{... | collective-permute-start | bytes 1474568 | tf_op jit(solution)/shard_map/ppermute | solution.py:444
  123.8 266.9 %collective-permute-start.7 = (bf16[480,512]{1,0:T(8,128)(2,1)}, bf16[480,512]{1,0:T(8,128)(2,1)}, u32[]{:S(2)}, u32[]{:S(2)}) collective-permute-start(bf16[480,512]{1,0:T(8,128)(2,1)} %get-tuple-element.56), channel_id=1, source_target_pairs={{0,8},{2,10},{4,12},{6,14},{8,16},{10,18},{12,20},{14,22},{16,24},... | collective-permute-start | bytes 1474568 | tf_op jit(solution)/shard_map/ppermute | solution.py:444
  368.1 10.4 %copy-start.8 = (bf16[512]{0:T(512)(128)(2,1)S(1)}, bf16[512]{0:T(512)(128)(2,1)}, u32[]{:S(2)}) copy-start(bf16[512]{0:T(512)(128)(2,1)} %param.29) | copy-start | bytes 3076
  373.7 9.6 %copy-start.3 = (bf16[480,512]{1,0:T(8,128)(2,1)}, bf16[480,512]{1,0:T(8,128)(2,1)S(1)}, u32[]{:S(2)}) copy-start(bf16[480,512]{1,0:T(8,128)(2,1)S(1)} %collective-permute-done) | copy-start | bytes 1474564
  373.7 17.0 %collective-permute-start.3 = (bf16[480,512]{1,0:T(8,128)(2,1)}, bf16[480,512]{1,0:T(8,128)(2,1)}, u32[]{:S(2)}, u32[]{:S(2)}) collective-permute-start(bf16[480,512]{1,0:T(8,128)(2,1)} %get-tuple-element.57), channel_id=1, source_target_pairs={{0,30},{2,0},{4,2},{6,4},{8,6},{10,8},{12,10},{14,12},{16,14},{18,... | collective-permute-start | bytes 1474568 | tf_op jit(solution)/shard_map/ppermute | solution.py:444
  376.0 22.2 %collective-permute-start.2 = (bf16[480,512]{1,0:T(8,128)(2,1)}, bf16[480,512]{1,0:T(8,128)(2,1)}, u32[]{:S(2)}, u32[]{:S(2)}) collective-permute-start(bf16[480,512]{1,0:T(8,128)(2,1)} %get-tuple-element.58), channel_id=1, source_target_pairs={{0,28},{2,30},{4,0},{6,2},{8,4},{10,6},{12,8},{14,10},{16,12},{18,... | collective-permute-start | bytes 1474568 | tf_op jit(solution)/shard_map/ppermute | solution.py:444
  378.5 25.2 %collective-permute-start.1 = (bf16[480,512]{1,0:T(8,128)(2,1)}, bf16[480,512]{1,0:T(8,128)(2,1)}, u32[]{:S(2)}, u32[]{:S(2)}) collective-permute-start(bf16[480,512]{1,0:T(8,128)(2,1)} %get-tuple-element.59), channel_id=1, source_target_pairs={{0,26},{2,28},{4,30},{6,0},{8,2},{10,4},{12,6},{14,8},{16,10},{18,... | collective-permute-start | bytes 1474568 | tf_op jit(solution)/shard_map/ppermute | solution.py:444
  378.6 4.7 %copy-start.5 = (bf16[512,512]{1,0:T(8,128)(2,1)S(1)}, bf16[512,512]{1,0:T(8,128)(2,1)}, u32[]{:S(2)}) copy-start(bf16[512,512]{1,0:T(8,128)(2,1)} %get-tuple-element.20) | copy-start | bytes 1572868
  386.0 17.7 %copy-start.1 = (f32[480,512]{1,0:T(8,128)S(1)}, f32[480,512]{1,0:T(8,128)}, u32[]{:S(2)}) copy-start(f32[480,512]{1,0:T(8,128)} %get-tuple-element.22) | copy-start | bytes 2949124
  386.0 17.7 %copy-start.4 = (bf16[480,512]{1,0:T(8,128)(2,1)S(1)}, bf16[480,512]{1,0:T(8,128)(2,1)}, u32[]{:S(2)}) copy-start(bf16[480,512]{1,0:T(8,128)(2,1)} %copy-done.3) | copy-start | bytes 1474564
  390.7 15.8 %copy-start.2 = (f32[480,512]{1,0:T(8,128)S(1)}, f32[480,512]{1,0:T(8,128)}, u32[]{:S(2)}) copy-start(f32[480,512]{1,0:T(8,128)} %get-tuple-element.21) | copy-start | bytes 2949124

commit v2 on v1

--- a/solution.py
+++ b/solution.py
@@ -25,8 +25,10 @@
 FF_BLOCK = 512
 NEGATIVE = -1e30
 EPSILON = 1e-5
-CHUNKS = 6
-CHUNK_ROWS = 1024
+GRAD_ROWS = 2 * FF + 4 * D
+SUMS = 16
+SHARD = 16
+STAGES = 8
 
 BF16 = jnp.bfloat16
 F32 = jnp.float32
@@ -150,7 +152,6 @@
     block_output,
     residual_grad,
     grads,
-    sums_up,
     sums,
     parts,
     own_part,
@@ -283,14 +284,15 @@
         density = jnp.exp(-0.5 * before * before) * 0.3989422804014327
         activated = (before * chance).astype(BF16)
         slope = chance + before * density
-        grads[pl.ds(pl.multiple_of(FF + c * FF_BLOCK, FF_BLOCK), FF_BLOCK), :] = dot(
+        grads[columns, :] = dot(
             activated, branch_grad[...], TN
         ).astype(BF16)
         branch[...] += dot(activated, w_down[columns, :], NN)
         before_full = dot(branch_grad[...], w_down[columns, :], NT) * slope
         before_grad = before_full.astype(BF16)
-        sums_up[:, columns] = jnp.sum(before_grad.astype(F32), 0, keepdims=True)
-        grads[columns, :] = dot(normed_mlp[...], before_grad, TN).astype(BF16)
+        sums[pl.ds(c, 1), :] = jnp.sum(before_grad.astype(F32), 0, keepdims=True)
+        up_rows = pl.ds(pl.multiple_of(FF + c * FF_BLOCK, FF_BLOCK), FF_BLOCK)
+        grads[up_rows, :] = dot(normed_mlp[...], before_grad, TN).astype(BF16)
         mlp_back[...] += dot(before_grad, w_up[:, columns], NT)
         return 0
 
@@ -301,9 +303,9 @@
     block_output[USED:, :] = jnp.zeros((ROWS - USED, D), BF16)
     unit_m, scale_m = normalise(residual_grad[...])
     back = mlp_back[...]
-    sums[0:1, :] = jnp.sum(branch_grad[...].astype(F32), 0, keepdims=True)
-    sums[1:2, :] = jnp.sum(back * unit_m, 0, keepdims=True)
-    sums[2:3, :] = jnp.sum(back, 0, keepdims=True)
+    sums[4:5, :] = jnp.sum(branch_grad[...].astype(F32), 0, keepdims=True)
+    sums[5:6, :] = jnp.sum(back * unit_m, 0, keepdims=True)
+    sums[6:7, :] = jnp.sum(back, 0, keepdims=True)
     res_grad = upstream + norm_backward(back, unit_m, scale_m, gain_m)
     residual_grad[...] = res_grad
     attended_grad = (live * res_grad).astype(BF16)
@@ -353,7 +355,7 @@
         rows = slice(c * D, (c + 1) * D)
         grads[base + D + c * D : base + 2 * D + c * D, :] = dot(
             keyval_grad[rows, :], normed_all[...], NN
-        ).astype(BF16)
+        ).T.astype(BF16)
     from_query = dot(query_grad[...], w_query[...], NT)
     normed = query_norm[...].astype(F32)
     shift_sum = jnp.sum(from_query, 0, keepdims=True)
@@ -374,19 +376,18 @@
             for i in range(1, VIEWS):
                 holds = lax.rem(my_view + i, VIEWS) == 0
                 parts[i - 1, PATCHES:, :] = jnp.where(holds, piece, 0.0).astype(BF16)
-    sums[3:4, :] = (gain_sum - shift_a * shift_sum) / gain_a
-    sums[4:5, :] = shift_sum
-    sums[5:8, :] = jnp.zeros((3, D), F32)
-
-
-def compute(*args):
+    sums[7:8, :] = (gain_sum - shift_a * shift_sum) / gain_a
+    sums[8:9, :] = shift_sum
+    sums[9:, :] = jnp.zeros((SUMS - 9, D), F32)
+
+
+def compute(grad_rows, *args):
     shape = jax.ShapeDtypeStruct
     outs = (
         shape((ROWS, D), BF16),
         shape((USED, D), F32),
-        shape((CHUNKS * CHUNK_ROWS, D), BF16),
-        shape((1, FF), F32),
-        shape((8, D), F32),
+        shape((grad_rows, D), BF16),
+        shape((SUMS, D), F32),
         shape((VIEWS - 1, USED, D), BF16),
         shape((USED, D), F32),
     )
@@ -420,7 +421,363 @@
     )(*args)
 
 
-def on_device(count, tokens, counts, slot_item, slot_view, keyframe, *rest):
+def reduce_kernel(
+    count,
+    groups,
+    chunks,
+    view,
+    parts,
+    own_part,
+    residual_grad,
+    tokens,
+    cotangent,
+    gain_attn,
+    grads,
+    sums,
+    grad_tokens,
+    summed,
+    sums_out,
+    acc,
+    arrived_core,
+    arrived_first,
+    arrived_second,
+    arrived_last,
+    send_sem,
+    recv_sem,
+    local_sem,
+    sums_at,
+    sums_send,
+    sums_recv,
+    swap_out,
+    swap_in,
+    far_out,
+    far_in,
+    swap_sem,
+    far_sem,
+):
+    me = lax.axis_index("view")
+    group = lax.axis_index("dp")
+    depth = count // 4
+    core = lax.rem(me, 2)
+    place = {"x": lax.rem(me // 2, 2), "y": group, "z": me // 4}
+    size = {"x": 2, "y": groups, "z": depth}
+    half = 2 * 2 * groups * depth * SHARD
+    orders = (("x", "y", "z"), ("y", "x", "z"))
+    arrived = (arrived_first, arrived_second, arrived_last)
+    step = 1 - 2 * core
+
+    def peer(dim, j):
+        at = lax.rem(place[dim] + j, size[dim])
+        if dim == "x":
+            return {"view": me + 2 * (at - place["x"])}
+        if dim == "y":
+            return {"dp": at}
+        return {"view": me + 4 * (at - place["z"])}
+
+    def along(offset):
+        return {"view": lax.rem(me + offset + count, count)}
+
+    sibling = {"view": me + step}
+    peers = [peer(dim, j) for dim in "xyz" for j in range(1, size[dim])]
+    greet([sibling] + peers + [along(offset) for offset in (4, -4, 2, -2)])
+
+    levels = []
+    for order in orders:
+        rows = half // 2
+        offset = 0
+        level = [(0, rows)]
+        for dim in order:
+            rows = rows // size[dim]
+            offset = offset + place[dim] * rows
+            level.append((offset, rows))
+        levels.append(level)
+
+    def copies(stage, k):
+        out = []
+
+        def add(source, target, device):
+            n = len(out)
+            out.append(
+                pltpu.make_async_remote_copy(
+                    source, target, send_sem.at[k, stage, n], recv_sem.at[k, stage, n], device, MESH
+                )
+            )
+
+        for p, order in enumerate(orders):
+            base = k * 2 * half + p * half
+
+            def whole(offset, rows):
+                return summed.at[pl.ds(pl.multiple_of(base + core * (half // 2) + offset, SHARD), rows)]
+
+            if stage == 0:
+                start = pl.multiple_of(base + (1 - core) * (half // 2), SHARD)
+                add(grads.at[pl.ds(start, half // 2)], arrived_core.at[k, p], sibling)
+            elif stage < 4:
+                dim = order[stage - 1]
+                offset, _ = levels[p][stage - 1]
+                _, rows = levels[p][stage]
+                for j in range(1, size[dim]):
+                    at = lax.rem(place[dim] + j, size[dim])
+                    start = pl.multiple_of(offset + at * rows, SHARD)
+                    if p == 0 or stage == 3:
+                        slot = p * (size[dim] - 1) + j - 1 if stage == 3 else j - 1
+                    else:
+                        slot = size["x" if stage == 1 else "y"] - 1 + j - 1
+                    add(
+                        acc.at[k, p, pl.ds(start, rows)],
+                        arrived[stage - 1].at[k, slot, pl.ds(0, rows)],
+                        peer(dim, j),
+                    )
+            elif stage < 7:
+                dim = order[6 - stage]
+                offset, rows = levels[p][7 - stage]
+                target = whole(offset, rows)
+                if stage == 4:
+                    source = acc.at[k, p, pl.ds(pl.multiple_of(offset, SHARD), rows)]
+                else:
+                    source = target
+                for j in range(1, size[dim]):
+                    add(source, target, peer(dim, j))
+            else:
+                target = whole(0, half // 2)
+                add(target, target, sibling)
+        return out
+
+    def own_shard(k, p):
+        offset, rows = levels[p][3]
+        start = k * 2 * half + p * half + core * (half // 2) + offset
+        return pltpu.make_async_copy(
+            acc.at[k, p, pl.ds(pl.multiple_of(offset, SHARD), rows)],
+            summed.at[pl.ds(pl.multiple_of(start, SHARD), rows)],
+            local_sem.at[k, p],
+        )
+
+    def start_stage(stage, k):
+        for copy in copies(stage, k):
+            copy.start()
+        if stage == 4:
+            for p in range(2):
+                own_shard(k, p).start()
+
+    def finish_stage(stage, k):
+        for copy in copies(stage, k):
+            copy.wait()
+        if stage == 4:
+            for p in range(2):
+                own_shard(k, p).wait()
+        for p, order in enumerate(orders):
+            if stage == 0:
+                start = pl.multiple_of(k * 2 * half + p * half + core * (half // 2), SHARD)
+                mine = grads[pl.ds(start, half // 2), :].astype(F32)
+                acc[k, p] = (mine + arrived_core[k, p].astype(F32)).astype(BF16)
+            elif stage < 4:
+                dim = order[stage - 1]
+                offset, rows = levels[p][stage]
+                at = pl.ds(pl.multiple_of(offset, SHARD), rows)
+                total = acc[k, p, at, :].astype(F32)
+                for j in range(1, size[dim]):
+                    if p == 0 or stage == 3:
+                        slot = p * (size[dim] - 1) + j - 1 if stage == 3 else j - 1
+                    else:
+                        slot = size["x" if stage == 1 else "y"] - 1 + j - 1
+                    total += arrived[stage - 1][k, slot, :rows, :].astype(F32)
+                acc[k, p, at, :] = total.astype(BF16)
+
+    def tick(t, _):
+        for stage in range(STAGES, -1, -1):
+            k = t - stage
+
+            def go():
+                if stage > 0:
+                    finish_stage(stage - 1, k)
+                if stage < STAGES:
+                    start_stage(stage, k)
+
+            pl.when(jnp.logical_and(k >= 0, k < chunks))(go)
+        return 0
+
+    sums_dims = ("core", "x", "y", "z")
+
+    def sums_copies(level):
+        dim = sums_dims[level]
+        if dim == "core":
+            targets = [(sibling, 2, core)]
+        else:
+            targets = [(peer(dim, j), size[dim], place[dim]) for j in range(1, size[dim])]
+        return [
+            pltpu.make_async_remote_copy(
+                sums_at.at[level, mine],
+                sums_at.at[level, mine],
+                sums_send.at[level, n],
+                sums_recv.at[level, n],
+                device,
+                MESH,
+            )
+            for n, (device, _, mine) in enumerate(targets)
+        ]
+
+    def sums_start(level, value):
+        dim = sums_dims[level]
+        sums_at[level, core if dim == "core" else place[dim]] = value
+        for copy in sums_copies(level):
+            copy.start()
+
+    def sums_finish(level):
+        for copy in sums_copies(level):
+            copy.wait()
+        dim = sums_dims[level]
+        total = sums_at[level, 0]
+        for i in range(1, 2 if dim == "core" else size[dim]):
+            total += sums_at[level, i]
+        return total
+
+    my_view = view[0]
+
+    def part_for(offset):
+        slot = lax.rem(offset + VIEWS, VIEWS) - 1
+        at = my_view + offset
+        valid = jnp.logical_and(at >= 0, at < VIEWS)
+        return jnp.where(valid, parts[slot], jnp.zeros((), BF16))
+
+    def swap(n):
+        return pltpu.make_async_remote_copy(
+            swap_out.at[n], swap_in.at[n], swap_sem.at[0, n], swap_sem.at[1, n], sibling, MESH
+        )
+
+    far = (2 + 0 * step, -2 + 0 * step, 4 * step, -4 * step)
+
+    def far_copy(n):
+        return pltpu.make_async_remote_copy(
+            far_out.at[n], far_in.at[n], far_sem.at[0, n], far_sem.at[1, n], along(far[n]), MESH
+        )
+
+    sums_start(0, sums[...])
+    for n, offset in enumerate((step, 2 + step, -2 + step, -3 * step)):
+        swap_out[n] = part_for(offset)
+        swap(n).start()
+    lax.fori_loop(0, 1, tick, 0)
+    far_out[3] = part_for(far[3])
+    far_copy(3).start()
+    sums_start(1, sums_finish(0))
+    for n in range(3):
+        swap(n + 1).wait()
+        far_out[n] = (part_for(far[n]).astype(F32) + swap_in[n + 1].astype(F32)).astype(BF16)
+        far_copy(n).start()
+    lax.fori_loop(1, 2, tick, 0)
+    sums_start(2, sums_finish(1))
+    lax.fori_loop(2, 3, tick, 0)
+    sums_start(3, sums_finish(2))
+    lax.fori_loop(3, chunks + STAGES, tick, 0)
+    sums_out[...] = sums_finish(3)
+    swap(0).wait()
+    for n in range(4):
+        far_copy(n).wait()
+    total = own_part[...] + swap_in[0].astype(F32)
+    for n in range(4):
+        total += far_in[n].astype(F32)
+    unit, scale = normalise(tokens[:USED, :].astype(F32))
+    gain = gain_attn[...].astype(F32)
+    grad_tokens[:USED, :] = residual_grad[...] + norm_backward(total, unit, scale, gain)
+    grad_tokens[USED:, :] = cotangent[USED:, :].astype(F32)
+
+
+def reduce(count, groups, *args):
+    depth = count // 4
+    half = 2 * 2 * groups * depth * SHARD
+    chunks = -(-GRAD_ROWS // (2 * half))
+    shape = jax.ShapeDtypeStruct
+    dma = pltpu.SemaphoreType.DMA
+    most = 2 * max(groups, depth)
+    levels = max(groups, depth)
+    first = max(half // 4, half // 2 // groups)
+    scratch = [
+        VMEM((chunks, 2, half // 2, D), BF16),
+        VMEM((chunks, 2, half // 2, D), BF16),
+        VMEM((chunks, groups, first, D), BF16),
+        VMEM((chunks, groups, half // 4 // groups, D), BF16),
+        VMEM((chunks, 2 * (depth - 1), SHARD, D), BF16),
+        dma((chunks, STAGES, most)),
+        dma((chunks, STAGES, most)),
+        dma((chunks, 2)),
+        VMEM((4, levels, SUMS, D), F32),
+        dma((4, levels)),
+        dma((4, levels)),
+        VMEM((4, USED, D), BF16),
+        VMEM((4, USED, D), BF16),
+        VMEM((4, USED, D), BF16),
+        VMEM((4, USED, D), BF16),
+        dma((2, 4)),
+        dma((2, 4)),
+    ]
+    return pl.pallas_call(
+        functools.partial(reduce_kernel, count, groups, chunks),
+        out_shape=(
+            shape((ROWS, D), F32),
+            shape((chunks * 2 * half, D), BF16),
+            shape((SUMS, D), F32),
+        ),
+        in_specs=[IN_SMEM] + [IN_VMEM] * (len(args) - 1),
+        out_specs=[IN_VMEM, ANYWHERE, IN_VMEM],
+        scratch_shapes=scratch,
+        compiler_params=pltpu.CompilerParams(
+            collective_id=1, has_side_effects=True, vmem_limit_bytes=60 * MIB
+        ),
+        name="reduce",
+    )(*args)
+
+
+def widen_kernel(block, down, up, out, query, keyval):
+    b = pl.program_id(0)
+    value = block[...].astype(F32)
+    blocks = FF // D
+    for target, first, last in (
+        (down, 0, blocks),
+        (up, blocks, 2 * blocks),
+        (out, 2 * blocks, 2 * blocks + 1),
+        (query, 2 * blocks + 1, 2 * blocks + 2),
+        (keyval, 2 * blocks + 2, 2 * blocks + 4),
+    ):
+
+        def store(target=target):
+            target[...] = value
+
+        pl.when(jnp.logical_and(b >= first, b < last))(store)
+
+
+def widen(summed):
+    blocks = FF // D
+    shape = jax.ShapeDtypeStruct
+
+    def at(first, number, by_rows):
+        def index(b):
+            i = jnp.clip(b - first, 0, number - 1)
+            return (i, 0) if by_rows else (0, i)
+
+        return pl.BlockSpec((D, D), index)
+
+    return pl.pallas_call(
+        widen_kernel,
+        grid=(GRAD_ROWS // D,),
+        out_shape=(
+            shape((FF, D), F32),
+            shape((D, FF), F32),
+            shape((D, D), F32),
+            shape((D, D), F32),
+            shape((D, 2 * D), F32),
+        ),
+        in_specs=[pl.BlockSpec((D, D), lambda b: (b, 0))],
+        out_specs=[
+            at(0, blocks, True),
+            at(blocks, blocks, False),
+            at(2 * blocks, 1, True),
+            at(2 * blocks + 1, 1, True),
+            at(2 * blocks + 2, 2, False),
+        ],
+        name="widen",
+    )(summed)
+
+
+def on_device(count, groups, tokens, counts, slot_item, slot_view, keyframe, *rest):
     weights, cotangent = rest[:-1], rest[-1]
     rows = tokens.reshape(ROWS, D)
     item = slot_item.reshape(())
@@ -430,48 +787,43 @@
     window = gather_window(block, count)
     weights = tuple(w.reshape(1, -1) if w.ndim == 1 else w for w in weights)
     cot = cotangent.reshape(ROWS, D)
-    block_output, residual_grad, grads, sums_up, sums, parts, own_part = compute(
-        slot_view.reshape(1), filled.astype(jnp.int32).reshape(1), window, cot, *weights
+    view = slot_view.reshape(1)
+    chunk = 2 * count * groups * SHARD
+    grad_rows = -(-GRAD_ROWS // chunk) * chunk
+    block_output, residual_grad, grads, sums, parts, own_part = compute(
+        grad_rows, view, filled.astype(jnp.int32).reshape(1), window, cot, *weights
     )
     block_output = jnp.concatenate([block_output[:USED], rows[USED:]])
-    view = slot_view.reshape(())
-    total = own_part
-    for offset in range(1 - VIEWS, VIEWS):
-        if offset != 0:
-            valid = (view + offset >= 0) & (view + offset < VIEWS)
-            sent = jnp.where(valid, parts[(offset + VIEWS) % VIEWS - 1], 0)
-            pairs = [(source, (source + offset) % count) for source in range(count)]
-            total = total + lax.ppermute(sent, "view", pairs).astype(F32)
-    gain = rest[7].astype(F32)
-    unit, scale = normalise(rows[:USED].astype(F32))
-    used = residual_grad + norm_backward(total, unit, scale, gain)
-    grad_tokens = jnp.concatenate([used, cot[USED:].astype(F32)])
-    grads, sums_up, sums = lax.psum((grads.astype(F32), sums_up, sums), ("view", "dp"))
+    grad_tokens, summed, sums = reduce(
+        count, groups, view, parts, own_part, residual_grad, rows, cot, weights[7], grads, sums
+    )
+    down, up, out, query, keyval = widen(summed)
     return (
         block_output.reshape(tokens.shape),
         grad_tokens.reshape(tokens.shape),
-        grads[2 * FF + D : 2 * FF + 2 * D],
-        grads[2 * FF + 2 * D :].T,
-        grads[2 * FF : 2 * FF + D],
-        jnp.concatenate([grads[c * D : (c + 1) * D] for c in range(FF // D)], 1),
-        sums_up.reshape(-1),
-        grads[FF : 2 * FF],
-        sums[0],
-        sums[3],
+        query,
+        keyval,
+        out,
+        up,
+        sums[:4].reshape(-1),
+        down,
         sums[4],
-        sums[1],
-        sums[2],
+        sums[7],
+        sums[8],
+        sums[5],
+        sums[6],
     )
 
 
 def solution(mesh):
     count = mesh.shape["view"]
+    groups = mesh.shape["dp"]
     slots = P("dp", "view", None)
     rows = P("dp", "view", None, None, None)
     in_specs = (rows, P("dp", "view"), slots, slots, slots) + (P(),) * 11 + (rows,)
     out_specs = (rows, rows) + (P(),) * 11
     return jax.shard_map(
-        functools.partial(on_device, count),
+        functools.partial(on_device, count, groups),
         mesh=mesh,
         in_specs=in_specs,
         out_specs=out_specs,

time: 409 us -> 242 us (0.59)
  blocking collectives: 240 us -> 0 us
  Pallas kernels: 104 us -> 222 us
  other arithmetic: 14.5 us -> 0.83 us
  waiting for transfers between devices: 13 us -> 0 us
  starting transfers between devices: 9.18 us -> 0 us
  local copies, waits for them, and re-layouts: 24 us -> 15.2 us
    psum x1 -> x0, blocking collectives: 240 us -> none  [on_device(): lax.psum((grads.astype(F32), sums_up, sums), ('view', 'dp'))]
    pallas_call x0 -> x2, Pallas kernels: none -> 118 us  [the longest x1 106 us: reduce(): pl.pallas_call(functools.partial(reduce_kernel, count, groups, chunks), o...]
    ppermute x8 -> x0, waiting for transfers between devices: 13 us -> none  [on_device(): total = total + lax.ppermute(sent, 'view', pairs).astype(F32)]
    slice x3 -> x1, local copies, waits for them, and re-layouts: 10.8 us -> 1.53 us  [on_device(): sums[6]]
    ppermute x8 -> x0, starting transfers between devices: 9.18 us -> none  [on_device(): total = total + lax.ppermute(sent, 'view', pairs).astype(F32)]
    concatenate x1 -> x0, other arithmetic: 4.73 us -> none  [on_device(): jnp.concatenate([grads[c * D:(c + 1) * D] for c in range(FF // D)], 1)]
  transfers between devices with their start and end apart: 8 -> 0, of which waited for: 2 -> 0; matrix products, arithmetic and copies ran while one was open for 5% -> 0% of each run, Pallas kernels for 0% -> 0%
where the time goes in v2:
time: 242 us; the launch traced here: 241 us
  Pallas kernels  222 us (92%)
  local copies, waits for them, and re-layouts  15.2 us (6%)
  between operations  3.29 us (1%)
    pallas_call x1, Pallas kernels, reduce(): pl.pallas_call(functools.partial(reduce_kernel, count, groups, chunks), o...  106 us
    pallas_call x1, Pallas kernels, compute(): pl.pallas_call(compute_kernel, out_shape=outs, in_specs=[IN_SMEM] * 2 + [...  60.1 us
    pallas_call x1, Pallas kernels, gather_window(): pl.pallas_call(functools.partial(gather_kernel, count), out_shape=jax.Sha...  43.8 us
    pallas_call x1, Pallas kernels, widen(): pl.pallas_call(widen_kernel, grid=(GRAD_ROWS // D,), out_shape=(shape((FF...  11.9 us
    reshape x6, local copies, waits for them, and re-layouts, on_device(): weights = tuple((w.reshape(1, -1) if w.ndim == 1 else w for w in weights))  7.58 us

profile of v2, /device:TPU:0, one launch (start us, length us, event | category | flops | bytes accessed | tf_op | source)
XLA Modules:
  0.0 241.2 jit_solution(11900499012131894259)
XLA Ops:
  3.2 1.3 reshape.85.gain_attn
  4.5 1.3 reshape.84.bias_down
  5.8 1.3 reshape.86.shift_attn
  7.0 1.3 reshape.87.gain_mlp
  8.3 1.3 reshape.88.shift_mlp
  9.5 1.3 reshape.83.bias_up
  10.8 0.8 slice_bitcast_fusion.1
  11.6 1.1 slice_bitcast_fusion
  12.7 0.8 concatenate.6.block
  13.5 43.8 %gather_window.1.window = bf16[9,496,512]{2,1,0:T(8,128)(2,1)} custom-call(bf16[496,512]{1,0:T(8,128)(2,1)} %concatenate.6.block), custom_call_target="tpu_custom_call" | custom-call | tf_op jit(solution)/shard_map/gather_window/pallas_call | solution.py:125
  57.3 60.1 %compute.1 = (bf16[512,512]{1,0:T(8,128)(2,1)}, f32[480,512]{1,0:T(8,128)}, bf16[6144,512]{1,0:T(8,128)(2,1)}, f32[16,512]{1,0:T(8,128)}, bf16[4,480,512]{2,1,0:T(8,128)(2,1)}, /*index=5*/f32[480,512]{1,0:T(8,128)}) custom-call(s32[1]{0:T(128)} %bitcast.24.view, s32[1]{0:T(128)} %bitcast.4.filled, bf16[9,496,512]{2,1,0:T(8,128)(2,1)} %gather_window.1.window, ...), custom_call_target="tpu_custom_call" | custom-call | tf_op jit(solution)/shard_map/compute/pallas_call | solution.py:413
  117.4 1.1 slice.35
  118.4 0.8 maximum_bitcast_fusion
  119.3 106.2 %reduce.1 = (f32[512,512]{1,0:T(8,128)}, bf16[6144,512]{1,0:T(8,128)(2,1)}, f32[16,512]{1,0:T(8,128)}) custom-call(s32[1]{0:T(128)} %bitcast.25.view, bf16[4,480,512]{2,1,0:T(8,128)(2,1)} %get-tuple-element.28.parts, f32[480,512]{1,0:T(8,128)} %get-tuple-element.29.own_part, f32[480,512]{1,0:T(8,128)} %get-tuple-element.30.residual_grad, ...), custom_call_target="tpu_custom_call" | custom-call | tf_op jit(solution)/shard_map/reduce/pallas_call | solution.py:712
  225.4 0.0 copy-start
  225.5 0.8 slice_bitcast_fusion.2
  226.3 1.5 fusion
  227.8 0.6 copy.30
  228.4 11.9 %widen.1 = (f32[2048,512]{1,0:T(8,128)}, f32[512,2048]{1,0:T(8,128)}, f32[512,512]{1,0:T(8,128)}, f32[512,512]{1,0:T(8,128)}, f32[512,1024]{1,0:T(8,128)}) custom-call(bf16[6144,512]{1,0:T(8,128)(2,1)} %get-tuple-element.34.block), custom_call_target="tpu_custom_call" | custom-call | tf_op jit(solution)/shard_map/widen/pallas_call | solution.py:758
  240.3 0.0 copy-done
  240.3 1.0 copy.36
Async XLA Ops:
  225.4 14.8 %copy-start = (f32[512,512]{1,0:T(8,128)S(1)}, f32[512,512]{1,0:T(8,128)}, u32[]{:S(2)}) copy-start(f32[512,512]{1,0:T(8,128)} %get-tuple-element.33) | copy-start | bytes 3145732

commit v3 on v1

v3 whole, which is shorter than its diff:
```python
import functools

import jax
import jax.numpy as jnp
from jax import lax
from jax.experimental import pallas as pl
from jax.experimental.pallas import tpu as pltpu
from jax.sharding import PartitionSpec as P

D = 512
HEADS = 8
HEAD_DIM = 64
PAIRS = HEADS // 2
PAIR = 2 * HEAD_DIM
VIEWS = 5
PATCHES = 400
LANG = 77
ROWS = 512
USED = 480
TAIL = USED - PATCHES
SENT = 496
KEYS = VIEWS * PATCHES + TAIL
KEYS_PADDED = 2176
FF = 2048
FF_BLOCK = 512
NEGATIVE = -1e30
EPSILON = 1e-5
GRAD_ROWS = 2 * FF + 4 * D
SUMS = 16
SHARD = 16
STAGES = 8
SKEW = 2

BF16 = jnp.bfloat16
F32 = jnp.float32
MESH = pl.DeviceIdType.MESH
NN = (((1,), (0,)), ((), ()))
NT = (((1,), (1,)), ((), ()))
TN = (((0,), (0,)), ((), ()))
TT = (((0,), (1,)), ((), ()))
MIB = 2**20

VMEM = pltpu.VMEM
IN_VMEM = pl.BlockSpec(memory_space=pltpu.VMEM)
IN_SMEM = pl.BlockSpec(memory_space=pltpu.SMEM)
ANYWHERE = pl.BlockSpec(memory_space=pl.ANY)


def dot(left, right, dims):
    return lax.dot_general(left, right, dims, preferred_element_type=F32)


def normalise(values):
    average = jnp.mean(values, -1, keepdims=True)
    centered = values - average
    variance = jnp.mean(centered * centered, -1, keepdims=True)
    scale = lax.rsqrt(variance + EPSILON)
    return centered * scale, scale


def norm_backward(grad, unit, scale, gain):
    grad = grad * gain
    first = jnp.mean(grad, -1, keepdims=True)
    second = jnp.mean(grad * unit, -1, keepdims=True)
    return scale * (grad - first - unit * second)


def greet(others):
    barrier = pltpu.get_barrier_semaphore()
    for other in others:
        pl.semaphore_signal(barrier, inc=1, device_id=other, device_id_type=MESH)
    pl.semaphore_wait(barrier, len(others))


def gather_kernel(count, block, window, own_sem, send_sem, recv_sem, pass_sem, given_sem):
    me = lax.axis_index("view")
    step = 1 - 2 * lax.rem(me, 2)

    def at(offset):
        return {"view": lax.rem(me + offset + count, count)}

    far = (4, -4, 2, -2)
    greet([at(offset) for offset in far] + [at(step)])
    own = pltpu.make_async_copy(block, window.at[4], own_sem)
    own.start()

    def to(k, offset):
        return pltpu.make_async_remote_copy(
            block, window.at[4 - offset], send_sem.at[k], recv_sem.at[k], at(offset), MESH
        )

    def across(k, offset, source):
        return pltpu.make_async_remote_copy(
            source,
            window.at[4 + offset - step],
            pass_sem.at[k],
            given_sem.at[k],
            at(step),
            MESH,
        )

    sends = [to(k, offset) for k, offset in enumerate(far)]
    for copy in sends:
        copy.start()
    passes = [across(0, 0, block)]
    passes[0].start()
    for k, offset in ((2, -2), (3, 2)):
        sends[k].wait_recv()
        copy = across(k - 1, offset, window.at[4 + offset])
        copy.start()
        passes.append(copy)
    even = lax.rem(me, 2) == 0
    for k in (0, 1):
        sends[k].wait_recv()
    copy = across(3, 4 * step, window.at[4 + 4 * step])
    copy.start()
    passes.append(copy)
    for copy in passes:
        copy.wait()
    for copy in sends:
        copy.wait_send()
    own.wait()


def gather_window(block, count):
    return pl.pallas_call(
        functools.partial(gather_kernel, count),
        out_shape=jax.ShapeDtypeStruct((2 * VIEWS - 1, SENT, D), BF16),
        in_specs=[ANYWHERE],
        out_specs=ANYWHERE,
        scratch_shapes=[pltpu.SemaphoreType.DMA] + [pltpu.SemaphoreType.DMA((4,))] * 4,
        compiler_params=pltpu.CompilerParams(collective_id=0, has_side_effects=True),
        name="gather_window",
    )(block)


def main_kernel(
    count,
    groups,
    chunks,
    part_rows,
    view,
    filled,
    window,
    tokens,
    cotangent,
    w_query,
    w_keyval,
    w_output,
    w_up,
    w_down,
    vectors,
    block_output,
    grad_tokens,
    summed,
    sums_out,
    spilled,
    normed_all,
    query_norm,
    key_bias,
    keyval,
    query,
    weights,
    mixed,
    mixed_full,
    inverse,
    keyval_grad,
    mixed_grad,
    normed_mlp,
    branch_grad,
    residual,
    branch,
    mlp_back,
    labels,
    arena,
    grads,
    arrived_core,
    arrived_first,
    arrived_second,
    arrived_last,
    far_in,
    sums_at,
    window_sem,
    weight_sem,
    spill_sem,
    send_sem,
    recv_sem,
    local_sem,
    sums_send,
    sums_recv,
    swap_sem,
    far_sem,
):
    me = lax.axis_index("view")
    group = lax.axis_index("dp")
    depth = count // 4
    core = lax.rem(me, 2)
    step = 1 - 2 * core
    place = {"x": lax.rem(me // 2, 2), "y": group, "z": me // 4}
    size = {"x": 2, "y": groups, "z": depth}
    orders = (("x", "y", "z"), ("y", "x", "z"))[-(2 if part_rows < D else 1) :]
    chunk_rows = len(orders) * part_rows
    fine = chunk_rows == D
    arrived = (arrived_first, arrived_second, arrived_last)

    def peer(dim, j):
        at = lax.rem(place[dim] + j, size[dim])
        if dim == "x":
            return {"view": me + 2 * (at - place["x"])}
        if dim == "y":
            return {"dp": at}
        return {"view": me + 4 * (at - place["z"])}

    def along(offset):
        return {"view": lax.rem(me + offset + count, count)}

    sibling = {"view": me + step}

    def window_at(n):
        return weights.at[n // 4, :, pl.ds(n % 4 * D, D)]

    def window_copies(n):
        return (
            pltpu.make_async_copy(
                window.at[n, pl.ds(0, USED), :], window_at(n), window_sem.at[0, n]
            ),
            pltpu.make_async_copy(
                window.at[n, pl.ds(USED, SENT - USED), :], labels.at[n], window_sem.at[1, n]
            ),
        )

    def weight_copies():
        blocks = FF // D
        return [
            pltpu.make_async_copy(
                w_up.at[:, pl.ds(c * D, D)], arena.at[c], weight_sem.at[c]
            )
            for c in range(blocks)
        ] + [
            pltpu.make_async_copy(
                w_down.at[pl.ds(c * D, D), :], arena.at[blocks + c], weight_sem.at[blocks + c]
            )
            for c in range(blocks)
        ]

    for n in range(2 * VIEWS - 1):
        for copy in window_copies(n):
            copy.start()
    for copy in weight_copies():
        copy.start()
    peers = [peer(dim, j) for dim in "xyz" for j in range(1, size[dim])]
    greet([sibling] + peers + [along(offset) for offset in (4, -4, 2, -2)])

    levels = []
    for order in orders:
        rows = part_rows
        offset = 0
        level = [(0, rows)]
        for dim in order:
            rows = rows // size[dim]
            offset = offset + place[dim] * rows
            level.append((offset, rows))
        levels.append(level)
    own_columns = pl.ds(pl.multiple_of(core * (D // 2), D // 2), D // 2)
    other_columns = pl.ds(pl.multiple_of((1 - core) * (D // 2), D // 2), D // 2)

    def slot_of(stage, p, j):
        slot = j - 1
        for order in orders[:p]:
            slot += size[order[stage - 1]] - 1
        return slot

    def rows_of(k, p, offset, rows):
        return pl.ds(pl.multiple_of(k * chunk_rows + p * part_rows + offset, SHARD), rows)

    def copies(stage, k):
        out = []

        def add(source, target, device):
            n = len(out)
            out.append(
                pltpu.make_async_remote_copy(
                    source, target, send_sem.at[k, stage, n], recv_sem.at[k, stage, n], device, MESH
                )
            )

        if stage == 0:
            add(grads.at[rows_of(k, 0, 0, chunk_rows), other_columns], arrived_core.at[k], sibling)
        elif stage == 7:
            whole = summed.at[rows_of(k, 0, 0, chunk_rows), own_columns]
            add(whole, whole, sibling)
        for p, order in enumerate(orders):
            if 0 < stage < 4:
                dim = order[stage - 1]
                offset, _ = levels[p][stage - 1]
                _, rows = levels[p][stage]
                for j in range(1, size[dim]):
                    at = offset + lax.rem(place[dim] + j, size[dim]) * rows
                    add(
                        grads.at[rows_of(k, p, at, rows), own_columns],
                        arrived[stage - 1].at[k, slot_of(stage, p, j), pl.ds(0, rows), :],
                        peer(dim, j),
                    )
            elif 4 <= stage < 7:
                dim = order[6 - stage]
                offset, rows = levels[p][7 - stage]
                at = rows_of(k, p, offset, rows)
                source = grads if stage == 4 else summed
                for j in range(1, size[dim]):
                    add(source.at[at, own_columns], summed.at[at, own_columns], peer(dim, j))
        return out

    def own_shard(k, p):
        at = rows_of(k, p, *levels[p][3])
        return pltpu.make_async_copy(
            grads.at[at, own_columns], summed.at[at, own_columns], local_sem.at[k, p]
        )

    def start_stage(stage, k):
        for copy in copies(stage, k):
            copy.start()
        if stage == 4:
            for p in range(len(orders)):
                own_shard(k, p).start()

    def finish_stage(stage, k):
        for copy in copies(stage, k):
            copy.wait()
        if stage == 4:
            for p in range(len(orders)):
                own_shard(k, p).wait()
        if stage == 0:
            at = rows_of(k, 0, 0, chunk_rows)
            total = grads[at, own_columns].astype(F32) + arrived_core[k].astype(F32)
            grads[at, own_columns] = total.astype(BF16)
        elif stage < 4:
            for p, order in enumerate(orders):
                offset, rows = levels[p][stage]
                at = rows_of(k, p, offset, rows)
                total = grads[at, own_columns].astype(F32)
                for j in range(1, size[order[stage - 1]]):
                    total += arrived[stage - 1][k, slot_of(stage, p, j), :rows, :].astype(F32)
                grads[at, own_columns] = total.astype(BF16)

    blocks = FF // D

    def tick(t):
        for stage in range(STAGES, -1, -1):
            at = t - SKEW * stage
            if fine:
                late = at - (2 * blocks + 1)
                early = jnp.logical_and(at >= 0, at < 2 * blocks)
                valid = jnp.logical_and(late >= 0, late < 2 * PAIRS)
                valid = jnp.logical_or(early, jnp.logical_and(valid, lax.rem(late, 2) == 0))
                k = jnp.where(early, at, 2 * blocks + late // 2)
            else:
                k = at
                valid = jnp.logical_and(at >= 0, at < chunks)

            def go(stage=stage, k=k):
                if stage > 0:
                    finish_stage(stage - 1, k)
                if stage < STAGES:
                    start_stage(stage, k)

            pl.when(valid)(go)

    sums_dims = ("core", "x", "y", "z")

    def sums_copies(level):
        dim = sums_dims[level]
        if dim == "core":
            targets, mine = [sibling], core
        else:
            targets, mine = [peer(dim, j) for j in range(1, size[dim])], place[dim]
        return [
            pltpu.make_async_remote_copy(
                sums_at.at[level, mine],
                sums_at.at[level, mine],
                sums_send.at[level, n],
                sums_recv.at[level, n],
                device,
                MESH,
            )
            for n, device in enumerate(targets)
        ]

    def sums_start(level, value):
        dim = sums_dims[level]
        sums_at[level, core if dim == "core" else place[dim]] = value
        for copy in sums_copies(level):
            copy.start()

    def sums_finish(level):
        for copy in sums_copies(level):
            copy.wait()
        dim = sums_dims[level]
        total = sums_at[level, 0]
        for i in range(1, 2 if dim == "core" else size[dim]):
            total += sums_at[level, i]
        return total

    my_view = view[0]
    my_filled = filled[0]
    gain_a = vectors[5:6, :]
    shift_a = vectors[6:7, :]
    gain_m = vectors[7:8, :]
    shift_m = vectors[8:9, :]

    own_rows = tokens[:USED, :]
    own_unit, _ = normalise(own_rows.astype(F32))
    own_normed = (own_unit * gain_a + shift_a).astype(BF16)
    query_norm[...] = own_normed
    normed_all[:PATCHES, :] = own_normed[:PATCHES, :]
    query[...] = (dot(own_normed, w_query[...], NN).astype(BF16) * HEAD_DIM**-0.5).astype(BF16)
    for n in range(2 * VIEWS - 1):
        for copy in window_copies(n):
            copy.wait()
    my_label = labels[VIEWS - 1, :, :PAIR].astype(F32)

    def bias_of(label):
        match = jnp.logical_and(label == my_label, label >= 0)
        return jnp.where(match, 0.0, NEGATIVE)[:1, :]

    def window_block(n, rows):
        return weights[n // 4, rows, n % 4 * D : (n % 4 + 1) * D]

    key_bias[:PATCHES, :] = jnp.broadcast_to(bias_of(my_label), (PATCHES, PAIR)).astype(BF16)
    language = own_rows[PATCHES:, :]
    language_bias = bias_of(my_label)
    for j in range(1, VIEWS):
        ahead = my_view + j < VIEWS
        block = jnp.where(
            ahead, window_block(4 + j, slice(0, USED)), window_block(j - 1, slice(0, USED))
        )
        label = jnp.where(ahead, labels[4 + j, :, :PAIR], labels[j - 1, :, :PAIR]).astype(F32)
        unit, _ = normalise(block[:PATCHES, :].astype(F32))
        rows = slice(j * PATCHES, (j + 1) * PATCHES)
        normed_all[rows, :] = (unit * gain_a + shift_a).astype(BF16)
        bias = bias_of(label)
        key_bias[rows, :] = jnp.broadcast_to(bias, (PATCHES, PAIR)).astype(BF16)
        holds = lax.rem(my_view + j, VIEWS) == 0
        language = jnp.where(holds, block[PATCHES:, :], language)
        language_bias = jnp.where(holds, bias, language_bias)
    unit, _ = normalise(language.astype(F32))
    normed_all[VIEWS * PATCHES : KEYS, :] = (unit * gain_a + shift_a).astype(BF16)
    index = lax.broadcasted_iota(jnp.int32, (TAIL, PAIR), 0)
    key_bias[VIEWS * PATCHES : KEYS, :] = jnp.where(
        index < LANG, jnp.broadcast_to(language_bias, (TAIL, PAIR)), NEGATIVE
    ).astype(BF16)
    normed_all[KEYS:, :] = jnp.zeros((KEYS_PADDED - KEYS, D), BF16)
    key_bias[KEYS:, :] = jnp.full((KEYS_PADDED - KEYS, PAIR), NEGATIVE, BF16)
    for c in range(2):
        columns = slice(c * D, (c + 1) * D)
        keyval[:, columns] = dot(normed_all[...], w_keyval[:, columns], NN).astype(BF16)

    lane = lax.broadcasted_iota(jnp.int32, (1, PAIR), 1)
    low_half = lane < HEAD_DIM

    def half_of(half, first, second):
        return jnp.where(low_half, first, second) if half == 0 else jnp.where(low_half, second, first)

    def head_keys(p, half):
        pair = keyval[:, pl.ds(pl.multiple_of(p * PAIR, PAIR), PAIR)]
        return half_of(half, pair, key_bias[...])

    def head_values(p, half):
        pair = keyval[:, pl.ds(pl.multiple_of(D + p * PAIR, PAIR), PAIR)]
        return half_of(half, pair, jnp.ones((), BF16))

    def spill(p, half):
        return pltpu.make_async_copy(
            weights.at[2 * lax.rem(p, 2) + half], spilled.at[2 * p + half], spill_sem.at[lax.rem(p, 2), half]
        )

    def unspill(p, half):
        return pltpu.make_async_copy(
            spilled.at[2 * p + half], weights.at[2 * lax.rem(p, 2) + half], spill_sem.at[lax.rem(p, 2), half]
        )

    def forward_pair(p, _):
        columns = pl.ds(pl.multiple_of(p * PAIR, PAIR), PAIR)
        pair = query[:, columns]
        outs = []
        totals = []

        def settle():
            for half in range(2):
                spill(p - 1, half).wait()

        pl.when(jnp.logical_and(p >= 1, p < 3))(settle)
        for half in range(2):
            one = (lane == HEAD_DIM * (1 - half)).astype(BF16)
            scores = dot(half_of(half, pair, one), head_keys(p, half), NT)
            top = jnp.max(scores, -1, keepdims=True)
            weight = jnp.exp(scores - top).astype(BF16)
            weights[2 * lax.rem(p, 2) + half] = weight
            out = dot(weight, head_values(p, half), NN)
            outs.append(out)
            totals.append(pltpu.roll(out, HEAD_DIM, 1))
        inv = 1.0 / jnp.where(low_half, totals[0], totals[1])
        full = jnp.where(low_half, outs[0], outs[1]) * inv
        inverse[:, columns] = inv
        mixed_full[:, columns] = full
        mixed[:, columns] = full.astype(BF16)

        def save():
            for half in range(2):
                spill(p, half).start()

        pl.when(p < 2)(save)
        return 0

    lax.fori_loop(0, PAIRS, forward_pair, 0)

    row = lax.broadcasted_iota(jnp.int32, (USED, PAIR), 0)
    has_language = (my_view == 0).astype(jnp.int32)
    live_rows = my_filled * (PATCHES + LANG * has_language)
    live = (row < live_rows).astype(F32)[:, :1]
    res = tokens[:USED, :].astype(F32) + live * dot(mixed[...], w_output[...], NN)
    residual[...] = res
    unit_m, scale_m = normalise(res)
    normed_mlp[...] = (unit_m * gain_m + shift_m).astype(BF16)
    upstream = cotangent[:USED, :].astype(F32)
    branch_grad[...] = (live * upstream).astype(BF16)
    branch[...] = jnp.zeros((USED, D), F32)
    mlp_back[...] = jnp.zeros((USED, D), F32)
    for copy in weight_copies():
        copy.wait()

    def feed_forward(c, _):
        up = arena[c]
        down = arena[blocks + c]
        before = dot(normed_mlp[...], up, NN) + vectors[pl.ds(c, 1), :]
        chance = 0.5 + 0.5 * lax.erf(before * 0.5**0.5)
        density = jnp.exp(-0.5 * before * before) * 0.3989422804014327
        activated = (before * chance).astype(BF16)
        slope = chance + before * density
        start = pl.multiple_of(2 * c * D, D)
        grads[pl.ds(start, D), :] = dot(activated, branch_grad[...], TN).astype(BF16)
        branch[...] += dot(activated, down, NN)
        before_full = dot(branch_grad[...], down, NT) * slope
        before_grad = before_full.astype(BF16)
        sums_out[pl.ds(c, 1), :] = jnp.sum(before_grad.astype(F32), 0, keepdims=True)
        grads[pl.ds(start + D, D), :] = dot(normed_mlp[...], before_grad, TN).astype(BF16)
        mlp_back[...] += dot(before_grad, up, NT)
        if fine:
            tick(2 * c)
            tick(2 * c + 1)
        return 0

    lax.fori_loop(0, blocks, feed_forward, 0)
    block_output[:USED, :] = (residual[...] + live * (branch[...] + vectors[4:5, :])).astype(BF16)
    block_output[USED:, :] = tokens[USED:, :]
    unit_m, scale_m = normalise(residual[...])
    back = mlp_back[...]
    sums_out[4:5, :] = jnp.sum(branch_grad[...].astype(F32), 0, keepdims=True)
    sums_out[5:6, :] = jnp.sum(back * unit_m, 0, keepdims=True)
    sums_out[6:7, :] = jnp.sum(back, 0, keepdims=True)
    res_grad = upstream + norm_backward(back, unit_m, scale_m, gain_m)
    grad_tokens[:USED, :] = res_grad
    grad_tokens[USED:, :] = cotangent[USED:, :].astype(F32)
    attended_grad = (live * res_grad).astype(BF16)
    base = 2 * FF
    out_grad = dot(mixed[...], attended_grad, TN).astype(BF16)
    for i in range(PAIRS):
        grads[base + i * D : base + i * D + PAIR, :] = out_grad[i * PAIR : (i + 1) * PAIR, :]
    mixed_grad[...] = dot(attended_grad, w_output[...], NT).astype(BF16)

    branch[...] = jnp.zeros((USED, D), F32)

    def backward_pair(i, _):
        p = PAIRS - 1 - i
        columns = pl.ds(pl.multiple_of(p * PAIR, PAIR), PAIR)
        grad = mixed_grad[:, columns].astype(F32)
        inv = inverse[:, columns]
        scaled = grad * inv
        product = scaled * mixed_full[:, columns]
        scaled_low = scaled.astype(BF16)
        scaled_t = scaled.T.astype(BF16)
        query_t = query[:, columns].astype(F32).T.astype(BF16)
        query_parts = []
        start = pl.multiple_of(p * PAIR, PAIR)

        def settle():
            for half in range(2):
                unspill(p, half).wait()

        pl.when(p < 2)(settle)
        for half in range(2):
            here = low_half if half == 0 else jnp.logical_not(low_half)
            dots = -jnp.sum(jnp.where(here, product, 0.0), -1, keepdims=True)
            dots_high = dots.astype(BF16)
            dots_low = (dots - dots_high.astype(F32)).astype(BF16)
            other = HEAD_DIM * (1 - half)
            rest = jnp.where(
                lane == other, dots_high, jnp.where(lane == other + 1, dots_low, jnp.zeros((), BF16))
            )
            weight = weights[2 * lax.rem(p, 2) + half]
            slope = dot(half_of(half, scaled_low, rest), head_values(p, half), NT)
            score_grad = weight * slope.astype(BF16)
            query_parts.append(dot(score_grad, head_keys(p, half), NN))
            rows = slice(half * HEAD_DIM, (half + 1) * HEAD_DIM)
            at = start + half * HEAD_DIM
            keyval_grad[pl.ds(at, HEAD_DIM), :] = dot(query_t[rows, :], score_grad, NN).astype(BF16)
            keyval_grad[pl.ds(D + at, HEAD_DIM), :] = dot(scaled_t[rows, :], weight, NN).astype(BF16)
            if fine and half == 0:
                tick(2 * blocks + 2 * i)

        def load():
            for half in range(2):
                unspill(p - 2, half).start()

        pl.when(p >= 2)(load)
        part = jnp.where(low_half, query_parts[0], query_parts[1]) * HEAD_DIM**-0.5
        query_grad = part.astype(BF16)
        at = pl.multiple_of(base + i * D, D)
        grads[pl.ds(at + PAIR, PAIR), :] = dot(query_grad, query_norm[...], TN).astype(BF16)
        for c in range(2):
            of_pair = keyval_grad[pl.ds(c * D + start, PAIR), :]
            grads[pl.ds(at + (2 + c) * PAIR, PAIR), :] = dot(of_pair, normed_all[...], NN).astype(
                BF16
            )
        branch[...] += dot(query_grad, w_query[:, columns], NT)
        if fine:
            tick(2 * blocks + 2 * i + 1)
        return 0

    lax.fori_loop(0, PAIRS, backward_pair, 0)

    from_query = branch[...]
    normed = query_norm[...].astype(F32)
    shift_sum = jnp.sum(from_query, 0, keepdims=True)
    gain_sum = jnp.sum(from_query * normed, 0, keepdims=True)

    def parts_at(j):
        return weights.at[0, :, (j - 1) * D : j * D]

    for j in range(VIEWS + 1):
        rows = slice(j * PATCHES, min((j + 1) * PATCHES, KEYS))
        piece = dot(keyval_grad[:, rows], w_keyval[...], TT)
        normed = normed_all[rows, :].astype(F32)
        shift_sum += jnp.sum(piece, 0, keepdims=True)
        gain_sum += jnp.sum(piece * normed, 0, keepdims=True)
        if j == 0:
            branch[:PATCHES, :] += piece
        elif j < VIEWS:
            parts_at(j)[:PATCHES, :] = piece.astype(BF16)
        else:
            branch[PATCHES:, :] += jnp.where(my_view == 0, piece, 0.0)
            for i in range(1, VIEWS):
                holds = lax.rem(my_view + i, VIEWS) == 0
                parts_at(i)[PATCHES:, :] = jnp.where(holds, piece, 0.0).astype(BF16)
    sums_out[7:8, :] = (gain_sum - shift_a * shift_sum) / gain_a
    sums_out[8:9, :] = shift_sum
    sums_out[9:, :] = jnp.zeros((SUMS - 9, D), F32)

    def part_for(offset):
        slot = lax.rem(offset + VIEWS, VIEWS) - 1
        at = my_view + offset
        valid = jnp.logical_and(at >= 0, at < VIEWS)
        value = jnp.zeros((USED, D), BF16)
        for n in range(VIEWS - 1):
            value = jnp.where(jnp.logical_and(valid, slot == n), parts_at(n + 1)[...], value)
        return value

    def swap(n):
        return pltpu.make_async_remote_copy(
            arena.at[n, pl.ds(0, USED), :],
            arena.at[4 + n, pl.ds(0, USED), :],
            swap_sem.at[0, n],
            swap_sem.at[1, n],
            sibling,
            MESH,
        )

    far = (2 + 0 * step, -2 + 0 * step, 4 * step, -4 * step)

    def far_copy(n):
        return pltpu.make_async_remote_copy(
            arena.at[(n + 1) % 4, pl.ds(0, USED), :],
            far_in.at[n],
            far_sem.at[0, n],
            far_sem.at[1, n],
            along(far[n]),
            MESH,
        )

    ticks = 2 * blocks + 2 * PAIRS if fine else 0
    last = ticks + STAGES * SKEW if fine else chunks + STAGES * SKEW

    def run_ticks(first, end):
        def body(t, _):
            tick(t)
            return 0

        lax.fori_loop(first, end, body, 0)

    if not fine:
        run_ticks(0, SKEW + 1)
        ticks = SKEW + 1
    sums_start(0, sums_out[...])
    for n, offset in enumerate((step, 2 + step, -2 + step, -3 * step)):
        arena[n, :USED, :] = part_for(offset)
        swap(n).start()
    run_ticks(ticks, ticks + 1)
    sums_start(1, sums_finish(0))
    swap(0).wait()
    arena[0, :USED, :] = part_for(far[3])
    far_copy(3).start()
    for n in range(3):
        swap(n + 1).wait()
        both = part_for(far[n]).astype(F32) + arena[5 + n, :USED, :].astype(F32)
        arena[n + 1, :USED, :] = both.astype(BF16)
        far_copy(n).start()
    run_ticks(ticks + 1, ticks + 2)
    sums_start(2, sums_finish(1))
    run_ticks(ticks + 2, ticks + 4)
    sums_start(3, sums_finish(2))
    run_ticks(ticks + 4, last)
    sums_out[...] = sums_finish(3)
    total = branch[...] + arena[4, :USED, :].astype(F32)
    for n in range(4):
        far_copy(n).wait()
        total += far_in[n].astype(F32)
    unit, scale = normalise(tokens[:USED, :].astype(F32))
    grad_tokens[:USED, :] += norm_backward(total, unit, scale, gain_a)


def main(count, groups, *args):
    depth = count // 4
    part_rows = 2 * groups * depth * SHARD
    parts = 2 if part_rows < D else 1
    chunk_rows = parts * part_rows
    chunks = -(-GRAD_ROWS // chunk_rows)
    shape = jax.ShapeDtypeStruct
    dma = pltpu.SemaphoreType.DMA
    wide = max(groups, depth)
    half = D // 2
    orders = ((2, groups, depth), (groups, 2, depth))[-parts:]
    slots = [sum(order[stage] - 1 for order in orders) for stage in range(3)]
    left = [part_rows // order[0] for order in orders]
    first = max(left)
    second = max(rows // order[1] for rows, order in zip(left, orders))
    scratch = [
        VMEM((KEYS_PADDED, D), BF16),
        VMEM((USED, D), BF16),
        VMEM((KEYS_PADDED, PAIR), BF16),
        VMEM((KEYS_PADDED, 2 * D), BF16),
        VMEM((USED, D), BF16),
        VMEM((4, USED, KEYS_PADDED), BF16),
        VMEM((USED, D), BF16),
        VMEM((USED, D), F32),
        VMEM((USED, D), F32),
        VMEM((2 * D, KEYS_PADDED), BF16),
        VMEM((USED, D), BF16),
        VMEM((USED, D), BF16),
        VMEM((USED, D), BF16),
        VMEM((USED, D), F32),
        VMEM((USED, D), F32),
        VMEM((USED, D), F32),
        VMEM((2 * VIEWS - 1, SENT - USED, D), BF16),
        VMEM((2 * FF // D, D, D), BF16),
        VMEM((chunks * chunk_rows, D), BF16),
        VMEM((chunks, chunk_rows, half), BF16),
        VMEM((chunks, slots[0], first, half), BF16),
        VMEM((chunks, slots[1], second, half), BF16),
        VMEM((chunks, slots[2], SHARD, half), BF16),
        VMEM((4, USED, D), BF16),
        VMEM((4, wide, SUMS, D), F32),
        dma((2, 2 * VIEWS - 1)),
        dma((2 * FF // D,)),
        dma((2, 2)),
        dma((chunks, STAGES, 2 * wide)),
        dma((chunks, STAGES, 2 * wide)),
        dma((chunks, 2)),
        dma((4, wide)),
        dma((4, wide)),
        dma((2, 4)),
        dma((2, 4)),
    ]
    return pl.pallas_call(
        functools.partial(main_kernel, count, groups, chunks, part_rows),
        out_shape=(
            shape((ROWS, D), BF16),
            shape((ROWS, D), F32),
            shape((chunks * chunk_rows, D), BF16),
            shape((SUMS, D), F32),
            shape((4, USED, KEYS_PADDED), BF16),
        ),
        in_specs=[IN_SMEM] * 2 + [ANYWHERE] + [IN_VMEM] * 5 + [ANYWHERE] * 2 + [IN_VMEM],
        out_specs=[IN_VMEM, IN_VMEM, ANYWHERE, IN_VMEM, ANYWHERE],
        scratch_shapes=scratch,
        compiler_params=pltpu.CompilerParams(
            collective_id=1, has_side_effects=True, vmem_limit_bytes=63 * MIB
        ),
        name="main",
    )(*args)


def widen_kernel(block, down, up, out, query, keyval):
    b = pl.program_id(0)
    blocks = FF // D

    def store_rows():
        down[...] = block[...].astype(F32)

    def store_columns():
        up[...] = block[...].astype(F32)

    def store_pair():
        out[...] = block[:PAIR, :].astype(F32)
        query[...] = block[PAIR : 2 * PAIR, :].astype(F32).T
        keyval[...] = block[2 * PAIR : 3 * PAIR, :].astype(F32).T

    def store_values():
        keyval[...] = block[3 * PAIR :, :].astype(F32).T

    early = b < 2 * blocks
    pl.when(jnp.logical_and(early, lax.rem(b, 2) == 0))(store_rows)
    pl.when(jnp.logical_and(early, lax.rem(b, 2) == 1))(store_columns)
    pl.when(jnp.logical_and(b >= 2 * blocks, b < 2 * blocks + PAIRS))(store_pair)
    pl.when(b >= 2 * blocks + PAIRS)(store_values)


def widen(summed):
    blocks = FF // D
    late = 2 * blocks + PAIRS
    shape = jax.ShapeDtypeStruct

    def pair(b):
        return PAIRS - 1 - jnp.clip(b - 2 * blocks, 0, PAIRS - 1)

    def keyval_column(b):
        return jnp.where(b < late, pair(b), 2 * PAIRS - 1 - (b - late))

    return pl.pallas_call(
        widen_kernel,
        grid=(late + PAIRS,),
        out_shape=(
            shape((FF, D), F32),
            shape((D, FF), F32),
            shape((D, D), F32),
            shape((D, D), F32),
            shape((D, 2 * D), F32),
        ),
        in_specs=[pl.BlockSpec((D, D), lambda b: (jnp.where(b < late, b, b - PAIRS), 0))],
        out_specs=[
            pl.BlockSpec((D, D), lambda b: (jnp.clip(b // 2, 0, blocks - 1), 0)),
            pl.BlockSpec((D, D), lambda b: (0, jnp.clip(b // 2, 0, blocks - 1))),
            pl.BlockSpec((PAIR, D), lambda b: (jnp.clip(b - 2 * blocks, 0, PAIRS - 1), 0)),
            pl.BlockSpec((D, PAIR), lambda b: (0, pair(b))),
            pl.BlockSpec((D, PAIR), lambda b: (0, keyval_column(b))),
        ],
        name="widen",
    )(summed)


def on_device(
    count,
    groups,
    tokens,
    counts,
    slot_item,
    slot_view,
    keyframe,
    w_query,
    w_keyval,
    w_output,
    w_up,
    bias_up,
    w_down,
    bias_down,
    gain_attn,
    shift_attn,
    gain_mlp,
    shift_mlp,
    cotangent,
):
    rows = tokens.reshape(ROWS, D)
    item = slot_item.reshape(())
    filled = (counts.reshape(()) > 0) & (keyframe.reshape(()) == 1) & (item >= 0)
    label = jnp.where(filled, item, -1).astype(BF16)
    block = jnp.concatenate([rows[:USED], jnp.broadcast_to(label, (SENT - USED, D))])
    window = gather_window(block, count)
    vectors = jnp.concatenate(
        [bias_up, bias_down, gain_attn, shift_attn, gain_mlp, shift_mlp, jnp.zeros((7 * D,), BF16)]
    )
    vectors = vectors.astype(F32).reshape(SUMS, D)
    block_output, grad_tokens, summed, sums, _ = main(
        count,
        groups,
        slot_view.reshape(1),
        filled.astype(jnp.int32).reshape(1),
        window,
        rows,
        cotangent.reshape(ROWS, D),
        w_query,
        w_keyval,
        w_output,
        w_up,
        w_down,
        vectors,
    )
    down, up, out, query, keyval = widen(summed)
    return (
        block_output.reshape(tokens.shape),
        grad_tokens.reshape(tokens.shape),
        query,
        keyval,
        out,
        up,
        sums[:4].reshape(-1),
        down,
        sums[4],
        sums[7],
        sums[8],
        sums[5],
        sums[6],
    )


def solution(mesh):
    count = mesh.shape["view"]
    groups = mesh.shape["dp"]
    slots = P("dp", "view", None)
    rows = P("dp", "view", None, None, None)
    in_specs = (rows, P("dp", "view"), slots, slots, slots) + (P(),) * 11 + (rows,)
    out_specs = (rows, rows) + (P(),) * 11
    return jax.shard_map(
        functools.partial(on_device, count, groups),
        mesh=mesh,
        in_specs=in_specs,
        out_specs=out_specs,
        check_vma=False,
    )
```

time: 409 us -> 229 us (0.56)
  blocking collectives: 240 us -> 0 us
  Pallas kernels: 104 us -> 212 us
  other arithmetic: 14.5 us -> 0 us
  waiting for transfers between devices: 13 us -> 0 us
  local copies, waits for them, and re-layouts: 24 us -> 12.4 us
  starting transfers between devices: 9.18 us -> 0 us
    psum x1 -> x0, blocking collectives: 240 us -> none  [on_device(): lax.psum((grads.astype(F32), sums_up, sums), ('view', 'dp'))]
    pallas_call x1 -> x2, Pallas kernels: 59.9 us -> 168 us  [the longest x1 155 us: main(): pl.pallas_call(functools.partial(main_kernel, count, groups, chunks, part...]
    ppermute x8 -> x0, waiting for transfers between devices: 13 us -> none  [on_device(): total = total + lax.ppermute(sent, 'view', pairs).astype(F32)]
    slice x5 -> x1, local copies, waits for them, and re-layouts: 10.9 us -> 1.46 us  [on_device(): sums[6]]
    ppermute x8 -> x0, starting transfers between devices: 9.18 us -> none  [on_device(): total = total + lax.ppermute(sent, 'view', pairs).astype(F32)]
    reshape x6 -> x0, local copies, waits for them, and re-layouts: 7.58 us -> none  [on_device(): weights = tuple((w.reshape(1, -1) if w.ndim == 1 else w for w in weights))]
    unnamed x19 -> x14, local copies, waits for them, and re-layouts: 1.86 us -> 8.18 us
    concatenate x1 -> x0, other arithmetic: 4.73 us -> none  [on_device(): jnp.concatenate([grads[c * D:(c + 1) * D] for c in range(FF // D)], 1)]
  transfers between devices with their start and end apart: 8 -> 0, of which waited for: 2 -> 0; matrix products, arithmetic and copies ran while one was open for 5% -> 0% of each run, Pallas kernels for 0% -> 0%
where the time goes in v3:
time: 229 us; the launch traced here: 228 us
  Pallas kernels  212 us (93%)
  local copies, waits for them, and re-layouts  12.4 us (5%)
  between operations  3.29 us (1%)
    pallas_call x1, Pallas kernels, main(): pl.pallas_call(functools.partial(main_kernel, count, groups, chunks, part...  155 us
    pallas_call x1, Pallas kernels, gather_window(): pl.pallas_call(functools.partial(gather_kernel, count), out_shape=jax.Sha...  43.8 us
    pallas_call x1, Pallas kernels, widen(): pl.pallas_call(widen_kernel, grid=(late + PAIRS,), out_shape=(shape((FF,...  13.8 us
    unnamed x14, local copies, waits for them, and re-layouts  8.18 us

profile of v3, /device:TPU:0, one launch (start us, length us, event | category | flops | bytes accessed | tf_op | source)
XLA Modules:
  0.0 228.0 jit_solution(3125060983693682882)
XLA Ops:
  3.2 0.7 constant_dynamic-update-slice_fusion
  3.9 0.9 dynamic-update-slice.1
  4.8 0.9 dynamic-update-slice.2
  5.6 0.9 dynamic-update-slice.3
  6.5 0.9 dynamic-update-slice.4
  7.4 0.9 dynamic-update-slice.5
  8.2 0.3 dynamic-update-slice.6
  8.5 0.6 reshape.74.vectors
  9.1 1.1 slice_bitcast_fusion
  10.2 0.8 concatenate.6.block
  11.0 43.8 %gather_window.1.window = bf16[9,496,512]{2,1,0:T(8,128)(2,1)} custom-call(bf16[496,512]{1,0:T(8,128)(2,1)} %concatenate.6.block), custom_call_target="tpu_custom_call" | custom-call | tf_op jit(solution)/shard_map/gather_window/pallas_call | solution.py:126
  54.8 154.7 %main.1 = (bf16[512,512]{1,0:T(8,128)(2,1)}, f32[512,512]{1,0:T(8,128)}, bf16[6144,512]{1,0:T(8,128)(2,1)}, f32[16,512]{1,0:T(8,128)}, bf16[4,480,2176]{2,1,0:T(8,128)(2,1)}) custom-call(s32[1]{0:T(128)} %bitcast.21.view, s32[1]{0:T(128)} %bitcast.4.filled, bf16[9,496,512]{2,1,0:T(8,128)(2,1)} %gather_window.1.window, bf16[512,512]{1,0:T(8,128)(2,1)} %bitcast.22, ...), custom_call_target="tpu_custom_call" | custom-call | tf_op jit(solution)/shard_map/main/pallas_call | solution.py:782
  209.5 0.0 copy-start.1
  209.6 0.0 copy-start
  209.6 0.8 slice_bitcast_fusion.1
  210.4 1.5 fusion
  211.9 0.6 copy.30
  212.5 13.8 %widen.1 = (f32[2048,512]{1,0:T(8,128)}, f32[512,2048]{1,0:T(8,128)}, f32[512,512]{1,0:T(8,128)}, f32[512,512]{1,0:T(8,128)}, f32[512,1024]{1,0:T(8,128)}) custom-call(bf16[6144,512]{1,0:T(8,128)(2,1)} %get-tuple-element.24.block), custom_call_target="tpu_custom_call" | custom-call | tf_op jit(solution)/shard_map/widen/pallas_call | solution.py:837
  226.2 0.0 copy-done.1
  226.2 0.8 copy.43
  227.0 0.0 copy-done
  227.0 1.0 copy.44
  (1 shorter events, 0.0 us)
Async XLA Ops:
  209.5 16.7 %copy-start.1 = (bf16[512,512]{1,0:T(8,128)(2,1)S(1)}, bf16[512,512]{1,0:T(8,128)(2,1)}, u32[]{:S(2)}) copy-start(bf16[512,512]{1,0:T(8,128)(2,1)} %get-tuple-element.22) | copy-start | bytes 1572868
  209.6 17.5 %copy-start = (f32[512,512]{1,0:T(8,128)S(1)}, f32[512,512]{1,0:T(8,128)}, u32[]{:S(2)}) copy-start(f32[512,512]{1,0:T(8,128)} %get-tuple-element.23) | copy-start | bytes 3145732

commit v4 on v3

--- a/solution.py
+++ b/solution.py
@@ -30,6 +30,8 @@
 SHARD = 16
 STAGES = 8
 SKEW = 2
+IN_FLIGHT = 4
+PIECES = ((0, 128), (128, 128), (256, 128), (384, 112))
 
 BF16 = jnp.bfloat16
 F32 = jnp.float32
@@ -72,84 +74,28 @@
     pl.semaphore_wait(barrier, len(others))
 
 
-def gather_kernel(count, block, window, own_sem, send_sem, recv_sem, pass_sem, given_sem):
-    me = lax.axis_index("view")
-    step = 1 - 2 * lax.rem(me, 2)
-
-    def at(offset):
-        return {"view": lax.rem(me + offset + count, count)}
-
-    far = (4, -4, 2, -2)
-    greet([at(offset) for offset in far] + [at(step)])
-    own = pltpu.make_async_copy(block, window.at[4], own_sem)
-    own.start()
-
-    def to(k, offset):
-        return pltpu.make_async_remote_copy(
-            block, window.at[4 - offset], send_sem.at[k], recv_sem.at[k], at(offset), MESH
-        )
-
-    def across(k, offset, source):
-        return pltpu.make_async_remote_copy(
-            source,
-            window.at[4 + offset - step],
-            pass_sem.at[k],
-            given_sem.at[k],
-            at(step),
-            MESH,
-        )
-
-    sends = [to(k, offset) for k, offset in enumerate(far)]
-    for copy in sends:
-        copy.start()
-    passes = [across(0, 0, block)]
-    passes[0].start()
-    for k, offset in ((2, -2), (3, 2)):
-        sends[k].wait_recv()
-        copy = across(k - 1, offset, window.at[4 + offset])
-        copy.start()
-        passes.append(copy)
-    even = lax.rem(me, 2) == 0
-    for k in (0, 1):
-        sends[k].wait_recv()
-    copy = across(3, 4 * step, window.at[4 + 4 * step])
-    copy.start()
-    passes.append(copy)
-    for copy in passes:
-        copy.wait()
-    for copy in sends:
-        copy.wait_send()
-    own.wait()
-
-
-def gather_window(block, count):
-    return pl.pallas_call(
-        functools.partial(gather_kernel, count),
-        out_shape=jax.ShapeDtypeStruct((2 * VIEWS - 1, SENT, D), BF16),
-        in_specs=[ANYWHERE],
-        out_specs=ANYWHERE,
-        scratch_shapes=[pltpu.SemaphoreType.DMA] + [pltpu.SemaphoreType.DMA((4,))] * 4,
-        compiler_params=pltpu.CompilerParams(collective_id=0, has_side_effects=True),
-        name="gather_window",
-    )(block)
-
-
 def main_kernel(
     count,
     groups,
     chunks,
     part_rows,
-    view,
-    filled,
-    window,
+    counts,
+    slot_item,
+    slot_view,
+    keyframe,
     tokens,
     cotangent,
     w_query,
     w_keyval,
     w_output,
+    bias_up,
+    bias_down,
+    gain_attn,
+    shift_attn,
+    gain_mlp,
+    shift_mlp,
     w_up,
     w_down,
-    vectors,
     block_output,
     grad_tokens,
     summed,
@@ -171,7 +117,8 @@
     residual,
     branch,
     mlp_back,
-    labels,
+    sent,
+    vectors,
     arena,
     grads,
     arrived_core,
@@ -180,7 +127,8 @@
     arrived_last,
     far_in,
     sums_at,
-    window_sem,
+    there_sem,
+    here_sem,
     weight_sem,
     spill_sem,
     send_sem,
@@ -216,18 +164,10 @@
 
     sibling = {"view": me + step}
 
-    def window_at(n):
-        return weights.at[n // 4, :, pl.ds(n % 4 * D, D)]
-
-    def window_copies(n):
-        return (
-            pltpu.make_async_copy(
-                window.at[n, pl.ds(0, USED), :], window_at(n), window_sem.at[0, n]
-            ),
-            pltpu.make_async_copy(
-                window.at[n, pl.ds(USED, SENT - USED), :], labels.at[n], window_sem.at[1, n]
-            ),
-        )
+    def window_at(offset, first, rows):
+        n = VIEWS - 1 + offset
+        columns = pl.ds(pl.multiple_of(lax.rem(n, 4) * D, D), D)
+        return weights.at[n // 4, pl.ds(first, rows), columns]
 
     def weight_copies():
         blocks = FF // D
@@ -243,13 +183,62 @@
             for c in range(blocks)
         ]
 
-    for n in range(2 * VIEWS - 1):
-        for copy in window_copies(n):
-            copy.start()
     for copy in weight_copies():
         copy.start()
+    my_view = slot_view[0]
+    is_filled = jnp.logical_and(
+        jnp.logical_and(counts[0] > 0, keyframe[0] == 1), slot_item[0] >= 0
+    )
+    my_filled = is_filled.astype(jnp.int32)
+    label_here = jnp.where(is_filled, slot_item[0], -1).astype(F32)
+    sent[: SENT - USED, :] = jnp.full((SENT - USED, D), label_here, F32).astype(BF16)
+    sent[SENT - USED :, :] = tokens[:USED, :]
     peers = [peer(dim, j) for dim in "xyz" for j in range(1, size[dim])]
-    greet([sibling] + peers + [along(offset) for offset in (4, -4, 2, -2)])
+    greet([sibling] + peers)
+
+    turn = 1 - 2 * place["x"]
+
+    def hop(kind, source, offset, first, rows, device):
+        return pltpu.make_async_remote_copy(
+            source,
+            window_at(offset, first, rows),
+            there_sem.at[kind],
+            here_sem.at[kind],
+            device,
+            MESH,
+        )
+
+    def piece_kind(line, q):
+        return line * len(PIECES) + q
+
+    def along_z(line, q):
+        first, rows = PIECES[q]
+        ahead = 4 - 8 * line
+        source = sent.at[pl.ds(first, rows), :]
+        return hop(piece_kind(line, q), source, -ahead, first, rows, along(ahead))
+
+    def relay_x(q):
+        first, rows = PIECES[q]
+        source = window_at(4 * turn, first, rows)
+        return hop(piece_kind(2, q), source, 2 * turn, first, rows, along(2 * turn))
+
+    def across_relayed(q):
+        first, rows = PIECES[q]
+        source = window_at(-2 * turn, first, rows)
+        return hop(piece_kind(3, q), source, -2 * turn - step, first, rows, sibling)
+
+    last_kind = 4 * len(PIECES)
+    direct_x = hop(last_kind, sent, -2 * turn, 0, SENT, along(2 * turn))
+    across_own = hop(last_kind + 1, sent, -step, 0, SENT, sibling)
+    across_x = hop(
+        last_kind + 2, window_at(2 * turn, 0, SENT), 2 * turn - step, 0, SENT, sibling
+    )
+    across_z = hop(last_kind + 3, window_at(4 * step, 0, SENT), 3 * step, 0, SENT, sibling)
+    for q in range(len(PIECES)):
+        for line in range(2):
+            along_z(line, q).start()
+    direct_x.start()
+    across_own.start()
 
     levels = []
     for order in orders:
@@ -273,19 +262,26 @@
     def rows_of(k, p, offset, rows):
         return pl.ds(pl.multiple_of(k * chunk_rows + p * part_rows + offset, SHARD), rows)
 
+    def held(k):
+        return lax.rem(k, IN_FLIGHT)
+
+    first_sem = [0]
+    for stage in range(STAGES):
+        first_sem.append(first_sem[-1] + stage_copies(stage, size, orders))
+
     def copies(stage, k):
         out = []
 
         def add(source, target, device):
-            n = len(out)
+            n = first_sem[stage] + len(out)
             out.append(
                 pltpu.make_async_remote_copy(
-                    source, target, send_sem.at[k, stage, n], recv_sem.at[k, stage, n], device, MESH
+                    source, target, send_sem.at[held(k), n], recv_sem.at[held(k), n], device, MESH
                 )
             )
 
         if stage == 0:
-            add(grads.at[rows_of(k, 0, 0, chunk_rows), other_columns], arrived_core.at[k], sibling)
+            add(grads.at[rows_of(k, 0, 0, chunk_rows), other_columns], arrived_core.at[held(k)], sibling)
         elif stage == 7:
             whole = summed.at[rows_of(k, 0, 0, chunk_rows), own_columns]
             add(whole, whole, sibling)
@@ -298,7 +294,7 @@
                     at = offset + lax.rem(place[dim] + j, size[dim]) * rows
                     add(
                         grads.at[rows_of(k, p, at, rows), own_columns],
-                        arrived[stage - 1].at[k, slot_of(stage, p, j), pl.ds(0, rows), :],
+                        arrived[stage - 1].at[held(k), slot_of(stage, p, j), pl.ds(0, rows), :],
                         peer(dim, j),
                     )
             elif 4 <= stage < 7:
@@ -313,7 +309,7 @@
     def own_shard(k, p):
         at = rows_of(k, p, *levels[p][3])
         return pltpu.make_async_copy(
-            grads.at[at, own_columns], summed.at[at, own_columns], local_sem.at[k, p]
+            grads.at[at, own_columns], summed.at[at, own_columns], local_sem.at[held(k), p]
         )
 
     def start_stage(stage, k):
@@ -331,7 +327,7 @@
                 own_shard(k, p).wait()
         if stage == 0:
             at = rows_of(k, 0, 0, chunk_rows)
-            total = grads[at, own_columns].astype(F32) + arrived_core[k].astype(F32)
+            total = grads[at, own_columns].astype(F32) + arrived_core[held(k)].astype(F32)
             grads[at, own_columns] = total.astype(BF16)
         elif stage < 4:
             for p, order in enumerate(orders):
@@ -339,7 +335,7 @@
                 at = rows_of(k, p, offset, rows)
                 total = grads[at, own_columns].astype(F32)
                 for j in range(1, size[order[stage - 1]]):
-                    total += arrived[stage - 1][k, slot_of(stage, p, j), :rows, :].astype(F32)
+                    total += arrived[stage - 1][held(k), slot_of(stage, p, j), :rows, :].astype(F32)
                 grads[at, own_columns] = total.astype(BF16)
 
     blocks = FF // D
@@ -400,59 +396,82 @@
             total += sums_at[level, i]
         return total
 
-    my_view = view[0]
-    my_filled = filled[0]
+    for c in range(blocks):
+        vectors[c : c + 1, :] = bias_up[c * D : (c + 1) * D].astype(F32).reshape(1, D)
+    for n, vector in enumerate((bias_down, gain_attn, shift_attn, gain_mlp, shift_mlp)):
+        vectors[4 + n : 5 + n, :] = vector[...].astype(F32).reshape(1, D)
     gain_a = vectors[5:6, :]
     shift_a = vectors[6:7, :]
     gain_m = vectors[7:8, :]
     shift_m = vectors[8:9, :]
 
+    def project_keys(first, rows, values):
+        unit, _ = normalise(values.astype(F32))
+        normed = (unit * gain_a + shift_a).astype(BF16)
+        normed_all[first : first + rows, :] = normed
+        keyval[first : first + rows, :] = dot(normed, w_keyval[...], NN).astype(BF16)
+
     own_rows = tokens[:USED, :]
     own_unit, _ = normalise(own_rows.astype(F32))
-    own_normed = (own_unit * gain_a + shift_a).astype(BF16)
-    query_norm[...] = own_normed
-    normed_all[:PATCHES, :] = own_normed[:PATCHES, :]
-    query[...] = (dot(own_normed, w_query[...], NN).astype(BF16) * HEAD_DIM**-0.5).astype(BF16)
-    for n in range(2 * VIEWS - 1):
-        for copy in window_copies(n):
-            copy.wait()
-    my_label = labels[VIEWS - 1, :, :PAIR].astype(F32)
+    query_norm[...] = (own_unit * gain_a + shift_a).astype(BF16)
+    query[...] = (dot(query_norm[...], w_query[...], NN).astype(BF16) * HEAD_DIM**-0.5).astype(BF16)
+    project_keys(0, PATCHES, own_rows[:PATCHES, :])
+    relayed = jnp.where(turn > 0, 1, 0)
+    for q in range(len(PIECES)):
+        along_z(relayed, q).wait_recv()
+        relay_x(q).start()
+    direct_x.wait_recv()
+    across_x.start()
+    for q in range(len(PIECES)):
+        along_z(1 - relayed, q).wait_recv()
+    across_z.start()
+    for q in range(len(PIECES)):
+        relay_x(q).wait_recv()
+        across_relayed(q).start()
+    for copy in (across_own, across_x, across_z):
+        copy.wait()
+    direct_x.wait_send()
+    for q in range(len(PIECES)):
+        for line in range(2):
+            along_z(line, q).wait_send()
+        relay_x(q).wait_send()
+        across_relayed(q).wait()
+    my_label = sent[: SENT - USED, :PAIR].astype(F32)
 
     def bias_of(label):
         match = jnp.logical_and(label == my_label, label >= 0)
         return jnp.where(match, 0.0, NEGATIVE)[:1, :]
 
-    def window_block(n, rows):
-        return weights[n // 4, rows, n % 4 * D : (n % 4 + 1) * D]
+    def block_at(n, first, rows, columns=D):
+        return weights[n // 4, first : first + rows, n % 4 * D : n % 4 * D + columns]
 
     key_bias[:PATCHES, :] = jnp.broadcast_to(bias_of(my_label), (PATCHES, PAIR)).astype(BF16)
     language = own_rows[PATCHES:, :]
     language_bias = bias_of(my_label)
+    top_rows = SENT - USED
     for j in range(1, VIEWS):
         ahead = my_view + j < VIEWS
-        block = jnp.where(
-            ahead, window_block(4 + j, slice(0, USED)), window_block(j - 1, slice(0, USED))
-        )
-        label = jnp.where(ahead, labels[4 + j, :, :PAIR], labels[j - 1, :, :PAIR]).astype(F32)
-        unit, _ = normalise(block[:PATCHES, :].astype(F32))
+        holds = lax.rem(my_view + j, VIEWS) == 0
+
+        def either(first, rows, columns=D):
+            return jnp.where(
+                ahead, block_at(4 + j, first, rows, columns), block_at(j - 1, first, rows, columns)
+            )
+
+        project_keys(j * PATCHES, PATCHES, either(top_rows, PATCHES))
+        bias = bias_of(either(0, top_rows, PAIR).astype(F32))
         rows = slice(j * PATCHES, (j + 1) * PATCHES)
-        normed_all[rows, :] = (unit * gain_a + shift_a).astype(BF16)
-        bias = bias_of(label)
         key_bias[rows, :] = jnp.broadcast_to(bias, (PATCHES, PAIR)).astype(BF16)
-        holds = lax.rem(my_view + j, VIEWS) == 0
-        language = jnp.where(holds, block[PATCHES:, :], language)
+        language = jnp.where(holds, either(top_rows + PATCHES, TAIL), language)
         language_bias = jnp.where(holds, bias, language_bias)
-    unit, _ = normalise(language.astype(F32))
-    normed_all[VIEWS * PATCHES : KEYS, :] = (unit * gain_a + shift_a).astype(BF16)
+    project_keys(VIEWS * PATCHES, TAIL, language)
     index = lax.broadcasted_iota(jnp.int32, (TAIL, PAIR), 0)
     key_bias[VIEWS * PATCHES : KEYS, :] = jnp.where(
         index < LANG, jnp.broadcast_to(language_bias, (TAIL, PAIR)), NEGATIVE
     ).astype(BF16)
     normed_all[KEYS:, :] = jnp.zeros((KEYS_PADDED - KEYS, D), BF16)
+    keyval[KEYS:, :] = jnp.zeros((KEYS_PADDED - KEYS, 2 * D), BF16)
     key_bias[KEYS:, :] = jnp.full((KEYS_PADDED - KEYS, PAIR), NEGATIVE, BF16)
-    for c in range(2):
-        columns = slice(c * D, (c + 1) * D)
-        keyval[:, columns] = dot(normed_all[...], w_keyval[:, columns], NN).astype(BF16)
 
     lane = lax.broadcasted_iota(jnp.int32, (1, PAIR), 1)
     low_half = lane < HEAD_DIM
@@ -470,12 +489,12 @@
 
     def spill(p, half):
         return pltpu.make_async_copy(
-            weights.at[2 * lax.rem(p, 2) + half], spilled.at[2 * p + half], spill_sem.at[lax.rem(p, 2), half]
+            weights.at[2 * lax.rem(p, 2) + half, pl.ds(0, USED), :], spilled.at[2 * p + half], spill_sem.at[lax.rem(p, 2), half]
         )
 
     def unspill(p, half):
         return pltpu.make_async_copy(
-            spilled.at[2 * p + half], weights.at[2 * lax.rem(p, 2) + half], spill_sem.at[lax.rem(p, 2), half]
+            spilled.at[2 * p + half], weights.at[2 * lax.rem(p, 2) + half, pl.ds(0, USED), :], spill_sem.at[lax.rem(p, 2), half]
         )
 
     def forward_pair(p, _):
@@ -494,7 +513,7 @@
             scores = dot(half_of(half, pair, one), head_keys(p, half), NT)
             top = jnp.max(scores, -1, keepdims=True)
             weight = jnp.exp(scores - top).astype(BF16)
-            weights[2 * lax.rem(p, 2) + half] = weight
+            weights[2 * lax.rem(p, 2) + half, :USED, :] = weight
             out = dot(weight, head_values(p, half), NN)
             outs.append(out)
             totals.append(pltpu.roll(out, HEAD_DIM, 1))
@@ -596,7 +615,7 @@
             rest = jnp.where(
                 lane == other, dots_high, jnp.where(lane == other + 1, dots_low, jnp.zeros((), BF16))
             )
-            weight = weights[2 * lax.rem(p, 2) + half]
+            weight = weights[2 * lax.rem(p, 2) + half, :USED, :]
             slope = dot(half_of(half, scaled_low, rest), head_values(p, half), NT)
             score_grad = weight * slope.astype(BF16)
             query_parts.append(dot(score_grad, head_keys(p, half), NN))
@@ -634,7 +653,7 @@
     gain_sum = jnp.sum(from_query * normed, 0, keepdims=True)
 
     def parts_at(j):
-        return weights.at[0, :, (j - 1) * D : j * D]
+        return weights.at[0, :USED, (j - 1) * D : j * D]
 
     for j in range(VIEWS + 1):
         rows = slice(j * PATCHES, min((j + 1) * PATCHES, KEYS))
@@ -674,17 +693,31 @@
             MESH,
         )
 
-    far = (2 + 0 * step, -2 + 0 * step, 4 * step, -4 * step)
-
-    def far_copy(n):
+    back_pieces = ((0, 160), (160, 160), (320, 160))
+
+    def back(kind, slot, target, offset, q):
+        first, rows = back_pieces[q]
+        n = kind * len(back_pieces) + q
         return pltpu.make_async_remote_copy(
-            arena.at[(n + 1) % 4, pl.ds(0, USED), :],
-            far_in.at[n],
+            arena.at[slot, pl.ds(first, rows), :],
+            far_in.at[target, pl.ds(first, rows), :],
             far_sem.at[0, n],
             far_sem.at[1, n],
-            along(far[n]),
+            along(offset),
             MESH,
         )
+
+    def back_relay(q):
+        return back(0, 1, 0, 2 * turn, q)
+
+    def back_x(q):
+        return back(1, 2, 1, 2 * turn, q)
+
+    def back_up(q):
+        return back(2, 3, 2, 4 * turn, q)
+
+    def back_down(q):
+        return back(3, 0, 3, -4 * turn, q)
 
     ticks = 2 * blocks + 2 * PAIRS if fine else 0
     last = ticks + STAGES * SKEW if fine else chunks + STAGES * SKEW
@@ -700,19 +733,36 @@
         run_ticks(0, SKEW + 1)
         ticks = SKEW + 1
     sums_start(0, sums_out[...])
-    for n, offset in enumerate((step, 2 + step, -2 + step, -3 * step)):
+    for n, offset in enumerate((step, step - 2 * turn, step + 2 * turn, -3 * step)):
         arena[n, :USED, :] = part_for(offset)
         swap(n).start()
     run_ticks(ticks, ticks + 1)
     sums_start(1, sums_finish(0))
+    pieces = range(len(back_pieces))
+    for n, offset in ((1, -2 * turn), (2, 2 * turn)):
+        swap(n).wait()
+        both = part_for(offset).astype(F32) + arena[4 + n, :USED, :].astype(F32)
+        arena[n, :USED, :] = both.astype(BF16)
+        for q in pieces:
+            (back_relay if n == 1 else back_x)(q).start()
     swap(0).wait()
-    arena[0, :USED, :] = part_for(far[3])
-    far_copy(3).start()
-    for n in range(3):
-        swap(n + 1).wait()
-        both = part_for(far[n]).astype(F32) + arena[5 + n, :USED, :].astype(F32)
-        arena[n + 1, :USED, :] = both.astype(BF16)
-        far_copy(n).start()
+    swap(3).wait()
+    shared = arena[7, :USED, :].astype(F32)
+    arena[0, :USED, :] = (
+        part_for(-4 * turn).astype(F32) + jnp.where(step == turn, 0.0, shared)
+    ).astype(BF16)
+    for q in pieces:
+        back_down(q).start()
+    arena[3, :USED, :] = (
+        part_for(4 * turn).astype(F32) + jnp.where(step == turn, shared, 0.0)
+    ).astype(BF16)
+    for q in pieces:
+        first, rows = back_pieces[q]
+        at = slice(first, first + rows)
+        back_relay(q).wait_recv()
+        both = arena[3, at, :].astype(F32) + far_in[0, at, :].astype(F32)
+        arena[3, at, :] = both.astype(BF16)
+        back_up(q).start()
     run_ticks(ticks + 1, ticks + 2)
     sums_start(2, sums_finish(1))
     run_ticks(ticks + 2, ticks + 4)
@@ -720,11 +770,20 @@
     run_ticks(ticks + 4, last)
     sums_out[...] = sums_finish(3)
     total = branch[...] + arena[4, :USED, :].astype(F32)
-    for n in range(4):
-        far_copy(n).wait()
+    for q in pieces:
+        back_relay(q).wait_send()
+        for copy in (back_x(q), back_up(q), back_down(q)):
+            copy.wait()
+    for n in range(1, 4):
         total += far_in[n].astype(F32)
     unit, scale = normalise(tokens[:USED, :].astype(F32))
     grad_tokens[:USED, :] += norm_backward(total, unit, scale, gain_a)
+
+
+def stage_copies(stage, size, orders):
+    if stage in (0, 7):
+        return 1
+    return sum(size[order[stage - 1 if stage < 4 else 6 - stage]] - 1 for order in orders)
 
 
 def main(count, groups, *args):
@@ -739,6 +798,8 @@
     half = D // 2
     orders = ((2, groups, depth), (groups, 2, depth))[-parts:]
     slots = [sum(order[stage] - 1 for order in orders) for stage in range(3)]
+    sems = 2 + 2 * sum(slots)
+    held = min(chunks, IN_FLIGHT)
     left = [part_rows // order[0] for order in orders]
     first = max(left)
     second = max(rows // order[1] for rows, order in zip(left, orders))
@@ -748,7 +809,7 @@
         VMEM((KEYS_PADDED, PAIR), BF16),
         VMEM((KEYS_PADDED, 2 * D), BF16),
         VMEM((USED, D), BF16),
-        VMEM((4, USED, KEYS_PADDED), BF16),
+        VMEM((4, SENT, KEYS_PADDED), BF16),
         VMEM((USED, D), BF16),
         VMEM((USED, D), F32),
         VMEM((USED, D), F32),
@@ -759,25 +820,27 @@
         VMEM((USED, D), F32),
         VMEM((USED, D), F32),
         VMEM((USED, D), F32),
-        VMEM((2 * VIEWS - 1, SENT - USED, D), BF16),
+        VMEM((SENT, D), BF16),
+        VMEM((SUMS, D), F32),
         VMEM((2 * FF // D, D, D), BF16),
         VMEM((chunks * chunk_rows, D), BF16),
-        VMEM((chunks, chunk_rows, half), BF16),
-        VMEM((chunks, slots[0], first, half), BF16),
-        VMEM((chunks, slots[1], second, half), BF16),
-        VMEM((chunks, slots[2], SHARD, half), BF16),
+        VMEM((held, chunk_rows, half), BF16),
+        VMEM((held, slots[0], first, half), BF16),
+        VMEM((held, slots[1], second, half), BF16),
+        VMEM((held, slots[2], SHARD, half), BF16),
         VMEM((4, USED, D), BF16),
         VMEM((4, wide, SUMS, D), F32),
-        dma((2, 2 * VIEWS - 1)),
+        dma((4 * len(PIECES) + 4,)),
+        dma((4 * len(PIECES) + 4,)),
         dma((2 * FF // D,)),
         dma((2, 2)),
-        dma((chunks, STAGES, 2 * wide)),
-        dma((chunks, STAGES, 2 * wide)),
-        dma((chunks, 2)),
+        dma((held, sems)),
+        dma((held, sems)),
+        dma((held, 2)),
         dma((4, wide)),
         dma((4, wide)),
         dma((2, 4)),
-        dma((2, 4)),
+        dma((2, 12)),
     ]
     return pl.pallas_call(
         functools.partial(main_kernel, count, groups, chunks, part_rows),
@@ -788,7 +851,7 @@
             shape((SUMS, D), F32),
             shape((4, USED, KEYS_PADDED), BF16),
         ),
-        in_specs=[IN_SMEM] * 2 + [ANYWHERE] + [IN_VMEM] * 5 + [ANYWHERE] * 2 + [IN_VMEM],
+        in_specs=[IN_SMEM] * 4 + [IN_VMEM] * 11 + [ANYWHERE] * 2,
         out_specs=[IN_VMEM, IN_VMEM, ANYWHERE, IN_VMEM, ANYWHERE],
         scratch_shapes=scratch,
         compiler_params=pltpu.CompilerParams(
@@ -798,62 +861,120 @@
     )(*args)
 
 
-def widen_kernel(block, down, up, out, query, keyval):
-    b = pl.program_id(0)
+def widen_kernel(
+    summed,
+    rows_in,
+    grad_in,
+    sums,
+    down,
+    up,
+    out,
+    query,
+    keyval,
+    rows_out,
+    grad_out,
+    grad_bias_up,
+    grad_bias_down,
+    grad_gain_mlp,
+    grad_shift_mlp,
+    grad_gain_attn,
+    grad_shift_attn,
+    narrow,
+    wide,
+    rows_held,
+    grad_held,
+    in_sem,
+    out_sem,
+    pass_sem,
+):
     blocks = FF // D
-
-    def store_rows():
-        down[...] = block[...].astype(F32)
-
-    def store_columns():
-        up[...] = block[...].astype(F32)
-
-    def store_pair():
-        out[...] = block[:PAIR, :].astype(F32)
-        query[...] = block[PAIR : 2 * PAIR, :].astype(F32).T
-        keyval[...] = block[2 * PAIR : 3 * PAIR, :].astype(F32).T
-
-    def store_values():
-        keyval[...] = block[3 * PAIR :, :].astype(F32).T
-
-    early = b < 2 * blocks
-    pl.when(jnp.logical_and(early, lax.rem(b, 2) == 0))(store_rows)
-    pl.when(jnp.logical_and(early, lax.rem(b, 2) == 1))(store_columns)
-    pl.when(jnp.logical_and(b >= 2 * blocks, b < 2 * blocks + PAIRS))(store_pair)
-    pl.when(b >= 2 * blocks + PAIRS)(store_values)
-
-
-def widen(summed):
-    blocks = FF // D
-    late = 2 * blocks + PAIRS
+    passes_in = [
+        pltpu.make_async_copy(rows_in, rows_held, pass_sem.at[0]),
+        pltpu.make_async_copy(grad_in, grad_held, pass_sem.at[1]),
+    ]
+    passes_out = [
+        pltpu.make_async_copy(rows_held, rows_out, pass_sem.at[2]),
+        pltpu.make_async_copy(grad_held, grad_out, pass_sem.at[3]),
+    ]
+    count = 2 * blocks + PAIRS
+    loads = [
+        pltpu.make_async_copy(summed.at[pl.ds(b * D, D), :], narrow.at[b], in_sem.at[b])
+        for b in range(count)
+    ]
+    for copy in passes_in + loads:
+        copy.start()
+    for c in range(blocks):
+        grad_bias_up[c * D : (c + 1) * D] = sums[c : c + 1, :].reshape(D)
+    rest = (grad_bias_down, grad_gain_mlp, grad_shift_mlp, grad_gain_attn, grad_shift_attn)
+    for n, target in enumerate(rest):
+        target[...] = sums[blocks + n : blocks + n + 1, :].reshape(D)
+    for copy in passes_in:
+        copy.wait()
+    for copy in passes_out:
+        copy.start()
+    stores = []
+
+    def store(b, source, target):
+        stores.append(pltpu.make_async_copy(source, target, out_sem.at[len(stores)]))
+        stores[-1].start()
+
+    for b in range(count):
+        loads[b].wait()
+        c = b // 2
+        if b < 2 * blocks:
+            wide[b] = narrow[b].astype(F32)
+            at = pl.ds(c * D, D)
+            store(b, wide.at[b], down.at[at, :] if b % 2 == 0 else up.at[:, at])
+        else:
+            i = b - 2 * blocks
+            p = PAIRS - 1 - i
+            wide[b, :PAIR, :] = narrow[b, :PAIR, :].astype(F32)
+            store(b, wide.at[b, pl.ds(0, PAIR), :], out.at[pl.ds(i * PAIR, PAIR), :])
+            base = 2 * blocks + PAIRS
+            for n, (target, column) in enumerate(((query, p), (keyval, p), (keyval, PAIRS + p))):
+                piece = narrow[b, (n + 1) * PAIR : (n + 2) * PAIR, :].astype(F32).T
+                columns = slice(p * PAIR, (p + 1) * PAIR)
+                wide[base + n, :, columns] = piece
+                store(
+                    b,
+                    wide.at[base + n, :, pl.ds(p * PAIR, PAIR)],
+                    target.at[:, pl.ds(column * PAIR, PAIR)],
+                )
+    for copy in stores + passes_out:
+        copy.wait()
+
+
+def widen(summed, rows, grad, sums):
+    blocks = 2 * FF // D + PAIRS
     shape = jax.ShapeDtypeStruct
-
-    def pair(b):
-        return PAIRS - 1 - jnp.clip(b - 2 * blocks, 0, PAIRS - 1)
-
-    def keyval_column(b):
-        return jnp.where(b < late, pair(b), 2 * PAIRS - 1 - (b - late))
-
+    dma = pltpu.SemaphoreType.DMA
     return pl.pallas_call(
         widen_kernel,
-        grid=(late + PAIRS,),
         out_shape=(
             shape((FF, D), F32),
             shape((D, FF), F32),
             shape((D, D), F32),
             shape((D, D), F32),
             shape((D, 2 * D), F32),
-        ),
-        in_specs=[pl.BlockSpec((D, D), lambda b: (jnp.where(b < late, b, b - PAIRS), 0))],
-        out_specs=[
-            pl.BlockSpec((D, D), lambda b: (jnp.clip(b // 2, 0, blocks - 1), 0)),
-            pl.BlockSpec((D, D), lambda b: (0, jnp.clip(b // 2, 0, blocks - 1))),
-            pl.BlockSpec((PAIR, D), lambda b: (jnp.clip(b - 2 * blocks, 0, PAIRS - 1), 0)),
-            pl.BlockSpec((D, PAIR), lambda b: (0, pair(b))),
-            pl.BlockSpec((D, PAIR), lambda b: (0, keyval_column(b))),
+            shape(rows.shape, rows.dtype),
+            shape(grad.shape, grad.dtype),
+            shape((FF,), F32),
+        )
+        + (shape((D,), F32),) * 5,
+        in_specs=[ANYWHERE] * 3 + [IN_VMEM],
+        out_specs=[ANYWHERE] * 7 + [IN_VMEM] * 6,
+        scratch_shapes=[
+            VMEM((blocks, D, D), BF16),
+            VMEM((blocks + 3, D, D), F32),
+            VMEM(rows.shape, rows.dtype),
+            VMEM(grad.shape, grad.dtype),
+            dma((blocks,)),
+            dma((blocks + 3 * PAIRS,)),
+            dma((4,)),
         ],
+        compiler_params=pltpu.CompilerParams(vmem_limit_bytes=60 * MIB),
         name="widen",
-    )(summed)
+    )(summed, rows, grad, sums)
 
 
 def on_device(
@@ -877,32 +998,31 @@
     shift_mlp,
     cotangent,
 ):
-    rows = tokens.reshape(ROWS, D)
-    item = slot_item.reshape(())
-    filled = (counts.reshape(()) > 0) & (keyframe.reshape(()) == 1) & (item >= 0)
-    label = jnp.where(filled, item, -1).astype(BF16)
-    block = jnp.concatenate([rows[:USED], jnp.broadcast_to(label, (SENT - USED, D))])
-    window = gather_window(block, count)
-    vectors = jnp.concatenate(
-        [bias_up, bias_down, gain_attn, shift_attn, gain_mlp, shift_mlp, jnp.zeros((7 * D,), BF16)]
-    )
-    vectors = vectors.astype(F32).reshape(SUMS, D)
     block_output, grad_tokens, summed, sums, _ = main(
         count,
         groups,
+        counts.reshape(1),
+        slot_item.reshape(1),
         slot_view.reshape(1),
-        filled.astype(jnp.int32).reshape(1),
-        window,
-        rows,
+        keyframe.reshape(1),
+        tokens.reshape(ROWS, D),
         cotangent.reshape(ROWS, D),
         w_query,
         w_keyval,
         w_output,
+        bias_up,
+        bias_down,
+        gain_attn,
+        shift_attn,
+        gain_mlp,
+        shift_mlp,
         w_up,
         w_down,
-        vectors,
     )
-    down, up, out, query, keyval = widen(summed)
+    down, up, out, query, keyval, block_output, grad_tokens, *small = widen(
+        summed, block_output, grad_tokens, sums
+    )
+    grad_bias_up, grad_bias_down, gain_mlp, shift_mlp, gain_attn, shift_attn = small
     return (
         block_output.reshape(tokens.shape),
         grad_tokens.reshape(tokens.shape),
@@ -910,13 +1030,13 @@
         keyval,
         out,
         up,
-        sums[:4].reshape(-1),
+        grad_bias_up,
         down,
-        sums[4],
-        sums[7],
-        sums[8],
-        sums[5],
-        sums[6],
+        grad_bias_down,
+        gain_attn,
+        shift_attn,
+        gain_mlp,
+        shift_mlp,
     )
 
 

time: 229 us -> 178 us (0.78)
  Pallas kernels: 212 us -> 174 us
  local copies, waits for them, and re-layouts: 12.4 us -> 0 us
    pallas_call x2 -> x1, Pallas kernels: 57.6 us -> 9.86 us  [widen(): pl.pallas_call(widen_kernel, out_shape=(shape((FF, D), F32), shape((D, FF...]
    pallas_call x1, Pallas kernels: 155 us -> 164 us  [main(): pl.pallas_call(functools.partial(main_kernel, count, groups, chunks, part...]
    unnamed x14 -> x0, local copies, waits for them, and re-layouts: 8.18 us -> none
    slice x2 -> x0, local copies, waits for them, and re-layouts: 2.52 us -> none  [the longest x1 1.46 us: on_device(): sums[6]]
where the time goes in v4:
time: 178 us
  Pallas kernels  174 us (98%)
  between operations  3.44 us (2%)
    pallas_call x1, Pallas kernels, main(): pl.pallas_call(functools.partial(main_kernel, count, groups, chunks, part...  164 us
    pallas_call x1, Pallas kernels, widen(): pl.pallas_call(widen_kernel, out_shape=(shape((FF, D), F32), shape((D, FF...  9.86 us

profile of v4, /device:TPU:0, one launch (start us, length us, event | category | flops | bytes accessed | tf_op | source)
XLA Modules:
  0.0 177.5 jit_solution(8695162606560765784)
XLA Ops:
  3.2 164.2 %main.1 = (bf16[512,512]{1,0:T(8,128)(2,1)}, f32[512,512]{1,0:T(8,128)}, bf16[6144,512]{1,0:T(8,128)(2,1)}, f32[16,512]{1,0:T(8,128)}, bf16[4,480,2176]{2,1,0:T(8,128)(2,1)}) custom-call(s32[1]{0:T(128)} %bitcast.8.counts, s32[1]{0:T(128)} %bitcast.9.slot_item, s32[1]{0:T(128)} %bitcast.10.slot_view, s32[1]{0:T(128)} %bitcast.11.keyframe, ...), custom_call_target="tpu_custom_call" | custom-call | tf_op jit(solution)/shard_map/main/pallas_call | solution.py:845
  167.5 9.9 %widen.1 = (f32[2048,512]{1,0:T(8,128)}, f32[512,2048]{1,0:T(8,128)}, f32[512,512]{1,0:T(8,128)}, f32[512,512]{1,0:T(8,128)}, f32[512,1024]{1,0:T(8,128)}, /*ind...) custom-call(bf16[6144,512]{1,0:T(8,128)(2,1)} %get-tuple-element.30., ...), custom_call_target="tpu_custom_call" | custom-call | tf_op jit(solution)/shard_map/widen/pallas_call | solution.py:951

commit v5 on v4

--- a/solution.py
+++ b/solution.py
@@ -31,6 +31,7 @@
 STAGES = 8
 SKEW = 2
 IN_FLIGHT = 4
+BESIDE = 1
 PIECES = ((0, 128), (128, 128), (256, 128), (384, 112))
 
 BF16 = jnp.bfloat16
@@ -344,11 +345,11 @@
         for stage in range(STAGES, -1, -1):
             at = t - SKEW * stage
             if fine:
-                late = at - (2 * blocks + 1)
+                late = at - (2 * blocks + 2 * BESIDE - 1)
                 early = jnp.logical_and(at >= 0, at < 2 * blocks)
-                valid = jnp.logical_and(late >= 0, late < 2 * PAIRS)
-                valid = jnp.logical_or(early, jnp.logical_and(valid, lax.rem(late, 2) == 0))
-                k = jnp.where(early, at, 2 * blocks + late // 2)
+                valid = jnp.logical_and(late >= 0, late < 2 * BESIDE * PAIRS)
+                valid = jnp.logical_or(early, jnp.logical_and(valid, lax.rem(late, 2 * BESIDE) == 0))
+                k = jnp.where(early, at, 2 * blocks + late // (2 * BESIDE))
             else:
                 k = at
                 valid = jnp.logical_and(at >= 0, at < chunks)
@@ -360,6 +361,13 @@
                     start_stage(stage, k)
 
             pl.when(valid)(go)
+
+    def run_ticks(first, end):
+        def body(t, _):
+            tick(t)
+            return 0
+
+        lax.fori_loop(first, end, body, 0)
 
     sums_dims = ("core", "x", "y", "z")
 
@@ -508,11 +516,13 @@
                 spill(p - 1, half).wait()
 
         pl.when(jnp.logical_and(p >= 1, p < 3))(settle)
+        scores = []
         for half in range(2):
             one = (lane == HEAD_DIM * (1 - half)).astype(BF16)
-            scores = dot(half_of(half, pair, one), head_keys(p, half), NT)
-            top = jnp.max(scores, -1, keepdims=True)
-            weight = jnp.exp(scores - top).astype(BF16)
+            scores.append(dot(half_of(half, pair, one), head_keys(p, half), NT))
+        for half in range(2):
+            top = jnp.max(scores[half], -1, keepdims=True)
+            weight = jnp.exp(scores[half] - top).astype(BF16)
             weights[2 * lax.rem(p, 2) + half, :USED, :] = weight
             out = dot(weight, head_values(p, half), NN)
             outs.append(out)
@@ -558,13 +568,14 @@
         start = pl.multiple_of(2 * c * D, D)
         grads[pl.ds(start, D), :] = dot(activated, branch_grad[...], TN).astype(BF16)
         branch[...] += dot(activated, down, NN)
+        if fine:
+            tick(2 * c)
         before_full = dot(branch_grad[...], down, NT) * slope
         before_grad = before_full.astype(BF16)
         sums_out[pl.ds(c, 1), :] = jnp.sum(before_grad.astype(F32), 0, keepdims=True)
         grads[pl.ds(start + D, D), :] = dot(normed_mlp[...], before_grad, TN).astype(BF16)
         mlp_back[...] += dot(before_grad, up, NT)
         if fine:
-            tick(2 * c)
             tick(2 * c + 1)
         return 0
 
@@ -624,7 +635,7 @@
             keyval_grad[pl.ds(at, HEAD_DIM), :] = dot(query_t[rows, :], score_grad, NN).astype(BF16)
             keyval_grad[pl.ds(D + at, HEAD_DIM), :] = dot(scaled_t[rows, :], weight, NN).astype(BF16)
             if fine and half == 0:
-                tick(2 * blocks + 2 * i)
+                run_ticks(2 * blocks + 2 * BESIDE * i, 2 * blocks + 2 * BESIDE * i + BESIDE)
 
         def load():
             for half in range(2):
@@ -642,7 +653,7 @@
             )
         branch[...] += dot(query_grad, w_query[:, columns], NT)
         if fine:
-            tick(2 * blocks + 2 * i + 1)
+            run_ticks(2 * blocks + 2 * BESIDE * i + BESIDE, 2 * blocks + 2 * BESIDE * (i + 1))
         return 0
 
     lax.fori_loop(0, PAIRS, backward_pair, 0)
@@ -719,32 +730,27 @@
     def back_down(q):
         return back(3, 0, 3, -4 * turn, q)
 
-    ticks = 2 * blocks + 2 * PAIRS if fine else 0
+    ticks = 2 * blocks + 2 * BESIDE * PAIRS if fine else 0
     last = ticks + STAGES * SKEW if fine else chunks + STAGES * SKEW
-
-    def run_ticks(first, end):
-        def body(t, _):
-            tick(t)
-            return 0
-
-        lax.fori_loop(first, end, body, 0)
 
     if not fine:
         run_ticks(0, SKEW + 1)
         ticks = SKEW + 1
     sums_start(0, sums_out[...])
-    for n, offset in enumerate((step, step - 2 * turn, step + 2 * turn, -3 * step)):
+    offsets = (step, step - 2 * turn, step + 2 * turn, -3 * step)
+    for n, offset in ((1, offsets[1]), (3, offsets[3]), (2, offsets[2]), (0, offsets[0])):
         arena[n, :USED, :] = part_for(offset)
         swap(n).start()
-    run_ticks(ticks, ticks + 1)
+    pieces = range(len(back_pieces))
+    run_ticks(ticks + 0, ticks + 6)
     sums_start(1, sums_finish(0))
-    pieces = range(len(back_pieces))
-    for n, offset in ((1, -2 * turn), (2, 2 * turn)):
-        swap(n).wait()
-        both = part_for(offset).astype(F32) + arena[4 + n, :USED, :].astype(F32)
-        arena[n, :USED, :] = both.astype(BF16)
-        for q in pieces:
-            (back_relay if n == 1 else back_x)(q).start()
+    swap(1).wait()
+    both = part_for(-2 * turn).astype(F32) + arena[5, :USED, :].astype(F32)
+    arena[1, :USED, :] = both.astype(BF16)
+    for q in pieces:
+        back_relay(q).start()
+    run_ticks(ticks + 6, ticks + 8)
+    sums_start(2, sums_finish(1))
     swap(0).wait()
     swap(3).wait()
     shared = arena[7, :USED, :].astype(F32)
@@ -756,18 +762,31 @@
     arena[3, :USED, :] = (
         part_for(4 * turn).astype(F32) + jnp.where(step == turn, shared, 0.0)
     ).astype(BF16)
+    at = slice(0, 160)
+    back_relay(0).wait_recv()
+    both = arena[3, at, :].astype(F32) + far_in[0, at, :].astype(F32)
+    arena[3, at, :] = both.astype(BF16)
+    back_up(0).start()
+    run_ticks(ticks + 8, ticks + 9)
+    at = slice(160, 320)
+    back_relay(1).wait_recv()
+    both = arena[3, at, :].astype(F32) + far_in[0, at, :].astype(F32)
+    arena[3, at, :] = both.astype(BF16)
+    back_up(1).start()
+    run_ticks(ticks + 9, ticks + 10)
+    at = slice(320, 480)
+    back_relay(2).wait_recv()
+    both = arena[3, at, :].astype(F32) + far_in[0, at, :].astype(F32)
+    arena[3, at, :] = both.astype(BF16)
+    back_up(2).start()
+    sums_start(3, sums_finish(2))
+    run_ticks(ticks + 10, ticks + 12)
+    swap(2).wait()
+    both = part_for(2 * turn).astype(F32) + arena[6, :USED, :].astype(F32)
+    arena[2, :USED, :] = both.astype(BF16)
     for q in pieces:
-        first, rows = back_pieces[q]
-        at = slice(first, first + rows)
-        back_relay(q).wait_recv()
-        both = arena[3, at, :].astype(F32) + far_in[0, at, :].astype(F32)
-        arena[3, at, :] = both.astype(BF16)
-        back_up(q).start()
-    run_ticks(ticks + 1, ticks + 2)
-    sums_start(2, sums_finish(1))
-    run_ticks(ticks + 2, ticks + 4)
-    sums_start(3, sums_finish(2))
-    run_ticks(ticks + 4, last)
+        back_x(q).start()
+    run_ticks(ticks + 12, last)
     sums_out[...] = sums_finish(3)
     total = branch[...] + arena[4, :USED, :].astype(F32)
     for q in pieces:

time: 178 us -> 161 us (0.904)
  Pallas kernels: 174 us -> 158 us
    pallas_call x1, Pallas kernels: 164 us -> 148 us  [main(): pl.pallas_call(functools.partial(main_kernel, count, groups, chunks, part...]
where the time goes in v5:
time: 161 us
  Pallas kernels  158 us (98%)
  between operations  3.42 us (2%)
    pallas_call x1, Pallas kernels, main(): pl.pallas_call(functools.partial(main_kernel, count, groups, chunks, part...  148 us
    pallas_call x1, Pallas kernels, widen(): pl.pallas_call(widen_kernel, out_shape=(shape((FF, D), F32), shape((D, FF...  9.86 us

profile of v5, /device:TPU:0, one launch (start us, length us, event | category | flops | bytes accessed | tf_op | source)
XLA Modules:
  0.0 161.2 jit_solution(3203250463873043635)
XLA Ops:
  3.2 147.9 %main.1 = (bf16[512,512]{1,0:T(8,128)(2,1)}, f32[512,512]{1,0:T(8,128)}, bf16[6144,512]{1,0:T(8,128)(2,1)}, f32[16,512]{1,0:T(8,128)}, bf16[4,480,2176]{2,1,0:T(8,128)(2,1)}) custom-call(s32[1]{0:T(128)} %bitcast.8.counts, s32[1]{0:T(128)} %bitcast.9.slot_item, s32[1]{0:T(128)} %bitcast.10.slot_view, s32[1]{0:T(128)} %bitcast.11.keyframe, ...), custom_call_target="tpu_custom_call" | custom-call | tf_op jit(solution)/shard_map/main/pallas_call | solution.py:864
  151.2 9.9 %widen.1 = (f32[2048,512]{1,0:T(8,128)}, f32[512,2048]{1,0:T(8,128)}, f32[512,512]{1,0:T(8,128)}, f32[512,512]{1,0:T(8,128)}, f32[512,1024]{1,0:T(8,128)}, /*ind...) custom-call(bf16[6144,512]{1,0:T(8,128)(2,1)} %get-tuple-element.30., ...), custom_call_target="tpu_custom_call" | custom-call | tf_op jit(solution)/shard_map/widen/pallas_call | solution.py:970

commit v6 on v5

--- a/solution.py
+++ b/solution.py
@@ -31,8 +31,10 @@
 STAGES = 8
 SKEW = 2
 IN_FLIGHT = 4
-BESIDE = 1
-PIECES = ((0, 128), (128, 128), (256, 128), (384, 112))
+LQ = 1
+READY = (10, 12, 16)
+PIECES = ((0, 128), (128, 144), (272, 144))
+MAIN = SENT - TAIL
 
 BF16 = jnp.bfloat16
 F32 = jnp.float32
@@ -85,10 +87,8 @@
     slot_view,
     keyframe,
     tokens,
-    cotangent,
     w_query,
     w_keyval,
-    w_output,
     bias_up,
     bias_down,
     gain_attn,
@@ -97,11 +97,12 @@
     shift_mlp,
     w_up,
     w_down,
+    cotangent_in,
+    w_output_in,
     block_output,
     grad_tokens,
     summed,
     sums_out,
-    spilled,
     normed_all,
     query_norm,
     key_bias,
@@ -112,10 +113,7 @@
     mixed_full,
     inverse,
     keyval_grad,
-    mixed_grad,
-    normed_mlp,
     branch_grad,
-    residual,
     branch,
     mlp_back,
     sent,
@@ -131,7 +129,6 @@
     there_sem,
     here_sem,
     weight_sem,
-    spill_sem,
     send_sem,
     recv_sem,
     local_sem,
@@ -182,8 +179,13 @@
                 w_down.at[pl.ds(c * D, D), :], arena.at[blocks + c], weight_sem.at[blocks + c]
             )
             for c in range(blocks)
+        ] + [
+            pltpu.make_async_copy(cotangent_in, cotangent, weight_sem.at[2 * blocks]),
+            pltpu.make_async_copy(w_output_in, w_output, weight_sem.at[2 * blocks + 1]),
         ]
 
+    cotangent = keyval_grad.at[pl.ds(0, ROWS), pl.ds(0, D)]
+    w_output = keyval_grad.at[pl.ds(0, D), pl.ds(D, D)]
     for copy in weight_copies():
         copy.start()
     my_view = slot_view[0]
@@ -209,36 +211,52 @@
             MESH,
         )
 
+    pieces_all = PIECES + ((MAIN, TAIL),)
+    tail = len(PIECES)
+
     def piece_kind(line, q):
-        return line * len(PIECES) + q
+        return line * len(pieces_all) + q
 
     def along_z(line, q):
-        first, rows = PIECES[q]
+        first, rows = pieces_all[q]
         ahead = 4 - 8 * line
         source = sent.at[pl.ds(first, rows), :]
         return hop(piece_kind(line, q), source, -ahead, first, rows, along(ahead))
 
     def relay_x(q):
-        first, rows = PIECES[q]
+        first, rows = pieces_all[q]
         source = window_at(4 * turn, first, rows)
         return hop(piece_kind(2, q), source, 2 * turn, first, rows, along(2 * turn))
 
     def across_relayed(q):
-        first, rows = PIECES[q]
+        first, rows = pieces_all[q]
         source = window_at(-2 * turn, first, rows)
         return hop(piece_kind(3, q), source, -2 * turn - step, first, rows, sibling)
 
-    last_kind = 4 * len(PIECES)
-    direct_x = hop(last_kind, sent, -2 * turn, 0, SENT, along(2 * turn))
-    across_own = hop(last_kind + 1, sent, -step, 0, SENT, sibling)
-    across_x = hop(
-        last_kind + 2, window_at(2 * turn, 0, SENT), 2 * turn - step, 0, SENT, sibling
-    )
-    across_z = hop(last_kind + 3, window_at(4 * step, 0, SENT), 3 * step, 0, SENT, sibling)
-    for q in range(len(PIECES)):
+    def direct_x(lang):
+        first, rows = (MAIN, TAIL) if lang else (0, MAIN)
+        source = sent.at[pl.ds(first, rows), :]
+        return hop(piece_kind(4, lang), source, -2 * turn, first, rows, along(2 * turn))
+
+    def across_x(lang):
+        first, rows = (MAIN, TAIL) if lang else (0, MAIN)
+        source = window_at(2 * turn, first, rows)
+        return hop(piece_kind(4, 2 + lang), source, 2 * turn - step, first, rows, sibling)
+
+    def across_z(lang):
+        first, rows = (MAIN, TAIL) if lang else (0, MAIN)
+        source = window_at(4 * step, first, rows)
+        return hop(piece_kind(5, lang), source, 3 * step, first, rows, sibling)
+
+    across_own = hop(piece_kind(5, 2), sent, -step, 0, SENT, sibling)
+    forth = turn > 0
+    back_turn = turn < 0
+    for q in range(tail):
         for line in range(2):
             along_z(line, q).start()
-    direct_x.start()
+    along_z(0, tail).start()
+    direct_x(0).start()
+    pl.when(forth)(lambda: direct_x(1).start())
     across_own.start()
 
     levels = []
@@ -345,11 +363,13 @@
         for stage in range(STAGES, -1, -1):
             at = t - SKEW * stage
             if fine:
-                late = at - (2 * blocks + 2 * BESIDE - 1)
-                early = jnp.logical_and(at >= 0, at < 2 * blocks)
-                valid = jnp.logical_and(late >= 0, late < 2 * BESIDE * PAIRS)
-                valid = jnp.logical_or(early, jnp.logical_and(valid, lax.rem(late, 2 * BESIDE) == 0))
-                k = jnp.where(early, at, 2 * blocks + late // (2 * BESIDE))
+                early = jnp.logical_and(at >= 0, at <= 2 * blocks)
+                valid = early
+                k = at
+                for n, ready in enumerate(READY):
+                    now = at == ready
+                    valid = jnp.logical_or(valid, now)
+                    k = jnp.where(now, 2 * blocks + 1 + n, k)
             else:
                 k = at
                 valid = jnp.logical_and(at >= 0, at < chunks)
@@ -424,26 +444,60 @@
     query_norm[...] = (own_unit * gain_a + shift_a).astype(BF16)
     query[...] = (dot(query_norm[...], w_query[...], NN).astype(BF16) * HEAD_DIM**-0.5).astype(BF16)
     project_keys(0, PATCHES, own_rows[:PATCHES, :])
-    relayed = jnp.where(turn > 0, 1, 0)
-    for q in range(len(PIECES)):
+    relayed = jnp.where(forth, 1, 0)
+    for q in range(tail):
         along_z(relayed, q).wait_recv()
         relay_x(q).start()
-    direct_x.wait_recv()
-    across_x.start()
-    for q in range(len(PIECES)):
+
+    def relay_tail():
+        along_z(0, tail).wait_recv()
+        relay_x(tail).start()
+
+    pl.when(back_turn)(relay_tail)
+    direct_x(0).wait_recv()
+    across_x(0).start()
+
+    def pass_tail_x():
+        direct_x(1).wait_recv()
+        across_x(1).start()
+
+    pl.when(back_turn)(pass_tail_x)
+    for q in range(tail):
         along_z(1 - relayed, q).wait_recv()
-    across_z.start()
-    for q in range(len(PIECES)):
+    pl.when(forth)(lambda: along_z(0, tail).wait_recv())
+    across_z(0).start()
+    pl.when(step < 0)(lambda: across_z(1).start())
+    for q in range(tail):
         relay_x(q).wait_recv()
         across_relayed(q).start()
-    for copy in (across_own, across_x, across_z):
+
+    def pass_tail_relayed():
+        relay_x(tail).wait_recv()
+        across_relayed(tail).start()
+
+    pl.when(forth)(pass_tail_relayed)
+    for copy in (across_own, across_x(0), across_z(0)):
         copy.wait()
-    direct_x.wait_send()
-    for q in range(len(PIECES)):
+    direct_x(0).wait_send()
+    for q in range(tail):
         for line in range(2):
             along_z(line, q).wait_send()
         relay_x(q).wait_send()
         across_relayed(q).wait()
+    along_z(0, tail).wait_send()
+
+    def settle_forth():
+        direct_x(1).wait_send()
+        across_relayed(tail).wait()
+
+    def settle_back():
+        relay_x(tail).wait_send()
+        across_x(1).wait()
+
+    pl.when(forth)(settle_forth)
+    pl.when(back_turn)(settle_back)
+    pl.when(step < 0)(lambda: across_z(1).wait_send())
+    pl.when(step > 0)(lambda: across_z(1).wait_recv())
     my_label = sent[: SENT - USED, :PAIR].astype(F32)
 
     def bias_of(label):
@@ -470,7 +524,7 @@
         bias = bias_of(either(0, top_rows, PAIR).astype(F32))
         rows = slice(j * PATCHES, (j + 1) * PATCHES)
         key_bias[rows, :] = jnp.broadcast_to(bias, (PATCHES, PAIR)).astype(BF16)
-        language = jnp.where(holds, either(top_rows + PATCHES, TAIL), language)
+        language = jnp.where(holds, block_at(j - 1, top_rows + PATCHES, TAIL), language)
         language_bias = jnp.where(holds, bias, language_bias)
     project_keys(VIEWS * PATCHES, TAIL, language)
     index = lax.broadcasted_iota(jnp.int32, (TAIL, PAIR), 0)
@@ -495,27 +549,12 @@
         pair = keyval[:, pl.ds(pl.multiple_of(D + p * PAIR, PAIR), PAIR)]
         return half_of(half, pair, jnp.ones((), BF16))
 
-    def spill(p, half):
-        return pltpu.make_async_copy(
-            weights.at[2 * lax.rem(p, 2) + half, pl.ds(0, USED), :], spilled.at[2 * p + half], spill_sem.at[lax.rem(p, 2), half]
-        )
-
-    def unspill(p, half):
-        return pltpu.make_async_copy(
-            spilled.at[2 * p + half], weights.at[2 * lax.rem(p, 2) + half, pl.ds(0, USED), :], spill_sem.at[lax.rem(p, 2), half]
-        )
-
     def forward_pair(p, _):
         columns = pl.ds(pl.multiple_of(p * PAIR, PAIR), PAIR)
         pair = query[:, columns]
         outs = []
         totals = []
 
-        def settle():
-            for half in range(2):
-                spill(p - 1, half).wait()
-
-        pl.when(jnp.logical_and(p >= 1, p < 3))(settle)
         scores = []
         for half in range(2):
             one = (lane == HEAD_DIM * (1 - half)).astype(BF16)
@@ -523,7 +562,7 @@
         for half in range(2):
             top = jnp.max(scores[half], -1, keepdims=True)
             weight = jnp.exp(scores[half] - top).astype(BF16)
-            weights[2 * lax.rem(p, 2) + half, :USED, :] = weight
+            weights[2 * p + half, :USED, :] = weight
             out = dot(weight, head_values(p, half), NN)
             outs.append(out)
             totals.append(pltpu.roll(out, HEAD_DIM, 1))
@@ -533,29 +572,25 @@
         mixed_full[:, columns] = full
         mixed[:, columns] = full.astype(BF16)
 
-        def save():
-            for half in range(2):
-                spill(p, half).start()
-
-        pl.when(p < 2)(save)
         return 0
 
     lax.fori_loop(0, PAIRS, forward_pair, 0)
 
+    for copy in weight_copies():
+        copy.wait()
     row = lax.broadcasted_iota(jnp.int32, (USED, PAIR), 0)
     has_language = (my_view == 0).astype(jnp.int32)
     live_rows = my_filled * (PATCHES + LANG * has_language)
     live = (row < live_rows).astype(F32)[:, :1]
     res = tokens[:USED, :].astype(F32) + live * dot(mixed[...], w_output[...], NN)
-    residual[...] = res
+    grad_tokens[:USED, :] = res
     unit_m, scale_m = normalise(res)
+    normed_mlp = sent.at[:USED, :]
     normed_mlp[...] = (unit_m * gain_m + shift_m).astype(BF16)
     upstream = cotangent[:USED, :].astype(F32)
     branch_grad[...] = (live * upstream).astype(BF16)
     branch[...] = jnp.zeros((USED, D), F32)
     mlp_back[...] = jnp.zeros((USED, D), F32)
-    for copy in weight_copies():
-        copy.wait()
 
     def feed_forward(c, _):
         up = arena[c]
@@ -580,9 +615,11 @@
         return 0
 
     lax.fori_loop(0, blocks, feed_forward, 0)
-    block_output[:USED, :] = (residual[...] + live * (branch[...] + vectors[4:5, :])).astype(BF16)
-    block_output[USED:, :] = tokens[USED:, :]
-    unit_m, scale_m = normalise(residual[...])
+    arena[0, :USED, :] = (grad_tokens[:USED, :] + live * (branch[...] + vectors[4:5, :])).astype(BF16)
+    arena[0, USED:, :] = tokens[USED:, :]
+    output_copy = pltpu.make_async_copy(arena.at[0], block_output, weight_sem.at[0])
+    output_copy.start()
+    unit_m, scale_m = normalise(grad_tokens[:USED, :])
     back = mlp_back[...]
     sums_out[4:5, :] = jnp.sum(branch_grad[...].astype(F32), 0, keepdims=True)
     sums_out[5:6, :] = jnp.sum(back * unit_m, 0, keepdims=True)
@@ -592,31 +629,23 @@
     grad_tokens[USED:, :] = cotangent[USED:, :].astype(F32)
     attended_grad = (live * res_grad).astype(BF16)
     base = 2 * FF
-    out_grad = dot(mixed[...], attended_grad, TN).astype(BF16)
-    for i in range(PAIRS):
-        grads[base + i * D : base + i * D + PAIR, :] = out_grad[i * PAIR : (i + 1) * PAIR, :]
+    grads[base : base + D, :] = dot(mixed[...], attended_grad, TN).astype(BF16)
+    mixed_grad = branch_grad
     mixed_grad[...] = dot(attended_grad, w_output[...], NT).astype(BF16)
 
     branch[...] = jnp.zeros((USED, D), F32)
-
-    def backward_pair(i, _):
-        p = PAIRS - 1 - i
+    if fine:
+        tick(2 * blocks)
+
+    def backward_pair(p, _):
         columns = pl.ds(pl.multiple_of(p * PAIR, PAIR), PAIR)
         grad = mixed_grad[:, columns].astype(F32)
-        inv = inverse[:, columns]
-        scaled = grad * inv
+        scaled = grad * inverse[:, columns]
         product = scaled * mixed_full[:, columns]
         scaled_low = scaled.astype(BF16)
         scaled_t = scaled.T.astype(BF16)
         query_t = query[:, columns].astype(F32).T.astype(BF16)
-        query_parts = []
         start = pl.multiple_of(p * PAIR, PAIR)
-
-        def settle():
-            for half in range(2):
-                unspill(p, half).wait()
-
-        pl.when(p < 2)(settle)
         for half in range(2):
             here = low_half if half == 0 else jnp.logical_not(low_half)
             dots = -jnp.sum(jnp.where(here, product, 0.0), -1, keepdims=True)
@@ -626,45 +655,43 @@
             rest = jnp.where(
                 lane == other, dots_high, jnp.where(lane == other + 1, dots_low, jnp.zeros((), BF16))
             )
-            weight = weights[2 * lax.rem(p, 2) + half, :USED, :]
+            weight = weights[2 * p + half, :USED, :]
             slope = dot(half_of(half, scaled_low, rest), head_values(p, half), NT)
             score_grad = weight * slope.astype(BF16)
-            query_parts.append(dot(score_grad, head_keys(p, half), NN))
+            weights[2 * p + half, :USED, :] = score_grad
             rows = slice(half * HEAD_DIM, (half + 1) * HEAD_DIM)
             at = start + half * HEAD_DIM
             keyval_grad[pl.ds(at, HEAD_DIM), :] = dot(query_t[rows, :], score_grad, NN).astype(BF16)
             keyval_grad[pl.ds(D + at, HEAD_DIM), :] = dot(scaled_t[rows, :], weight, NN).astype(BF16)
-            if fine and half == 0:
-                run_ticks(2 * blocks + 2 * BESIDE * i, 2 * blocks + 2 * BESIDE * i + BESIDE)
-
-        def load():
-            for half in range(2):
-                unspill(p - 2, half).start()
-
-        pl.when(p >= 2)(load)
+        at = pl.multiple_of(base + D + 2 * PAIR * p, 2 * PAIR)
+        for c in range(2):
+            of_pair = keyval_grad[pl.ds(c * D + start, PAIR), :]
+            grads[pl.ds(at + c * PAIR, PAIR), :] = dot(of_pair, normed_all[...], NN).astype(BF16)
+        if fine:
+            tick(2 * blocks + 1 + p)
+        return 0
+
+    lax.fori_loop(0, PAIRS, backward_pair, 0)
+
+    def query_pair(p, _):
+        columns = pl.ds(pl.multiple_of(p * PAIR, PAIR), PAIR)
+        query_parts = [
+            dot(weights[2 * p + half, :USED, :], head_keys(p, half), NN) for half in range(2)
+        ]
         part = jnp.where(low_half, query_parts[0], query_parts[1]) * HEAD_DIM**-0.5
         query_grad = part.astype(BF16)
-        at = pl.multiple_of(base + i * D, D)
-        grads[pl.ds(at + PAIR, PAIR), :] = dot(query_grad, query_norm[...], TN).astype(BF16)
-        for c in range(2):
-            of_pair = keyval_grad[pl.ds(c * D + start, PAIR), :]
-            grads[pl.ds(at + (2 + c) * PAIR, PAIR), :] = dot(of_pair, normed_all[...], NN).astype(
-                BF16
-            )
+        at = pl.multiple_of(base + 3 * D + p * PAIR, PAIR)
+        grads[pl.ds(at, PAIR), :] = dot(query_grad, query_norm[...], TN).astype(BF16)
         branch[...] += dot(query_grad, w_query[:, columns], NT)
         if fine:
-            run_ticks(2 * blocks + 2 * BESIDE * i + BESIDE, 2 * blocks + 2 * BESIDE * (i + 1))
+            run_ticks(ticks + LQ * p, ticks + LQ * (p + 1))
         return 0
 
-    lax.fori_loop(0, PAIRS, backward_pair, 0)
-
-    from_query = branch[...]
-    normed = query_norm[...].astype(F32)
-    shift_sum = jnp.sum(from_query, 0, keepdims=True)
-    gain_sum = jnp.sum(from_query * normed, 0, keepdims=True)
+    shift_sum = jnp.zeros((1, D), F32)
+    gain_sum = jnp.zeros((1, D), F32)
 
     def parts_at(j):
-        return weights.at[0, :USED, (j - 1) * D : j * D]
+        return normed_all.at[(j - 1) * USED : j * USED, :]
 
     for j in range(VIEWS + 1):
         rows = slice(j * PATCHES, min((j + 1) * PATCHES, KEYS))
@@ -673,18 +700,14 @@
         shift_sum += jnp.sum(piece, 0, keepdims=True)
         gain_sum += jnp.sum(piece * normed, 0, keepdims=True)
         if j == 0:
-            branch[:PATCHES, :] += piece
+            mlp_back[:PATCHES, :] = piece
         elif j < VIEWS:
             parts_at(j)[:PATCHES, :] = piece.astype(BF16)
         else:
-            branch[PATCHES:, :] += jnp.where(my_view == 0, piece, 0.0)
+            mlp_back[PATCHES:, :] = jnp.where(my_view == 0, piece, 0.0)
             for i in range(1, VIEWS):
                 holds = lax.rem(my_view + i, VIEWS) == 0
                 parts_at(i)[PATCHES:, :] = jnp.where(holds, piece, 0.0).astype(BF16)
-    sums_out[7:8, :] = (gain_sum - shift_a * shift_sum) / gain_a
-    sums_out[8:9, :] = shift_sum
-    sums_out[9:, :] = jnp.zeros((SUMS - 9, D), F32)
-
     def part_for(offset):
         slot = lax.rem(offset + VIEWS, VIEWS) - 1
         at = my_view + offset
@@ -704,7 +727,7 @@
             MESH,
         )
 
-    back_pieces = ((0, 160), (160, 160), (320, 160))
+    back_pieces = ((0, 144), (144, 128), (272, 128), (PATCHES, TAIL))
 
     def back(kind, slot, target, offset, q):
         first, rows = back_pieces[q]
@@ -730,27 +753,41 @@
     def back_down(q):
         return back(3, 0, 3, -4 * turn, q)
 
-    ticks = 2 * blocks + 2 * BESIDE * PAIRS if fine else 0
-    last = ticks + STAGES * SKEW if fine else chunks + STAGES * SKEW
+    ticks = 2 * blocks + 1 + PAIRS if fine else 0
+    last = READY[-1] + STAGES * SKEW + 1 if fine else chunks + STAGES * SKEW
 
     if not fine:
+        lax.fori_loop(0, PAIRS, query_pair, 0)
         run_ticks(0, SKEW + 1)
         ticks = SKEW + 1
-    sums_start(0, sums_out[...])
+    output_copy.wait()
     offsets = (step, step - 2 * turn, step + 2 * turn, -3 * step)
     for n, offset in ((1, offsets[1]), (3, offsets[3]), (2, offsets[2]), (0, offsets[0])):
         arena[n, :USED, :] = part_for(offset)
         swap(n).start()
-    pieces = range(len(back_pieces))
-    run_ticks(ticks + 0, ticks + 6)
+    pieces = range(len(back_pieces) - 1)
+    lang = len(back_pieces) - 1
+    pieces = range(len(back_pieces) - 1)
+    lang = len(back_pieces) - 1
+    if fine:
+        lax.fori_loop(0, 4, query_pair, 0)
+        ticks = ticks + LQ * PAIRS
+    from_query = branch[...]
+    shift_sum += jnp.sum(from_query, 0, keepdims=True)
+    gain_sum += jnp.sum(from_query * query_norm[...].astype(F32), 0, keepdims=True)
+    sums_out[7:8, :] = (gain_sum - shift_a * shift_sum) / gain_a
+    sums_out[8:9, :] = shift_sum
+    sums_out[9:, :] = jnp.zeros((SUMS - 9, D), F32)
+    sums_start(0, sums_out[...])
+    run_ticks(ticks + 0, ticks + 4)
     sums_start(1, sums_finish(0))
+    run_ticks(ticks + 4, ticks + 8)
     swap(1).wait()
     both = part_for(-2 * turn).astype(F32) + arena[5, :USED, :].astype(F32)
     arena[1, :USED, :] = both.astype(BF16)
     for q in pieces:
         back_relay(q).start()
-    run_ticks(ticks + 6, ticks + 8)
-    sums_start(2, sums_finish(1))
+    pl.when(forth)(lambda: back_relay(lang).start())
     swap(0).wait()
     swap(3).wait()
     shared = arena[7, :USED, :].astype(F32)
@@ -759,44 +796,71 @@
     ).astype(BF16)
     for q in pieces:
         back_down(q).start()
+    pl.when(forth)(lambda: back_down(lang).start())
     arena[3, :USED, :] = (
         part_for(4 * turn).astype(F32) + jnp.where(step == turn, shared, 0.0)
     ).astype(BF16)
-    at = slice(0, 160)
+    run_ticks(ticks + 8, ticks + 10)
+    sums_start(2, sums_finish(1))
+    at = slice(0, 144)
     back_relay(0).wait_recv()
     both = arena[3, at, :].astype(F32) + far_in[0, at, :].astype(F32)
     arena[3, at, :] = both.astype(BF16)
     back_up(0).start()
-    run_ticks(ticks + 8, ticks + 9)
-    at = slice(160, 320)
+    run_ticks(ticks + 10, ticks + 11)
+    at = slice(144, 272)
     back_relay(1).wait_recv()
     both = arena[3, at, :].astype(F32) + far_in[0, at, :].astype(F32)
     arena[3, at, :] = both.astype(BF16)
     back_up(1).start()
-    run_ticks(ticks + 9, ticks + 10)
-    at = slice(320, 480)
+    run_ticks(ticks + 11, ticks + 12)
+    at = slice(272, 400)
     back_relay(2).wait_recv()
     both = arena[3, at, :].astype(F32) + far_in[0, at, :].astype(F32)
     arena[3, at, :] = both.astype(BF16)
     back_up(2).start()
+
+    def up_lang():
+        at = slice(PATCHES, USED)
+        back_relay(lang).wait_recv()
+        both = arena[3, at, :].astype(F32) + far_in[0, at, :].astype(F32)
+        arena[3, at, :] = both.astype(BF16)
+        back_up(lang).start()
+
+    pl.when(back_turn)(up_lang)
     sums_start(3, sums_finish(2))
-    run_ticks(ticks + 10, ticks + 12)
+    run_ticks(ticks + 12, ticks + 14)
     swap(2).wait()
     both = part_for(2 * turn).astype(F32) + arena[6, :USED, :].astype(F32)
     arena[2, :USED, :] = both.astype(BF16)
     for q in pieces:
         back_x(q).start()
-    run_ticks(ticks + 12, last)
+    pl.when(back_turn)(lambda: back_x(lang).start())
+    run_ticks(ticks + 14, last)
     sums_out[...] = sums_finish(3)
-    total = branch[...] + arena[4, :USED, :].astype(F32)
     for q in pieces:
         back_relay(q).wait_send()
         for copy in (back_x(q), back_up(q), back_down(q)):
             copy.wait()
-    for n in range(1, 4):
-        total += far_in[n].astype(F32)
-    unit, scale = normalise(tokens[:USED, :].astype(F32))
-    grad_tokens[:USED, :] += norm_backward(total, unit, scale, gain_a)
+
+    def settle_lang_forth():
+        back_relay(lang).wait_send()
+        back_down(lang).wait()
+        back_x(lang).wait_recv()
+
+    def settle_lang_back():
+        back_x(lang).wait_send()
+        back_up(lang).wait()
+
+    pl.when(forth)(settle_lang_forth)
+    pl.when(back_turn)(settle_lang_back)
+    for at, whole in ((slice(0, PATCHES), True), (slice(PATCHES, USED), False)):
+        total = branch[at, :] + mlp_back[at, :] + arena[4, at, :].astype(F32)
+        for n, came in ((1, forth), (2, back_turn), (3, forth)):
+            part = far_in[n, at, :].astype(F32)
+            total += part if whole else jnp.where(came, part, 0.0)
+        unit, scale = normalise(tokens[at, :].astype(F32))
+        grad_tokens[at, :] += norm_backward(total, unit, scale, gain_a)
 
 
 def stage_copies(stage, size, orders):
@@ -828,15 +892,12 @@
         VMEM((KEYS_PADDED, PAIR), BF16),
         VMEM((KEYS_PADDED, 2 * D), BF16),
         VMEM((USED, D), BF16),
-        VMEM((4, SENT, KEYS_PADDED), BF16),
+        VMEM((HEADS, SENT, KEYS_PADDED), BF16),
         VMEM((USED, D), BF16),
         VMEM((USED, D), F32),
         VMEM((USED, D), F32),
         VMEM((2 * D, KEYS_PADDED), BF16),
         VMEM((USED, D), BF16),
-        VMEM((USED, D), BF16),
-        VMEM((USED, D), BF16),
-        VMEM((USED, D), F32),
         VMEM((USED, D), F32),
         VMEM((USED, D), F32),
         VMEM((SENT, D), BF16),
@@ -849,17 +910,16 @@
         VMEM((held, slots[2], SHARD, half), BF16),
         VMEM((4, USED, D), BF16),
         VMEM((4, wide, SUMS, D), F32),
-        dma((4 * len(PIECES) + 4,)),
-        dma((4 * len(PIECES) + 4,)),
-        dma((2 * FF // D,)),
-        dma((2, 2)),
+        dma((6 * (len(PIECES) + 1),)),
+        dma((6 * (len(PIECES) + 1),)),
+        dma((2 * FF // D + 2,)),
         dma((held, sems)),
         dma((held, sems)),
         dma((held, 2)),
         dma((4, wide)),
         dma((4, wide)),
         dma((2, 4)),
-        dma((2, 12)),
+        dma((2, 16)),
     ]
     return pl.pallas_call(
         functools.partial(main_kernel, count, groups, chunks, part_rows),
@@ -868,13 +928,12 @@
             shape((ROWS, D), F32),
             shape((chunks * chunk_rows, D), BF16),
             shape((SUMS, D), F32),
-            shape((4, USED, KEYS_PADDED), BF16),
         ),
-        in_specs=[IN_SMEM] * 4 + [IN_VMEM] * 11 + [ANYWHERE] * 2,
-        out_specs=[IN_VMEM, IN_VMEM, ANYWHERE, IN_VMEM, ANYWHERE],
+        in_specs=[IN_SMEM] * 4 + [IN_VMEM] * 9 + [ANYWHERE] * 4,
+        out_specs=[ANYWHERE, IN_VMEM, ANYWHERE, IN_VMEM],
         scratch_shapes=scratch,
         compiler_params=pltpu.CompilerParams(
-            collective_id=1, has_side_effects=True, vmem_limit_bytes=63 * MIB
+            collective_id=1, has_side_effects=True, vmem_limit_bytes=63 * MIB + (0 if parts == 2 else 800 * 1024)
         ),
         name="main",
     )(*args)
@@ -915,56 +974,61 @@
         pltpu.make_async_copy(rows_held, rows_out, pass_sem.at[2]),
         pltpu.make_async_copy(grad_held, grad_out, pass_sem.at[3]),
     ]
-    count = 2 * blocks + PAIRS
+    count = 2 * blocks + 4
     loads = [
         pltpu.make_async_copy(summed.at[pl.ds(b * D, D), :], narrow.at[b], in_sem.at[b])
         for b in range(count)
     ]
-    for copy in passes_in + loads:
+    order = [count - 1, count - 2, count - 3] + list(range(count - 3))
+    for b in order:
+        loads[b].start()
+    for copy in passes_in:
         copy.start()
     for c in range(blocks):
         grad_bias_up[c * D : (c + 1) * D] = sums[c : c + 1, :].reshape(D)
     rest = (grad_bias_down, grad_gain_mlp, grad_shift_mlp, grad_gain_attn, grad_shift_attn)
     for n, target in enumerate(rest):
         target[...] = sums[blocks + n : blocks + n + 1, :].reshape(D)
-    for copy in passes_in:
-        copy.wait()
-    for copy in passes_out:
-        copy.start()
     stores = []
 
     def store(b, source, target):
         stores.append(pltpu.make_async_copy(source, target, out_sem.at[len(stores)]))
         stores[-1].start()
 
-    for b in range(count):
+    for b in order:
         loads[b].wait()
         c = b // 2
         if b < 2 * blocks:
             wide[b] = narrow[b].astype(F32)
             at = pl.ds(c * D, D)
             store(b, wide.at[b], down.at[at, :] if b % 2 == 0 else up.at[:, at])
+        elif b == 2 * blocks:
+            wide[b] = narrow[b].astype(F32)
+            store(b, wide.at[b], out)
+        elif b == 2 * blocks + 3:
+            wide[b] = narrow[b].astype(F32).T
+            store(b, wide.at[b], query)
         else:
-            i = b - 2 * blocks
-            p = PAIRS - 1 - i
-            wide[b, :PAIR, :] = narrow[b, :PAIR, :].astype(F32)
-            store(b, wide.at[b, pl.ds(0, PAIR), :], out.at[pl.ds(i * PAIR, PAIR), :])
-            base = 2 * blocks + PAIRS
-            for n, (target, column) in enumerate(((query, p), (keyval, p), (keyval, PAIRS + p))):
-                piece = narrow[b, (n + 1) * PAIR : (n + 2) * PAIR, :].astype(F32).T
-                columns = slice(p * PAIR, (p + 1) * PAIR)
-                wide[base + n, :, columns] = piece
-                store(
-                    b,
-                    wide.at[base + n, :, pl.ds(p * PAIR, PAIR)],
-                    target.at[:, pl.ds(column * PAIR, PAIR)],
-                )
+            pairs = 2 * (b - 2 * blocks - 1)
+            for n in range(2):
+                for c in range(2):
+                    first = (2 * n + c) * PAIR
+                    at = pl.ds(first, PAIR)
+                    wide[b, :, first : first + PAIR] = (
+                        narrow[b, first : first + PAIR, :].astype(F32).T
+                    )
+                    column = c * D + (pairs + n) * PAIR
+                    store(b, wide.at[b, :, at], keyval.at[:, pl.ds(column, PAIR)])
+    for copy in passes_in:
+        copy.wait()
+    for copy in passes_out:
+        copy.start()
     for copy in stores + passes_out:
         copy.wait()
 
 
 def widen(summed, rows, grad, sums):
-    blocks = 2 * FF // D + PAIRS
+    blocks = GRAD_ROWS // D
     shape = jax.ShapeDtypeStruct
     dma = pltpu.SemaphoreType.DMA
     return pl.pallas_call(
@@ -984,11 +1048,11 @@
         out_specs=[ANYWHERE] * 7 + [IN_VMEM] * 6,
         scratch_shapes=[
             VMEM((blocks, D, D), BF16),
-            VMEM((blocks + 3, D, D), F32),
+            VMEM((blocks, D, D), F32),
             VMEM(rows.shape, rows.dtype),
             VMEM(grad.shape, grad.dtype),
             dma((blocks,)),
-            dma((blocks + 3 * PAIRS,)),
+            dma((blocks + 6,)),
             dma((4,)),
         ],
         compiler_params=pltpu.CompilerParams(vmem_limit_bytes=60 * MIB),
@@ -1017,7 +1081,7 @@
     shift_mlp,
     cotangent,
 ):
-    block_output, grad_tokens, summed, sums, _ = main(
+    block_output, grad_tokens, summed, sums = main(
         count,
         groups,
         counts.reshape(1),
@@ -1025,10 +1089,8 @@
         slot_view.reshape(1),
         keyframe.reshape(1),
         tokens.reshape(ROWS, D),
-        cotangent.reshape(ROWS, D),
         w_query,
         w_keyval,
-        w_output,
         bias_up,
         bias_down,
         gain_attn,
@@ -1037,6 +1099,8 @@
         shift_mlp,
         w_up,
         w_down,
+        cotangent.reshape(ROWS, D),
+        w_output,
     )
     down, up, out, query, keyval, block_output, grad_tokens, *small = widen(
         summed, block_output, grad_tokens, sums

time: 161 us -> 157 us (0.975)
  Pallas kernels: 158 us -> 154 us
    pallas_call x1, Pallas kernels: 148 us -> 145 us  [main(): pl.pallas_call(functools.partial(main_kernel, count, groups, chunks, part...]
where the time goes in v6:
time: 157 us
  Pallas kernels  154 us (98%)
  between operations  3.44 us (2%)
    pallas_call x1, Pallas kernels, main(): pl.pallas_call(functools.partial(main_kernel, count, groups, chunks, part...  145 us
    pallas_call x1, Pallas kernels, widen(): pl.pallas_call(widen_kernel, out_shape=(shape((FF, D), F32), shape((D, FF...  8.61 us

profile of v6, /device:TPU:0, one launch (start us, length us, event | category | flops | bytes accessed | tf_op | source)
XLA Modules:
  0.0 157.1 jit_solution(7081984708590491914)
XLA Ops:
  3.2 145.0 %main.1 = (bf16[512,512]{1,0:T(8,128)(2,1)}, f32[512,512]{1,0:T(8,128)}, bf16[6144,512]{1,0:T(8,128)(2,1)}, f32[16,512]{1,0:T(8,128)}) custom-call(s32[1]{0:T(128)} %bitcast.8.counts, s32[1]{0:T(128)} %bitcast.9.slot_item, s32[1]{0:T(128)} %bitcast.10.slot_view, s32[1]{0:T(128)} %bitcast.11.keyframe, bf16[512,512]{1,0:T(8,128)(2,1)} %bitcast.12, ...), custom_call_target="tpu_custom_call" | custom-call | tf_op jit(solution)/shard_map/main/pallas_call | solution.py:924
  148.2 8.6 %widen.1 = (f32[2048,512]{1,0:T(8,128)}, f32[512,2048]{1,0:T(8,128)}, f32[512,512]{1,0:T(8,128)}, f32[512,512]{1,0:T(8,128)}, f32[512,1024]{1,0:T(8,128)}, /*ind...) custom-call(bf16[6144,512]{1,0:T(8,128)(2,1)} %get-tuple-element.30., ...), custom_call_target="tpu_custom_call" | custom-call | tf_op jit(solution)/shard_map/widen/pallas_call | solution.py:1034

commit v7 on v6

--- a/solution.py
+++ b/solution.py
@@ -829,14 +829,13 @@
 
     pl.when(back_turn)(up_lang)
     sums_start(3, sums_finish(2))
-    run_ticks(ticks + 12, ticks + 14)
     swap(2).wait()
     both = part_for(2 * turn).astype(F32) + arena[6, :USED, :].astype(F32)
     arena[2, :USED, :] = both.astype(BF16)
     for q in pieces:
         back_x(q).start()
     pl.when(back_turn)(lambda: back_x(lang).start())
-    run_ticks(ticks + 14, last)
+    run_ticks(ticks + 12, last)
     sums_out[...] = sums_finish(3)
     for q in pieces:
         back_relay(q).wait_send()

time: 157 us -> 156 us (level)
  Pallas kernels: 154 us -> 152 us
where the time goes in v7:
time: 156 us
  Pallas kernels  152 us (97%)
  between operations  3.42 us (2%)
    pallas_call x1, Pallas kernels, main(): pl.pallas_call(functools.partial(main_kernel, count, groups, chunks, part...  144 us
    pallas_call x1, Pallas kernels, widen(): pl.pallas_call(widen_kernel, out_shape=(shape((FF, D), F32), shape((D, FF...  8.61 us

profile of v7, /device:TPU:0, one launch (start us, length us, event | category | flops | bytes accessed | tf_op | source)
XLA Modules:
  0.0 155.9 jit_solution(11993150476827552871)
XLA Ops:
  3.2 143.8 %main.1 = (bf16[512,512]{1,0:T(8,128)(2,1)}, f32[512,512]{1,0:T(8,128)}, bf16[6144,512]{1,0:T(8,128)(2,1)}, f32[16,512]{1,0:T(8,128)}) custom-call(s32[1]{0:T(128)} %bitcast.8.counts, s32[1]{0:T(128)} %bitcast.9.slot_item, s32[1]{0:T(128)} %bitcast.10.slot_view, s32[1]{0:T(128)} %bitcast.11.keyframe, bf16[512,512]{1,0:T(8,128)(2,1)} %bitcast.12, ...), custom_call_target="tpu_custom_call" | custom-call | tf_op jit(solution)/shard_map/main/pallas_call | solution.py:923
  147.1 8.6 %widen.1 = (f32[2048,512]{1,0:T(8,128)}, f32[512,2048]{1,0:T(8,128)}, f32[512,512]{1,0:T(8,128)}, f32[512,512]{1,0:T(8,128)}, f32[512,1024]{1,0:T(8,128)}, /*ind...) custom-call(bf16[6144,512]{1,0:T(8,128)(2,1)} %get-tuple-element.30., ...), custom_call_target="tpu_custom_call" | custom-call | tf_op jit(solution)/shard_map/widen/pallas_call | solution.py:1033
